TPU v7x, 128 devices: a whole 4x4x4 slice. The times are simulated.
128 devices in a mesh: wa: 8 (over z, core), grid: 16 (over y, x).
Axes of the slice: x: 4, y: 4, z: 4, core: 2. Of those that a mesh axis runs over, the one named last changes fastest.
Arguments:
- jones: bfloat16 [32, 4, 2, 512, 512], P('wa', None, None, 'grid'), may hold values from -6 to 6
- owner: int32 [32], replicated, may hold values from 0 to 31, each once
- mask: int32 [3, 4, 4], replicated, may hold values 0 or 1
- w_operator: bfloat16 [16, 2, 512, 512], P('wa', None, 'grid'), may hold values from -0.1875 to 0.1875
Outputs:
- conv: bfloat16 [512, 16, 3, 16, 2, 512], P('grid', 'wa')
Inputs may be any that keep to these rules, and one draw needn't show every extreme that they name: owner[t] is the slot that holds type t; every slot holds exactly one type.
All inputs are finite; a program needn't handle non-finite values.
Results may differ from a plain program's by a relative error of at most 0.0058.
Values may be sent and summed in bfloat16 or wider, within the bound.
No kernel may reach another device: no remote copies, remote signals or barrier semaphores. Data moves between devices by JAX's collectives and lax.ppermute only.
A program may use at most 576 MiB of HBM per device.

v0:
```python
import jax
import jax.numpy as jnp
import numpy as np
from jax import lax
from jax.experimental import pallas as pl
from jax.experimental.pallas import tpu as pltpu
from jax.sharding import PartitionSpec as P

RUN = 3
G = 512
ROWS = 32
PLANES = 2

CLASSES = (((1, 3, 4, 12), (3, 4, 12, 1)), ((4, 12, 1, 3), (12, 1, 3, 4)))
ZCLASSES = ((2, 6), (6, 2))

PAIRS = ((0, 1), (0, 2), (0, 3), (1, 2), (1, 3), (2, 3))


def term(a, b):
    return 8 * (a // 2) + 4 * (b // 2) + 2 * (a % 2) + b % 2


def block_masks():
    table = np.zeros((2, 2, 16), np.int32)
    for core in range(2):
        for half in range(2):
            for block in range(16):
                for step in range(4):
                    if block >> step & 1:
                        table[core, half, block] ^= CLASSES[core][half][step]
    return table


def exchange(value, wa_mask, grid_mask):
    perm = []
    for wa in range(8):
        for grid in range(16):
            core = wa % 2
            perm.append((wa * 16 + grid, (wa ^ wa_mask(core)) * 16 + (grid ^ grid_mask(core))))
    return lax.ppermute(value, ("wa", "grid"), perm)


def swap_core(value):
    return exchange(value, lambda core: 1, lambda core: 0)


def swap_z(value, step):
    return exchange(value, lambda core: ZCLASSES[core][step], lambda core: 0)


def swap_grid(value, half, step):
    return exchange(value, lambda core: 0, lambda core: CLASSES[core][half][step])


def transform_kernel(index, *refs):
    (place, keep, ku, k3, k40, k41, own3, own40, own41, far3, far40, far41) = refs[:12]
    out, fields, operator, real, imag, left, staged, field_sem, operator_sem, out_sem = refs[-10:]
    core = place[0]
    own4 = (own40, own41)
    far4 = (far40, far41)
    k4 = (k40, k41)
    for half in range(2):
        for block in range(16):
            row = pl.multiple_of(place[1 + 16 * half + block] * ROWS, ROWS)
            low = block < 8
            source = own3.at[half, block] if low else own4[half].at[block - 8]
            pltpu.make_async_copy(
                source, fields.at[core, pl.ds(2 * half, 2), pl.ds(row, ROWS)], field_sem
            ).start()
            far_row = pl.multiple_of(place[33 + 16 * half + block] * ROWS, ROWS)
            source = far3.at[half, block] if low else far4[half].at[block - 8]
            pltpu.make_async_copy(
                source, fields.at[1 - core, pl.ds(2 * half, 2), pl.ds(far_row, ROWS)], field_sem
            ).start()
    for half in range(2):
        for block in range(16):
            row = pl.multiple_of(place[1 + 16 * half + block] * ROWS, ROWS)
            source = k3.at[half, block] if block < 8 else k4[half].at[block - 8]
            pltpu.make_async_copy(
                source, operator.at[half, :, pl.ds(row, ROWS)], operator_sem
            ).start()
    pltpu.make_async_copy(fields, fields, field_sem).wait()

    def products(a, b, want_imag):
        def chunk(step, carry):
            rows = pl.ds(pl.multiple_of(step * 64, 64), 64)
            ar = fields[0, a, rows].astype(jnp.float32)
            ai = fields[1, a, rows].astype(jnp.float32)
            br = fields[0, b, rows].astype(jnp.float32)
            bi = fields[1, b, rows].astype(jnp.float32)
            real[rows] = (ar * br + ai * bi).astype(jnp.bfloat16)
            if want_imag:
                imag[rows] = (ai * br - ar * bi).astype(jnp.bfloat16)
            return carry

        lax.fori_loop(0, G // 64, chunk, 0)

    def put(plane, entry, scale, value, turned):
        rows = pl.ds(pl.multiple_of(entry * 64, 64), 64)
        left[plane, rows, 0:G] = (value * scale).astype(jnp.bfloat16)
        left[plane, rows, G : 2 * G] = (turned * scale).astype(jnp.bfloat16)

    def pair(a, b):
        products(a, b, True)
        first = 8 * (a // 2) + 4 * (b // 2) + 2 * (a % 2) + b % 2
        second = 8 * (b // 2) + 4 * (a // 2) + 2 * (b % 2) + a % 2
        for plane in range(PLANES):
            rows = slice(plane * 128, plane * 128 + 128)
            pa = jnp.dot(ku[rows], real[...], preferred_element_type=jnp.float32)
            pb = jnp.dot(ku[rows], imag[...], preferred_element_type=jnp.float32)
            put(plane, first, keep[first], pa[:64] + pb[64:], pa[64:] - pb[:64])
            put(plane, second, keep[second], pa[:64] - pb[64:], pa[64:] + pb[:64])

    def square(a):
        products(a, a, False)
        entry = 8 * (a // 2) + 4 * (a // 2) + 2 * (a % 2) + a % 2
        for plane in range(PLANES):
            rows = slice(plane * 128, plane * 128 + 128)
            pa = jnp.dot(ku[rows], real[...], preferred_element_type=jnp.float32)
            put(plane, entry, keep[entry], pa[:64], pa[64:])

    def square_step(a, carry):
        square(a)
        return carry

    def pair_step(step, carry):
        a = jnp.where(step < 3, 0, jnp.where(step < 5, 1, 2))
        b = jnp.where(step < 3, step + 1, jnp.where(step < 5, step - 1, 3))
        pair(a, b)
        return carry

    lax.fori_loop(0, 4, square_step, 0)
    lax.fori_loop(0, 6, pair_step, 0)
    pltpu.make_async_copy(operator, operator, operator_sem).wait()

    contract = (((1,), (1,)), ((), ()))

    for plane in range(PLANES):
        def second_pass(group, carry, plane=plane):
            rows = pl.ds(pl.multiple_of(group * 256, 256), 256)
            total = lax.dot_general(
                left[plane, rows, 0:G], operator[plane, 0], contract, preferred_element_type=jnp.float32
            ) + lax.dot_general(
                left[plane, rows, G : 2 * G], operator[plane, 1], contract, preferred_element_type=jnp.float32
            )
            staged[plane, pl.ds(group * 4, 4)] = total.astype(jnp.bfloat16).reshape(4, ROWS, 2, G)
            for entry in range(4):
                pltpu.make_async_copy(
                    staged.at[plane, group * 4 + entry],
                    out.at[:, plane, index, group * 4 + entry],
                    out_sem,
                ).start()
            return carry

        lax.fori_loop(0, 4, second_pass, 0)
    pltpu.make_async_copy(staged, staged, out_sem).wait()


def transform(index, place, keep, ku, operators, own, far, previous):
    anywhere = pl.BlockSpec(memory_space=pl.ANY)
    scalars = pl.BlockSpec(memory_space=pltpu.SMEM)
    operands = [place, keep, ku, *operators, *own, *far]
    specs = [scalars, scalars, pl.BlockSpec(memory_space=pltpu.VMEM)] + [anywhere] * 9
    aliases = {}
    if previous is not None:
        aliases = {len(operands): 0}
        operands.append(previous)
        specs.append(anywhere)

    def kernel(*refs):
        transform_kernel(index, *refs)

    return pl.pallas_call(
        kernel,
        out_shape=jax.ShapeDtypeStruct((ROWS, PLANES, RUN, 16, 2, G), jnp.bfloat16),
        in_specs=specs,
        out_specs=anywhere,
        input_output_aliases=aliases,
        scratch_shapes=[
            pltpu.VMEM((2, 4, G, G), jnp.bfloat16),
            pltpu.VMEM((PLANES, 2, G, G), jnp.bfloat16),
            pltpu.VMEM((G, G), jnp.bfloat16),
            pltpu.VMEM((G, G), jnp.bfloat16),
            pltpu.VMEM((PLANES, 16 * 64, 2 * G), jnp.bfloat16),
            pltpu.VMEM((PLANES, 16, ROWS, 2, G), jnp.bfloat16),
            pltpu.SemaphoreType.DMA,
            pltpu.SemaphoreType.DMA,
            pltpu.SemaphoreType.DMA,
        ],
        compiler_params=pltpu.CompilerParams(vmem_limit_bytes=40 * 1024 * 1024),
        cost_estimate=pl.CostEstimate(flops=4_300_000_000, bytes_accessed=9_000_000, transcendentals=0),
        name="transform",
    )(*operands)


def gather_operator(w_operator):
    lows, highs = [], []
    for half in range(2):
        held = w_operator[half][None]
        for step in range(3):
            held = jnp.concatenate([held, swap_grid(held, half, step)], 0)
        lows.append(held)
        highs.append(swap_grid(held, half, 3))
    return jnp.stack(lows), highs[0], highs[1]


def select(flags, yes, no):
    return jnp.where(flags[:, None, None, None], yes, no)


def body(jones, owner, mask, w_operator):
    wa = lax.axis_index("wa")
    grid = lax.axis_index("grid")
    core = wa % 2
    slots = owner[:RUN]
    holder = slots // 4
    held = [lax.dynamic_index_in_dim(jones, slots[index] % 4, 0, keepdims=False) for index in range(RUN)]
    mine = jnp.stack([lax.dynamic_index_in_dim(one, core, 1, keepdims=False) for one in held])
    other = jnp.stack([lax.dynamic_index_in_dim(one, 1 - core, 1, keepdims=False) for one in held])
    rows = select(holder % 2 == core, mine, swap_core(other))
    first = jnp.where(core == 0, ZCLASSES[0][0], ZCLASSES[1][0]) // 2
    here = holder // 2 == wa // 2
    rows = select(here, rows, swap_z(rows, 0))
    near = here | (holder // 2 == (wa // 2 ^ first))
    rows = select(near, rows, swap_z(rows, 1))

    operators = gather_operator(w_operator)

    streams = []
    for half in range(2):
        stream = rows[None, :, 2 * half : 2 * half + 2]
        for step in range(2):
            stream = jnp.concatenate([stream, swap_grid(stream, half, step)], 0)
        streams.append((stream, swap_grid(stream, half, 2)))
    masks = jnp.asarray(block_masks())
    own_place = grid ^ lax.dynamic_index_in_dim(masks, core, 0, keepdims=False)
    far_place = grid ^ lax.dynamic_index_in_dim(masks, 1 - core, 0, keepdims=False)
    place = jnp.concatenate([core[None], own_place.reshape(-1), far_place.reshape(-1)]).astype(jnp.int32)
    kr, ki = w_operator[:, 0], w_operator[:, 1]
    plain = jnp.stack([kr, ki], 2).reshape(PLANES, 2 * ROWS, G)
    turned = jnp.stack([-ki, kr], 2).reshape(PLANES, 2 * ROWS, G)
    ku = jnp.concatenate([plain, turned], 1).reshape(PLANES * 4 * ROWS, G)
    keep = mask.reshape(RUN, 16).astype(jnp.float32)

    own, far = [], []
    for index in range(RUN):
        low = jnp.stack([jnp.concatenate([near_[:, index], far_[:, index]], 0) for near_, far_ in streams])
        high = [swap_grid(low[half], half, 3) for half in range(2)]
        own.append((low, *high))
        far.append((swap_core(low), swap_core(high[0]), swap_core(high[1])))
    result = None
    for index in range(RUN):
        result = transform(index, place, keep[index], ku, operators, own[index], far[index], result)
    return result


def solution(mesh):
    return jax.shard_map(
        body,
        mesh=mesh,
        in_specs=(P("wa", None, None, "grid", None), P(), P(), P("wa", None, "grid", None)),
        out_specs=P("grid", "wa", None, None, None, None),
        check_vma=False,
    )
```

profile of v0, /device:TPU:1, one launch (start us, length us, event | category | flops | bytes accessed | tf_op | source)
XLA Modules:
  0.0 147.9 jit_solution(438617857247506490)
XLA Ops:
  0.0 1.4 fusion.14
  8.5 1.5 %collective-permute-start.8 = (bf16[3,4,32,512]{3,2,1,0:T(8,128)(2,1)S(1)}, bf16[3,4,32,512]{3,2,1,0:T(8,128)(2,1)S(1)}, u32[]{:S(2)}, u32[]{:S(2)}) collective-permute-start(bf16[3,4,32,512]{3,2,1,0:T(8,128)(2,1)S(1)} %pad_maximum_fusion.14), channel_id=1, source_target_pairs={{0,16},{1,17},{2,18},{3,19},{4,20},{5,21},{6,22},{7,23},{8,24},{9,... | collective-permute-start | bytes 1179656 | tf_op jit(solution)/shard_map/ppermute | solution.py:41
  11.4 3.9 %collective-permute-start.9 = (bf16[3,4,32,512]{3,2,1,0:T(8,128)(2,1)S(1)}, bf16[3,4,32,512]{3,2,1,0:T(8,128)(2,1)S(1)}, u32[]{:S(2)}, u32[]{:S(2)}) collective-permute-start(bf16[3,4,32,512]{3,2,1,0:T(8,128)(2,1)S(1)} %maximum_select_fusion), channel_id=1, source_target_pairs={{0,32},{1,33},{2,34},{3,35},{4,36},{5,37},{6,38},{7,39},{8,40},{9,... | collective-permute-start | bytes 1179656 | tf_op jit(solution)/shard_map/ppermute | solution.py:41
  15.3 5.2 %collective-permute-done.9 = bf16[3,4,32,512]{3,2,1,0:T(8,128)(2,1)S(1)} collective-permute-done((bf16[3,4,32,512]{3,2,1,0:T(8,128)(2,1)S(1)}, bf16[3,4,32,512]{3,2,1,0:T(8,128)(2,1)S(1)}, u32[]{:S(2)}, u32[]{:S(2)}) %collective-permute-start.9) | collective-permute-done | bytes 393248 | tf_op jit(solution)/shard_map/ppermute | solution.py:41
  21.6 1.4 collective-permute-start
  23.0 1.9 %collective-permute-start.3 = (bf16[1,2,32,512]{3,2,1,0:T(8,128)(2,1)S(1)}, bf16[1,2,32,512]{3,2,1,0:T(8,128)(2,1)S(1)}, u32[]{:S(2)}, u32[]{:S(2)}) collective-permute-start(bf16[1,2,32,512]{3,2,1,0:T(8,128)(2,1)S(1)} %get-tuple-element.45), channel_id=1, source_target_pairs={{0,3},{1,2},{2,1},{3,0},{4,7},{5,6},{6,5},{7,4},{8,11},{9,10},{10,... | collective-permute-start | bytes 196616 | tf_op jit(solution)/shard_map/ppermute | solution.py:41
  25.8 1.8 %collective-permute-start.1 = (bf16[2,2,32,512]{3,2,1,0:T(8,128)(2,1)S(1)}, bf16[2,2,32,512]{3,2,1,0:T(8,128)(2,1)S(1)}, u32[]{:S(2)}, u32[]{:S(2)}) collective-permute-start(bf16[2,2,32,512]{3,2,1,0:T(8,128)(2,1)S(1)} %pad_maximum_fusion.22), channel_id=1, source_target_pairs={{0,3},{1,2},{2,1},{3,0},{4,7},{5,6},{6,5},{7,4},{8,11},{9,10},{10,... | collective-permute-start | bytes 393224 | tf_op jit(solution)/shard_map/ppermute | solution.py:41
  27.8 1.4 collective-permute-start.11
  32.2 1.8 %collective-permute-start.14 = (bf16[1,3,2,32,512]{4,3,2,1,0:T(8,128)(2,1)S(1)}, bf16[1,3,2,32,512]{4,3,2,1,0:T(8,128)(2,1)S(1)}, u32[]{:S(2)}, u32[]{:S(2)}) collective-permute-start(bf16[1,3,2,32,512]{4,3,2,1,0:T(8,128)(2,1)S(1)} %get-tuple-element.43), channel_id=1, source_target_pairs={{0,3},{1,2},{2,1},{3,0},{4,7},{5,6},{6,5},{7,4},{8,11},{9,10},{10,... | collective-permute-start | bytes 589832 | tf_op jit(solution)/shard_map/ppermute | solution.py:41
  35.3 2.6 %collective-permute-start.5 = (bf16[4,2,32,512]{3,2,1,0:T(8,128)(2,1)S(1)}, bf16[4,2,32,512]{3,2,1,0:T(8,128)(2,1)S(1)}, u32[]{:S(2)}, u32[]{:S(2)}) collective-permute-start(bf16[4,2,32,512]{3,2,1,0:T(8,128)(2,1)S(1)} %pad_maximum_fusion.19), channel_id=1, source_target_pairs={{0,12},{1,13},{2,14},{3,15},{4,8},{5,9},{6,10},{7,11},{8,4},{9,5},... | collective-permute-start | bytes 786440 | tf_op jit(solution)/shard_map/ppermute | solution.py:41
  38.7 3.8 %collective-permute-done.12 = bf16[2,3,2,32,512]{4,3,2,0,1:T(8,128)(2,1)S(1)} collective-permute-done((bf16[2,3,2,32,512]{4,3,2,0,1:T(8,128)(2,1)S(1)}, bf16[2,3,2,32,512]{4,3,2,0,1:T(8,128)(2,1)S(1)}, u32[]{:S(2)}, u32[]{:S(2)}) %collective-permute-start.12) | collective-permute-done | bytes 393248 | tf_op jit(solution)/shard_map/ppermute | solution.py:41
  43.8 2.2 %collective-permute-start.6 = (bf16[8,2,32,512]{3,2,1,0:T(8,128)(2,1)S(1)}, bf16[8,2,32,512]{3,2,1,0:T(8,128)(2,1)S(1)}, u32[]{:S(2)}, u32[]{:S(2)}) collective-permute-start(bf16[8,2,32,512]{3,2,1,0:T(8,128)(2,1)S(1)} %get-tuple-element.40), channel_id=1, source_target_pairs={{0,12},{1,13},{2,14},{3,15},{4,8},{5,9},{6,10},{7,11},{8,4},{9,5},... | collective-permute-start | bytes 1572872 | tf_op jit(solution)/shard_map/ppermute | solution.py:41
  47.7 6.1 %collective-permute-done.13 = bf16[4,3,2,32,512]{4,3,2,0,1:T(8,128)(2,1)S(1)} collective-permute-done((bf16[4,3,2,32,512]{4,3,2,0,1:T(8,128)(2,1)S(1)}, bf16[4,3,2,32,512]{4,3,2,0,1:T(8,128)(2,1)S(1)}, u32[]{:S(2)}, u32[]{:S(2)}) %collective-permute-start.13) | collective-permute-done | bytes 786464 | tf_op jit(solution)/shard_map/ppermute | solution.py:41
  53.9 1.9 %collective-permute-start.27 = (bf16[8,2,32,512]{3,2,1,0:T(8,128)(2,1)S(1)}, bf16[8,2,32,512]{3,2,1,0:T(8,128)(2,1)S(1)}, u32[]{:S(2)}, u32[]{:S(2)}) collective-permute-start(bf16[8,2,32,512]{3,2,1,0:T(8,128)(2,1)S(1)} %get-tuple-element.28), channel_id=1, source_target_pairs={{0,12},{1,13},{2,14},{3,15},{4,8},{5,9},{6,10},{7,11},{8,4},{9,5},... | collective-permute-start | bytes 1572872 | tf_op jit(solution)/shard_map/ppermute | solution.py:41
  55.8 6.9 %collective-permute-done.16 = bf16[4,3,2,32,512]{4,3,2,0,1:T(8,128)(2,1)S(1)} collective-permute-done((bf16[4,3,2,32,512]{4,3,2,0,1:T(8,128)(2,1)S(1)}, bf16[4,3,2,32,512]{4,3,2,0,1:T(8,128)(2,1)S(1)}, u32[]{:S(2)}, u32[]{:S(2)}) %collective-permute-start.16) | collective-permute-done | bytes 786464 | tf_op jit(solution)/shard_map/ppermute | solution.py:41
  63.0 2.3 %collective-permute-start.22 = (bf16[8,2,32,512]{3,2,1,0:T(8,128)(2,1)S(1)}, bf16[8,2,32,512]{3,2,1,0:T(8,128)(2,1)}, u32[]{:S(2)}, u32[]{:S(2)}) collective-permute-start(bf16[8,2,32,512]{3,2,1,0:T(8,128)(2,1)S(1)} %get-tuple-element.32), channel_id=1, source_target_pairs={{0,12},{1,13},{2,14},{3,15},{4,8},{5,9},{6,10},{7,11},{8,4},{9,5},... | collective-permute-start | bytes 1572872 | tf_op jit(solution)/shard_map/ppermute | solution.py:41
  67.3 1.4 collective-permute-start.23
  69.8 10.4 %collective-permute-start.29 = (bf16[2,8,2,32,512]{4,3,2,1,0:T(8,128)(2,1)}, bf16[2,8,2,32,512]{4,3,2,1,0:T(8,128)(2,1)}, u32[]{:S(2)}, u32[]{:S(2)}) collective-permute-start(bf16[2,8,2,32,512]{4,3,2,1,0:T(8,128)(2,1)} %pad_maximum_fusion.3.refs_6_), channel_id=1, source_target_pairs={{0,16},{1,17},{2,18},{3,19},{4,20},{5,21},{6,22},{7,23},{8,24},{9,... | collective-permute-start | bytes 3145736 | tf_op jit(solution)/shard_map/ppermute | solution.py:41
  80.2 1.6 %collective-permute-start.17 = (bf16[8,2,32,512]{3,2,1,0:T(8,128)(2,1)}, bf16[8,2,32,512]{3,2,1,0:T(8,128)(2,1)}, u32[]{:S(2)}, u32[]{:S(2)}) collective-permute-start(bf16[8,2,32,512]{3,2,1,0:T(8,128)(2,1)} %get-tuple-element.36), channel_id=1, source_target_pairs={{0,12},{1,13},{2,14},{3,15},{4,8},{5,9},{6,10},{7,11},{8,4},{9,5},... | collective-permute-start | bytes 1572872 | tf_op jit(solution)/shard_map/ppermute | solution.py:41
  85.2 1.4 collective-permute-start.30
  87.9 2.2 %collective-permute-done.17.refs_7_ = bf16[8,2,32,512]{3,2,1,0:T(8,128)(2,1)} collective-permute-done((bf16[8,2,32,512]{3,2,1,0:T(8,128)(2,1)}, bf16[8,2,32,512]{3,2,1,0:T(8,128)(2,1)}, u32[]{:S(2)}, u32[]{:S(2)}) %collective-permute-start.17) | collective-permute-done | bytes 524320 | tf_op jit(solution)/shard_map/ppermute | solution.py:41
  98.8 15.4 %transform.3.refs_12_ = bf16[32,2,3,16,2,512]{5,4,3,2,1,0:T(2,128)(2,1)} custom-call(s32[65]{0:T(128)S(1)} %pad_add_fusion.refs_0_, f32[16]{0:T(128)S(1)} %squeeze.82.refs_1_, bf16[256,512]{1,0:T(8,128)(2,1)S(1)} %bitcast.71, bf16[2,8,2,32,512]{4,3,2,1,0:T(8,128)(2,1)S(1)} %pad_maximum_fusion.refs_3_, ...), custom_call_target="tpu_custom_call" | custom-call | flops 4300000256 | bytes 9000000 | tf_op jit(solution)/shard_map/transform/pallas_call | solution.py:174
  114.2 16.7 %transform.4.refs_12_ = bf16[32,2,3,16,2,512]{5,4,3,2,1,0:T(2,128)(2,1)} custom-call(s32[65]{0:T(128)S(1)} %pad_add_fusion.refs_0_, f32[16]{0:T(128)S(1)} %squeeze.77.refs_1_, bf16[256,512]{1,0:T(8,128)(2,1)S(1)} %bitcast.72, bf16[2,8,2,32,512]{4,3,2,1,0:T(8,128)(2,1)S(1)} %pad_maximum_fusion.refs_3_, ...), custom_call_target="tpu_custom_call", output_to_operand_aliasing={{}: (12, {})} | custom-call | flops 4300000256 | bytes 9000000 | tf_op jit(solution)/shard_map/transform/pallas_call | solution.py:174
  131.0 16.7 %transform.5 = bf16[32,2,3,16,2,512]{5,4,3,2,1,0:T(2,128)(2,1)} custom-call(s32[65]{0:T(128)S(1)} %pad_add_fusion.refs_0_, f32[16]{0:T(128)S(1)} %squeeze.69.refs_1_, bf16[256,512]{1,0:T(8,128)(2,1)S(1)} %bitcast.73, bf16[2,8,2,32,512]{4,3,2,1,0:T(8,128)(2,1)S(1)} %pad_maximum_fusion.refs_3_, ...), custom_call_target="tpu_custom_call", output_to_operand_aliasing={{}: (12, {})} | custom-call | flops 4300000256 | bytes 9000000 | tf_op jit(solution)/shard_map/transform/pallas_call | solution.py:174
  (109 shorter events, 29.7 us)
Async XLA Ops:
  11.4 9.1 %collective-permute-start.9 = (bf16[3,4,32,512]{3,2,1,0:T(8,128)(2,1)S(1)}, bf16[3,4,32,512]{3,2,1,0:T(8,128)(2,1)S(1)}, u32[]{:S(2)}, u32[]{:S(2)}) collective-permute-start(bf16[3,4,32,512]{3,2,1,0:T(8,128)(2,1)S(1)} %maximum_select_fusion), channel_id=1, source_target_pairs={{0,32},{1,33},{2,34},{3,35},{4,36},{5,37},{6,38},{7,39},{8,40},{9,... | collective-permute-start | bytes 1179656 | tf_op jit(solution)/shard_map/ppermute | solution.py:41
  20.6 7.0 %collective-permute-start.10 = (bf16[3,4,32,512]{3,2,1,0:T(8,128)(2,1)S(1)}, bf16[3,4,32,512]{3,2,1,0:T(8,128)(2,1)S(1)}, u32[]{:S(2)}, u32[]{:S(2)}) collective-permute-start(bf16[3,4,32,512]{3,2,1,0:T(8,128)(2,1)S(1)} %broadcast_select_fusion), channel_id=1, source_target_pairs={{0,96},{1,97},{2,98},{3,99},{4,100},{5,101},{6,102},{7,103},{8,104... | collective-permute-start | bytes 1179656 | tf_op jit(solution)/shard_map/ppermute | solution.py:41
  31.2 11.7 %collective-permute-start.2 = (bf16[4,2,32,512]{3,2,1,0:T(8,128)(2,1)S(1)}, bf16[4,2,32,512]{3,2,1,0:T(8,128)(2,1)S(1)}, u32[]{:S(2)}, u32[]{:S(2)}) collective-permute-start(bf16[4,2,32,512]{3,2,1,0:T(8,128)(2,1)S(1)} %pad_maximum_fusion.18), channel_id=1, source_target_pairs={{0,4},{1,5},{2,6},{3,7},{4,0},{5,1},{6,2},{7,3},{8,12},{9,13},{10,... | collective-permute-start | bytes 786440 | tf_op jit(solution)/shard_map/ppermute | solution.py:41
  34.0 8.4 %collective-permute-start.12 = (bf16[2,3,2,32,512]{4,3,2,0,1:T(8,128)(2,1)S(1)}, bf16[2,3,2,32,512]{4,3,2,0,1:T(8,128)(2,1)S(1)}, u32[]{:S(2)}, u32[]{:S(2)}) collective-permute-start(bf16[2,3,2,32,512]{4,3,2,0,1:T(8,128)(2,1)S(1)} %pad_maximum_fusion.15), channel_id=1, source_target_pairs={{0,3},{1,2},{2,1},{3,0},{4,7},{5,6},{6,5},{7,4},{8,11},{9,10},{10,... | collective-permute-start | bytes 1179656 | tf_op jit(solution)/shard_map/ppermute | solution.py:41
  35.3 10.7 %collective-permute-start.5 = (bf16[4,2,32,512]{3,2,1,0:T(8,128)(2,1)S(1)}, bf16[4,2,32,512]{3,2,1,0:T(8,128)(2,1)S(1)}, u32[]{:S(2)}, u32[]{:S(2)}) collective-permute-start(bf16[4,2,32,512]{3,2,1,0:T(8,128)(2,1)S(1)} %pad_maximum_fusion.19), channel_id=1, source_target_pairs={{0,12},{1,13},{2,14},{3,15},{4,8},{5,9},{6,10},{7,11},{8,4},{9,5},... | collective-permute-start | bytes 786440 | tf_op jit(solution)/shard_map/ppermute | solution.py:41
  38.0 8.9 %collective-permute-start.15 = (bf16[2,3,2,32,512]{4,3,2,1,0:T(8,128)(2,1)S(1)}, bf16[2,3,2,32,512]{4,3,2,1,0:T(8,128)(2,1)S(1)}, u32[]{:S(2)}, u32[]{:S(2)}) collective-permute-start(bf16[2,3,2,32,512]{4,3,2,1,0:T(8,128)(2,1)S(1)} %pad_maximum_fusion.16), channel_id=1, source_target_pairs={{0,4},{1,5},{2,6},{3,7},{4,0},{5,1},{6,2},{7,3},{8,12},{9,13},{10,... | collective-permute-start | bytes 1179656 | tf_op jit(solution)/shard_map/ppermute | solution.py:41
  42.6 11.2 %collective-permute-start.13 = (bf16[4,3,2,32,512]{4,3,2,0,1:T(8,128)(2,1)S(1)}, bf16[4,3,2,32,512]{4,3,2,0,1:T(8,128)(2,1)S(1)}, u32[]{:S(2)}, u32[]{:S(2)}) collective-permute-start(bf16[4,3,2,32,512]{4,3,2,0,1:T(8,128)(2,1)S(1)} %pad_maximum_fusion.4), channel_id=1, source_target_pairs={{0,4},{1,5},{2,6},{3,7},{4,0},{5,1},{6,2},{7,3},{8,12},{9,13},{10,... | collective-permute-start | bytes 2359304 | tf_op jit(solution)/shard_map/ppermute | solution.py:41
  43.8 23.6 %collective-permute-start.6 = (bf16[8,2,32,512]{3,2,1,0:T(8,128)(2,1)S(1)}, bf16[8,2,32,512]{3,2,1,0:T(8,128)(2,1)S(1)}, u32[]{:S(2)}, u32[]{:S(2)}) collective-permute-start(bf16[8,2,32,512]{3,2,1,0:T(8,128)(2,1)S(1)} %get-tuple-element.40), channel_id=1, source_target_pairs={{0,12},{1,13},{2,14},{3,15},{4,8},{5,9},{6,10},{7,11},{8,4},{9,5},... | collective-permute-start | bytes 1572872 | tf_op jit(solution)/shard_map/ppermute | solution.py:41
  46.9 22.9 %collective-permute-start.7 = (bf16[8,2,32,512]{3,2,1,0:T(8,128)(2,1)S(1)}, bf16[8,2,32,512]{3,2,1,0:T(8,128)(2,1)S(1)}, u32[]{:S(2)}, u32[]{:S(2)}) collective-permute-start(bf16[8,2,32,512]{3,2,1,0:T(8,128)(2,1)S(1)} %get-tuple-element.38), channel_id=1, source_target_pairs={{0,1},{1,0},{2,3},{3,2},{4,5},{5,4},{6,7},{7,6},{8,9},{9,8},{10,11... | collective-permute-start | bytes 1572872 | tf_op jit(solution)/shard_map/ppermute | solution.py:41
  47.0 15.6 %collective-permute-start.16 = (bf16[4,3,2,32,512]{4,3,2,0,1:T(8,128)(2,1)S(1)}, bf16[4,3,2,32,512]{4,3,2,0,1:T(8,128)(2,1)S(1)}, u32[]{:S(2)}, u32[]{:S(2)}) collective-permute-start(bf16[4,3,2,32,512]{4,3,2,0,1:T(8,128)(2,1)S(1)} %copy.14), channel_id=1, source_target_pairs={{0,12},{1,13},{2,14},{3,15},{4,8},{5,9},{6,10},{7,11},{8,4},{9,5},... | collective-permute-start | bytes 2359304 | tf_op jit(solution)/shard_map/ppermute | solution.py:41
  53.9 26.3 %collective-permute-start.27 = (bf16[8,2,32,512]{3,2,1,0:T(8,128)(2,1)S(1)}, bf16[8,2,32,512]{3,2,1,0:T(8,128)(2,1)S(1)}, u32[]{:S(2)}, u32[]{:S(2)}) collective-permute-start(bf16[8,2,32,512]{3,2,1,0:T(8,128)(2,1)S(1)} %get-tuple-element.28), channel_id=1, source_target_pairs={{0,12},{1,13},{2,14},{3,15},{4,8},{5,9},{6,10},{7,11},{8,4},{9,5},... | collective-permute-start | bytes 1572872 | tf_op jit(solution)/shard_map/ppermute | solution.py:41
  62.9 19.1 %collective-permute-start.28 = (bf16[8,2,32,512]{3,2,1,0:T(8,128)(2,1)S(1)}, bf16[8,2,32,512]{3,2,1,0:T(8,128)(2,1)S(1)}, u32[]{:S(2)}, u32[]{:S(2)}) collective-permute-start(bf16[8,2,32,512]{3,2,1,0:T(8,128)(2,1)S(1)} %get-tuple-element.26), channel_id=1, source_target_pairs={{0,1},{1,0},{2,3},{3,2},{4,5},{5,4},{6,7},{7,6},{8,9},{9,8},{10,11... | collective-permute-start | bytes 1572872 | tf_op jit(solution)/shard_map/ppermute | solution.py:41
  63.0 21.1 %collective-permute-start.22 = (bf16[8,2,32,512]{3,2,1,0:T(8,128)(2,1)S(1)}, bf16[8,2,32,512]{3,2,1,0:T(8,128)(2,1)}, u32[]{:S(2)}, u32[]{:S(2)}) collective-permute-start(bf16[8,2,32,512]{3,2,1,0:T(8,128)(2,1)S(1)} %get-tuple-element.32), channel_id=1, source_target_pairs={{0,12},{1,13},{2,14},{3,15},{4,8},{5,9},{6,10},{7,11},{8,4},{9,5},... | collective-permute-start | bytes 1572872 | tf_op jit(solution)/shard_map/ppermute | solution.py:41
  67.3 17.9 %collective-permute-start.23 = (bf16[8,2,32,512]{3,2,1,0:T(8,128)(2,1)}, bf16[8,2,32,512]{3,2,1,0:T(8,128)(2,1)}, u32[]{:S(2)}, u32[]{:S(2)}) collective-permute-start(bf16[8,2,32,512]{3,2,1,0:T(8,128)(2,1)} %get-tuple-element.30), channel_id=1, source_target_pairs={{0,1},{1,0},{2,3},{3,2},{4,5},{5,4},{6,7},{7,6},{8,9},{9,8},{10,11... | collective-permute-start | bytes 1572872 | tf_op jit(solution)/shard_map/ppermute | solution.py:41
  69.8 24.4 %collective-permute-start.29 = (bf16[2,8,2,32,512]{4,3,2,1,0:T(8,128)(2,1)}, bf16[2,8,2,32,512]{4,3,2,1,0:T(8,128)(2,1)}, u32[]{:S(2)}, u32[]{:S(2)}) collective-permute-start(bf16[2,8,2,32,512]{4,3,2,1,0:T(8,128)(2,1)} %pad_maximum_fusion.3.refs_6_), channel_id=1, source_target_pairs={{0,16},{1,17},{2,18},{3,19},{4,20},{5,21},{6,22},{7,23},{8,24},{9,... | collective-permute-start | bytes 3145736 | tf_op jit(solution)/shard_map/ppermute | solution.py:41
  80.2 9.9 %collective-permute-start.17 = (bf16[8,2,32,512]{3,2,1,0:T(8,128)(2,1)}, bf16[8,2,32,512]{3,2,1,0:T(8,128)(2,1)}, u32[]{:S(2)}, u32[]{:S(2)}) collective-permute-start(bf16[8,2,32,512]{3,2,1,0:T(8,128)(2,1)} %get-tuple-element.36), channel_id=1, source_target_pairs={{0,12},{1,13},{2,14},{3,15},{4,8},{5,9},{6,10},{7,11},{8,4},{9,5},... | collective-permute-start | bytes 1572872 | tf_op jit(solution)/shard_map/ppermute | solution.py:41
  82.7 13.6 %collective-permute-start.24 = (bf16[2,8,2,32,512]{4,3,2,1,0:T(8,128)(2,1)S(1)}, bf16[2,8,2,32,512]{4,3,2,1,0:T(8,128)(2,1)S(1)}, u32[]{:S(2)}, u32[]{:S(2)}) collective-permute-start(bf16[2,8,2,32,512]{4,3,2,1,0:T(8,128)(2,1)S(1)} %pad_maximum_fusion.2.refs_6_), channel_id=1, source_target_pairs={{0,16},{1,17},{2,18},{3,19},{4,20},{5,21},{6,22},{7,23},{8,24},{9,... | collective-permute-start | bytes 3145736 | tf_op jit(solution)/shard_map/ppermute | solution.py:41
  84.2 8.6 %collective-permute-start.18 = (bf16[8,2,32,512]{3,2,1,0:T(8,128)(2,1)}, bf16[8,2,32,512]{3,2,1,0:T(8,128)(2,1)}, u32[]{:S(2)}, u32[]{:S(2)}) collective-permute-start(bf16[8,2,32,512]{3,2,1,0:T(8,128)(2,1)} %get-tuple-element.34), channel_id=1, source_target_pairs={{0,1},{1,0},{2,3},{3,2},{4,5},{5,4},{6,7},{7,6},{8,9},{9,8},{10,11... | collective-permute-start | bytes 1572872 | tf_op jit(solution)/shard_map/ppermute | solution.py:41
  85.2 9.1 %collective-permute-start.30 = (bf16[8,2,32,512]{3,2,1,0:T(8,128)(2,1)}, bf16[8,2,32,512]{3,2,1,0:T(8,128)(2,1)}, u32[]{:S(2)}, u32[]{:S(2)}) collective-permute-start(bf16[8,2,32,512]{3,2,1,0:T(8,128)(2,1)} %copy-done), channel_id=1, source_target_pairs={{0,16},{1,17},{2,18},{3,19},{4,20},{5,21},{6,22},{7,23},{8,24},{9,... | collective-permute-start | bytes 1572872 | tf_op jit(solution)/shard_map/ppermute | solution.py:41
  92.8 38.2 %collective-permute-start.19 = (bf16[2,8,2,32,512]{4,3,2,1,0:T(8,128)(2,1)S(1)}, bf16[2,8,2,32,512]{4,3,2,1,0:T(8,128)(2,1)S(1)}, u32[]{:S(2)}, u32[]{:S(2)}) collective-permute-start(bf16[2,8,2,32,512]{4,3,2,1,0:T(8,128)(2,1)S(1)} %pad_maximum_fusion.1.refs_6_), channel_id=1, source_target_pairs={{0,16},{1,17},{2,18},{3,19},{4,20},{5,21},{6,22},{7,23},{8,24},{9,... | collective-permute-start | bytes 3145736 | tf_op jit(solution)/shard_map/ppermute | solution.py:41
  94.3 20.0 %collective-permute-start.25 = (bf16[8,2,32,512]{3,2,1,0:T(8,128)(2,1)}, bf16[8,2,32,512]{3,2,1,0:T(8,128)(2,1)S(1)}, u32[]{:S(2)}, u32[]{:S(2)}) collective-permute-start(bf16[8,2,32,512]{3,2,1,0:T(8,128)(2,1)} %collective-permute-done.22.refs_7_), channel_id=1, source_target_pairs={{0,16},{1,17},{2,18},{3,19},{4,20},{5,21},{6,22},{7,23},{8,24},{9,... | collective-permute-start | bytes 1572872 | tf_op jit(solution)/shard_map/ppermute | solution.py:41
  94.3 19.9 %collective-permute-start.26 = (bf16[8,2,32,512]{3,2,1,0:T(8,128)(2,1)}, bf16[8,2,32,512]{3,2,1,0:T(8,128)(2,1)S(1)}, u32[]{:S(2)}, u32[]{:S(2)}) collective-permute-start(bf16[8,2,32,512]{3,2,1,0:T(8,128)(2,1)} %collective-permute-done.23.refs_8_), channel_id=1, source_target_pairs={{0,16},{1,17},{2,18},{3,19},{4,20},{5,21},{6,22},{7,23},{8,24},{9,... | collective-permute-start | bytes 1572872 | tf_op jit(solution)/shard_map/ppermute | solution.py:41
  96.1 34.9 %collective-permute-start.20 = (bf16[8,2,32,512]{3,2,1,0:T(8,128)(2,1)}, bf16[8,2,32,512]{3,2,1,0:T(8,128)(2,1)S(1)}, u32[]{:S(2)}, u32[]{:S(2)}) collective-permute-start(bf16[8,2,32,512]{3,2,1,0:T(8,128)(2,1)} %collective-permute-done.17.refs_7_), channel_id=1, source_target_pairs={{0,16},{1,17},{2,18},{3,19},{4,20},{5,21},{6,22},{7,23},{8,24},{9,... | collective-permute-start | bytes 1572872 | tf_op jit(solution)/shard_map/ppermute | solution.py:41
  96.3 34.7 %collective-permute-start.21 = (bf16[8,2,32,512]{3,2,1,0:T(8,128)(2,1)}, bf16[8,2,32,512]{3,2,1,0:T(8,128)(2,1)S(1)}, u32[]{:S(2)}, u32[]{:S(2)}) collective-permute-start(bf16[8,2,32,512]{3,2,1,0:T(8,128)(2,1)} %collective-permute-done.18.refs_8_), channel_id=1, source_target_pairs={{0,16},{1,17},{2,18},{3,19},{4,20},{5,21},{6,22},{7,23},{8,24},{9,... | collective-permute-start | bytes 1572872 | tf_op jit(solution)/shard_map/ppermute | solution.py:41
  (15 other events, 134.7 us)
where the time goes:
time: 148 us
  Pallas kernels  48.9 us (33%)
  starting transfers between devices  46.1 us (31%)
  waiting for transfers between devices  26 us (18%)
  other arithmetic  11.3 us (8%)
  local copies, waits for them, and re-layouts  9.37 us (6%)
  between operations  6.23 us (4%)
    pallas_call x3, Pallas kernels, transform(): pl.pallas_call(kernel, out_shape=jax.ShapeDtypeStruct((ROWS, PLANES, RUN,...  48.9 us
    ppermute x32, starting transfers between devices, exchange(): return lax.ppermute(value, ('wa', 'grid'), perm)  46.1 us
    ppermute x32, waiting for transfers between devices, exchange(): return lax.ppermute(value, ('wa', 'grid'), perm)  26 us
    concatenate x6, other arithmetic, body(): jnp.concatenate([near_[:, index], far_[:, index]], 0)  3.25 us
  transfers between devices with their start and end apart: 32, of which 9 were waited for; matrix products, arithmetic and copies ran while one was open for 10% of the time, Pallas kernels for 22%

commit v1 on v0

v1 whole, which is shorter than its diff:
```python
import jax
import jax.numpy as jnp
import numpy as np
from jax import lax
from jax.experimental import pallas as pl
from jax.experimental.pallas import tpu as pltpu
from jax.sharding import PartitionSpec as P

RUN = 3
G = 512
ROWS = 32
PLANES = 2

CLASSES = (((1, 3, 4, 12), (3, 4, 12, 1)), ((4, 12, 1, 3), (12, 1, 3, 4)))
ZCLASSES = ((2, 6), (6, 2))

TASKS = (
    ("s", 0, 1),
    ("p", 0, 1),
    ("s", 2, 3),
    ("p", 2, 3),
    ("p", 0, 2),
    ("p", 0, 3),
    ("p", 1, 2),
    ("p", 1, 3),
)


def term(a, b):
    return 8 * (a // 2) + 4 * (b // 2) + 2 * (a % 2) + b % 2


def block_masks():
    table = np.zeros((2, 2, 16), np.int32)
    for core in range(2):
        for half in range(2):
            for block in range(16):
                for step in range(4):
                    if block >> step & 1:
                        table[core, half, block] ^= CLASSES[core][half][step]
    return table


MASKS = block_masks()


def exchange(value, wa_mask, grid_mask):
    perm = []
    for wa in range(8):
        for grid in range(16):
            core = wa % 2
            perm.append((wa * 16 + grid, (wa ^ wa_mask(core)) * 16 + (grid ^ grid_mask(core))))
    return lax.ppermute(value, ("wa", "grid"), perm)


def swap_core(value):
    return exchange(value, lambda core: 1, lambda core: 0)


def swap_z(value, step):
    return exchange(value, lambda core: ZCLASSES[core][step], lambda core: 0)


def swap_grid(value, half, step):
    return exchange(value, lambda core: 0, lambda core: CLASSES[core][half][step])


def pick_kernel(ids, owner, jones, mine, other, semaphore):
    core = ids[0]
    copies = []
    for index in range(RUN):
        slot = owner[index] & 3
        for entry in range(4):
            for part, target in ((core, mine), (1 - core, other)):
                copies.append(
                    pltpu.make_async_copy(
                        jones.at[slot, entry, part], target.at[index, entry], semaphore.at[len(copies)]
                    )
                )
    for copy in copies:
        copy.start()
    for copy in copies:
        copy.wait()


def pick(ids, owner, jones):
    shape = jax.ShapeDtypeStruct((RUN, 4, ROWS, G), jnp.bfloat16)
    scalars = pl.BlockSpec(memory_space=pltpu.SMEM)
    return pl.pallas_call(
        pick_kernel,
        out_shape=(shape, shape),
        in_specs=[scalars, scalars, pl.BlockSpec(memory_space=pl.ANY)],
        out_specs=(pl.BlockSpec(memory_space=pltpu.VMEM), pl.BlockSpec(memory_space=pltpu.VMEM)),
        scratch_shapes=[pltpu.SemaphoreType.DMA((RUN * 8,))],
        compiler_params=pltpu.CompilerParams(vmem_limit_bytes=60 * 1024 * 1024),
        name="pick",
    )(ids, owner, jones)


def transform_kernel(index, *refs):
    ids, keep, ku, k30, k31, k40, k41, own3, own40, own41, far3, far40, far41 = refs[:13]
    out, fields, operator, real0, imag0, real1, imag1, left, staged, sem0, sem1, operator_sem, out_sem = refs[-13:]
    core, grid = ids[0], ids[1]
    own4 = (own40, own41)
    far4 = (far40, far41)
    k3 = (k30, k31)
    k4 = (k40, k41)
    field_sems = (sem0, sem1)
    pairs = ((real0, imag0), (real1, imag1))
    for half in range(2):
        for block in range(16):
            masks = (int(MASKS[0, half, block]), int(MASKS[1, half, block]))
            row = pl.multiple_of((grid ^ jnp.where(core == 0, masks[0], masks[1])) * ROWS, ROWS)
            far_row = pl.multiple_of((grid ^ jnp.where(core == 0, masks[1], masks[0])) * ROWS, ROWS)
            source = own3.at[half, block] if block < 8 else own4[half].at[block - 8]
            pltpu.make_async_copy(
                source, fields.at[half, core, :, pl.ds(row, ROWS)], field_sems[half]
            ).start()
            source = far3.at[half, block] if block < 8 else far4[half].at[block - 8]
            pltpu.make_async_copy(
                source, fields.at[half, 1 - core, :, pl.ds(far_row, ROWS)], field_sems[half]
            ).start()
    for half in range(2):
        for block in range(16):
            masks = (int(MASKS[0, half, block]), int(MASKS[1, half, block]))
            row = pl.multiple_of((grid ^ jnp.where(core == 0, masks[0], masks[1])) * ROWS, ROWS)
            source = k3[half].at[block] if block < 8 else k4[half].at[block - 8]
            pltpu.make_async_copy(source, operator.at[half, :, pl.ds(row, ROWS)], operator_sem).start()

    def products(task, pair):
        kind, a, b = task
        real, imag = pair
        for step in range(G // ROWS):
            rows = slice(step * ROWS, step * ROWS + ROWS)
            ar = fields[a // 2, 0, a % 2, rows].astype(jnp.float32)
            ai = fields[a // 2, 1, a % 2, rows].astype(jnp.float32)
            br = fields[b // 2, 0, b % 2, rows].astype(jnp.float32)
            bi = fields[b // 2, 1, b % 2, rows].astype(jnp.float32)
            if kind == "s":
                real[rows] = (ar * ar + ai * ai).astype(jnp.bfloat16)
                imag[rows] = (br * br + bi * bi).astype(jnp.bfloat16)
            else:
                real[rows] = (ar * br + ai * bi).astype(jnp.bfloat16)
                imag[rows] = (ai * br - ar * bi).astype(jnp.bfloat16)

    def put(plane, entry, columns, value, turned):
        rows = slice(entry * 64, entry * 64 + 64)
        left[plane, rows, columns] = (value * keep[entry]).astype(jnp.bfloat16)
        beside = slice(columns.start + G, columns.stop + G)
        left[plane, rows, beside] = (turned * keep[entry]).astype(jnp.bfloat16)

    def first_pass(task, pair):
        kind, a, b = task
        real, imag = pair
        for start in range(0, G, 256):
            columns = slice(start, start + 256)
            both_a = jnp.dot(ku[...], real[:, columns], preferred_element_type=jnp.float32)
            both_b = jnp.dot(ku[...], imag[:, columns], preferred_element_type=jnp.float32)
            for plane in range(PLANES):
                at = plane * 128
                xa, ya = both_a[at : at + 64], both_a[at + 64 : at + 128]
                xb, yb = both_b[at : at + 64], both_b[at + 64 : at + 128]
                if kind == "s":
                    put(plane, term(a, a), columns, xa, ya)
                    put(plane, term(b, b), columns, xb, yb)
                else:
                    put(plane, term(a, b), columns, xa + yb, ya - xb)
                    put(plane, term(b, a), columns, xa - yb, ya + xb)

    pltpu.make_async_copy(fields.at[0], fields.at[0], sem0).wait()
    products(TASKS[0], pairs[0])
    for step in range(8):
        if step == 1:
            pltpu.make_async_copy(fields.at[1], fields.at[1], sem1).wait()
        if step < 7:
            products(TASKS[step + 1], pairs[(step + 1) % 2])
        first_pass(TASKS[step], pairs[step % 2])

    pltpu.make_async_copy(operator, operator, operator_sem).wait()
    contract = (((1,), (1,)), ((), ()))
    for plane in range(PLANES):
        for group in range(4):
            rows = slice(group * 256, group * 256 + 256)
            total = lax.dot_general(
                left[plane, rows, 0:G], operator[plane, 0], contract, preferred_element_type=jnp.float32
            ) + lax.dot_general(
                left[plane, rows, G : 2 * G], operator[plane, 1], contract, preferred_element_type=jnp.float32
            )
            staged[plane, group * 4 : group * 4 + 4] = total.astype(jnp.bfloat16).reshape(4, ROWS, 2, G)
            for entry in range(group * 4, group * 4 + 4):
                pltpu.make_async_copy(
                    staged.at[plane, entry], out.at[:, plane, index, entry], out_sem
                ).start()
    pltpu.make_async_copy(staged, staged, out_sem).wait()


def transform(index, ids, keep, ku, operators, own, far, previous):
    anywhere = pl.BlockSpec(memory_space=pl.ANY)
    scalars = pl.BlockSpec(memory_space=pltpu.SMEM)
    operands = [ids, keep, ku, *operators, *own, *far]
    specs = [scalars, scalars, pl.BlockSpec(memory_space=pltpu.VMEM)] + [anywhere] * 10
    aliases = {}
    if previous is not None:
        aliases = {len(operands): 0}
        operands.append(previous)
        specs.append(anywhere)

    def kernel(*refs):
        transform_kernel(index, *refs)

    return pl.pallas_call(
        kernel,
        out_shape=jax.ShapeDtypeStruct((ROWS, PLANES, RUN, 16, 2, G), jnp.bfloat16),
        in_specs=specs,
        out_specs=anywhere,
        input_output_aliases=aliases,
        scratch_shapes=[
            pltpu.VMEM((2, 2, 2, G, G), jnp.bfloat16),
            pltpu.VMEM((PLANES, 2, G, G), jnp.bfloat16),
            pltpu.VMEM((G, G), jnp.bfloat16),
            pltpu.VMEM((G, G), jnp.bfloat16),
            pltpu.VMEM((G, G), jnp.bfloat16),
            pltpu.VMEM((G, G), jnp.bfloat16),
            pltpu.VMEM((PLANES, 16 * 64, 2 * G), jnp.bfloat16),
            pltpu.VMEM((PLANES, 16, ROWS, 2, G), jnp.bfloat16),
            pltpu.SemaphoreType.DMA,
            pltpu.SemaphoreType.DMA,
            pltpu.SemaphoreType.DMA,
            pltpu.SemaphoreType.DMA,
        ],
        compiler_params=pltpu.CompilerParams(vmem_limit_bytes=24 * 1024 * 1024),
        cost_estimate=pl.CostEstimate(flops=1_000_000, bytes_accessed=1_000_000, transcendentals=0),
        name="transform",
    )(*operands)


def after(value, *others):
    return lax.optimization_barrier((value, *others))[0]


def choose(flags, yes, no):
    return jnp.where(flags[:, None, None, None], yes, no)


def body(jones, owner, mask, w_operator):
    wa = lax.axis_index("wa")
    grid = lax.axis_index("grid")
    core = wa & 1
    ids = jnp.stack([core, grid]).astype(jnp.int32)
    mine, other = pick(ids, owner, jones)

    planes = [w_operator[half][None] for half in range(2)]
    planes = [jnp.concatenate([planes[half], swap_grid(planes[half], half, 0)], 0) for half in range(2)]

    holder = owner[:RUN] >> 2
    rows = choose((holder & 1) == core, mine, swap_core(other))
    first = ZCLASSES[0][0] + core * (ZCLASSES[1][0] - ZCLASSES[0][0])
    apart = (holder ^ wa) & 6
    rows = after(rows, *planes)
    planes = [jnp.concatenate([planes[half], swap_grid(planes[half], half, 1)], 0) for half in range(2)]
    rows = choose(apart == 0, rows, swap_z(rows, 0))
    rows = after(rows, *planes)
    planes = [jnp.concatenate([planes[half], swap_grid(planes[half], half, 2)], 0) for half in range(2)]
    rows = choose((apart == 0) | (apart == first), rows, swap_z(rows, 1))
    rows = after(rows, *planes)
    last_planes = [swap_grid(planes[half], half, 3) for half in range(2)]
    operators = (*planes, *last_planes)

    streams = []
    for half in range(2):
        stream = rows[None, :, 2 * half : 2 * half + 2]
        stream = jnp.concatenate([stream, swap_grid(stream, half, 0)], 0)
        stream = jnp.concatenate([stream, swap_grid(stream, half, 1)], 0)
        stream = after(stream, *last_planes)
        streams.append((stream, swap_grid(stream, half, 2)))

    kr, ki = w_operator[:, 0], w_operator[:, 1]
    plain = jnp.stack([kr, ki], 2).reshape(PLANES, 2 * ROWS, G)
    turned = jnp.stack([-ki, kr], 2).reshape(PLANES, 2 * ROWS, G)
    ku = jnp.concatenate([plain, turned], 1).reshape(PLANES * 4 * ROWS, G)
    keep = mask.reshape(RUN, 16).astype(jnp.float32)

    lows = []
    highs = []
    for index in range(RUN):
        low = jnp.stack([jnp.concatenate([near[:, index], far[:, index]], 0) for near, far in streams])
        send = [low[half] for half in range(2)]
        if index == 2:
            send = [after(send[half], highs[0][half]) for half in range(2)]
        lows.append(low)
        highs.append([swap_grid(send[half], half, 3) for half in range(2)])
    result = None
    for index in range(RUN):
        own = (lows[index], *highs[index])
        sent = highs[index]
        if result is not None:
            sent = [after(one, result) for one in sent]
        far = (swap_core(lows[index]), *[swap_core(one) for one in sent])
        result = transform(index, ids, keep[index], ku, operators, own, far, result)
    return result


def solution(mesh):
    return jax.shard_map(
        body,
        mesh=mesh,
        in_specs=(P("wa", None, None, "grid", None), P(), P(), P("wa", None, "grid", None)),
        out_specs=P("grid", "wa", None, None, None, None),
        check_vma=False,
    )
```

time: 148 us -> 134 us (0.905)
  Pallas kernels: 48.9 us -> 36.8 us
  waiting for transfers between devices: 26 us -> 33.6 us
  between operations: 6.23 us -> 0.55 us
  starting transfers between devices: 46.1 us -> 43.5 us
    pallas_call x3, Pallas kernels: 48.9 us -> 34 us  [transform(): pl.pallas_call(kernel, out_shape=jax.ShapeDtypeStruct((ROWS, PLANES, RUN,...]
    ppermute x32, waiting for transfers between devices: 26 us -> 33.6 us  [exchange(): return lax.ppermute(value, ('wa', 'grid'), perm)]
    pallas_call x0 -> x1, Pallas kernels: none -> 2.86 us  [pick(): pl.pallas_call(pick_kernel, out_shape=(shape, shape), in_specs=[scalars,...]
    squeeze x7, local copies, waits for them, and re-layouts: 0.51 us -> 3.34 us  [the longest x2 1.55 us: body(): near[:, index]]
    ppermute x32, starting transfers between devices: 46.1 us -> 43.5 us  [exchange(): return lax.ppermute(value, ('wa', 'grid'), perm)]
    another operation x5 -> x6, other arithmetic: 3.85 us -> 2.04 us  [the longest x5 1.39 us: body(): jnp.stack([jnp.concatenate([near[:, index], far[:, index]], 0) for near,...]
    concatenate x17 -> x14, other arithmetic: 5.38 us -> 5.95 us  [the longest x4 5.53 us: body(): jnp.concatenate([near[:, index], far[:, index]], 0)]
  transfers between devices with their start and end apart: 32 -> 32, of which waited for: 9 -> 13; matrix products, arithmetic and copies ran while one was open for 10% -> 9% of each run, Pallas kernels for 22% -> 17%
where the time goes in v1:
time: 134 us; the launch traced here: 133 us
  starting transfers between devices  43.5 us (32%)
  Pallas kernels  36.8 us (27%)
  waiting for transfers between devices  33.6 us (25%)
  other arithmetic  10.4 us (8%)
  local copies, waits for them, and re-layouts  8.07 us (6%)
    ppermute x32, starting transfers between devices, exchange(): return lax.ppermute(value, ('wa', 'grid'), perm)  43.5 us
    pallas_call x3, Pallas kernels, transform(): pl.pallas_call(kernel, out_shape=jax.ShapeDtypeStruct((ROWS, PLANES, RUN,...  34 us
    ppermute x32, waiting for transfers between devices, exchange(): return lax.ppermute(value, ('wa', 'grid'), perm)  33.6 us
    concatenate x4, other arithmetic, body(): jnp.concatenate([near[:, index], far[:, index]], 0)  5.53 us
    unnamed x14, local copies, waits for them, and re-layouts  3.44 us
    pallas_call x1, Pallas kernels, pick(): pl.pallas_call(pick_kernel, out_shape=(shape, shape), in_specs=[scalars,...  2.86 us
  transfers between devices with their start and end apart: 32, of which 13 were waited for; matrix products, arithmetic and copies ran while one was open for 9% of the time, Pallas kernels for 17%

profile of v1, /device:TPU:1, one launch (start us, length us, event | category | flops | bytes accessed | tf_op | source)
XLA Modules:
  0.0 132.9 jit_solution(12367490794347795215)
XLA Ops:
  0.7 2.9 %pick.1 = (bf16[3,4,32,512]{3,2,1,0:T(8,128)(2,1)}, bf16[3,4,32,512]{3,2,1,0:T(8,128)(2,1)}) custom-call(s32[2]{0:T(128)} %pad_add_fusion.ids.refs_0_, s32[32]{0:T(128)} %owner.1, bf16[4,4,2,32,512]{4,3,2,1,0:T(8,128)(2,1)} %jones.1), custom_call_target="tpu_custom_call" | custom-call | tf_op jit(solution)/shard_map/pick/pallas_call | solution.py:89
  7.4 1.9 %collective-permute-start.3 = (bf16[1,2,32,512]{3,2,1,0:T(8,128)(2,1)S(1)}, bf16[1,2,32,512]{3,2,1,0:T(8,128)(2,1)S(1)}, u32[]{:S(2)}, u32[]{:S(2)}) collective-permute-start(bf16[1,2,32,512]{3,2,1,0:T(8,128)(2,1)S(1)} %get-tuple-element.57), channel_id=1, source_target_pairs={{0,3},{1,2},{2,1},{3,0},{4,7},{5,6},{6,5},{7,4},{8,11},{9,10},{10,... | collective-permute-start | bytes 196616 | tf_op jit(solution)/shard_map/ppermute | solution.py:53
  10.0 2.0 %collective-permute-done.3 = bf16[1,2,32,512]{3,2,1,0:T(8,128)(2,1)S(1)} collective-permute-done((bf16[1,2,32,512]{3,2,1,0:T(8,128)(2,1)S(1)}, bf16[1,2,32,512]{3,2,1,0:T(8,128)(2,1)S(1)}, u32[]{:S(2)}, u32[]{:S(2)}) %collective-permute-start.3) | collective-permute-done | bytes 65568 | tf_op jit(solution)/shard_map/ppermute | solution.py:53
  13.1 3.8 %collective-permute-start.9 = (bf16[3,4,32,512]{3,2,1,0:T(8,128)(2,1)S(1)}, bf16[3,4,32,512]{3,2,1,0:T(8,128)(2,1)S(1)}, u32[]{:S(2)}, u32[]{:S(2)}) collective-permute-start(bf16[3,4,32,512]{3,2,1,0:T(8,128)(2,1)S(1)} %broadcast_select_fusion), channel_id=1, source_target_pairs={{0,32},{1,33},{2,34},{3,35},{4,36},{5,37},{6,38},{7,39},{8,40},{9,... | collective-permute-start | bytes 1179656 | tf_op jit(solution)/shard_map/ppermute | solution.py:53
  17.9 1.9 %collective-permute-start.1 = (bf16[2,2,32,512]{3,2,1,0:T(8,128)(2,1)S(1)}, bf16[2,2,32,512]{3,2,1,0:T(8,128)(2,1)S(1)}, u32[]{:S(2)}, u32[]{:S(2)}) collective-permute-start(bf16[2,2,32,512]{3,2,1,0:T(8,128)(2,1)S(1)} %pad_maximum_fusion.20), channel_id=1, source_target_pairs={{0,3},{1,2},{2,1},{3,0},{4,7},{5,6},{6,5},{7,4},{8,11},{9,10},{10,... | collective-permute-start | bytes 393224 | tf_op jit(solution)/shard_map/ppermute | solution.py:53
  21.1 2.5 %collective-permute-start.5 = (bf16[4,2,32,512]{3,2,1,0:T(8,128)(2,1)S(1)}, bf16[4,2,32,512]{3,2,1,0:T(8,128)(2,1)S(1)}, u32[]{:S(2)}, u32[]{:S(2)}) collective-permute-start(bf16[4,2,32,512]{3,2,1,0:T(8,128)(2,1)S(1)} %pad_maximum_fusion.17), channel_id=1, source_target_pairs={{0,12},{1,13},{2,14},{3,15},{4,8},{5,9},{6,10},{7,11},{8,4},{9,5},... | collective-permute-start | bytes 786440 | tf_op jit(solution)/shard_map/ppermute | solution.py:53
  23.9 4.0 %collective-permute-done.5 = bf16[4,2,32,512]{3,2,1,0:T(8,128)(2,1)S(1)} collective-permute-done((bf16[4,2,32,512]{3,2,1,0:T(8,128)(2,1)S(1)}, bf16[4,2,32,512]{3,2,1,0:T(8,128)(2,1)S(1)}, u32[]{:S(2)}, u32[]{:S(2)}) %collective-permute-start.5) | collective-permute-done | bytes 262176 | tf_op jit(solution)/shard_map/ppermute | solution.py:53
  30.9 1.8 %collective-permute-start.14 = (bf16[1,3,2,32,512]{4,3,2,1,0:T(8,128)(2,1)S(1)}, bf16[1,3,2,32,512]{4,3,2,1,0:T(8,128)(2,1)S(1)}, u32[]{:S(2)}, u32[]{:S(2)}) collective-permute-start(bf16[1,3,2,32,512]{4,3,2,1,0:T(8,128)(2,1)S(1)} %get-tuple-element.56), channel_id=1, source_target_pairs={{0,3},{1,2},{2,1},{3,0},{4,7},{5,6},{6,5},{7,4},{8,11},{9,10},{10,... | collective-permute-start | bytes 589832 | tf_op jit(solution)/shard_map/ppermute | solution.py:53
  32.7 4.0 %collective-permute-done.14 = bf16[1,3,2,32,512]{4,3,2,1,0:T(8,128)(2,1)S(1)} collective-permute-done((bf16[1,3,2,32,512]{4,3,2,1,0:T(8,128)(2,1)S(1)}, bf16[1,3,2,32,512]{4,3,2,1,0:T(8,128)(2,1)S(1)}, u32[]{:S(2)}, u32[]{:S(2)}) %collective-permute-start.14) | collective-permute-done | bytes 196640 | tf_op jit(solution)/shard_map/ppermute | solution.py:53
  36.9 2.2 %collective-permute-start.6 = (bf16[8,2,32,512]{3,2,1,0:T(8,128)(2,1)S(1)}, bf16[8,2,32,512]{3,2,1,0:T(8,128)(2,1)S(1)}, u32[]{:S(2)}, u32[]{:S(2)}) collective-permute-start(bf16[8,2,32,512]{3,2,1,0:T(8,128)(2,1)S(1)} %pad_maximum_fusion.5.refs_3_), channel_id=1, source_target_pairs={{0,12},{1,13},{2,14},{3,15},{4,8},{5,9},{6,10},{7,11},{8,4},{9,5},... | collective-permute-start | bytes 1572872 | tf_op jit(solution)/shard_map/ppermute | solution.py:53
  40.9 4.4 %collective-permute-done.15 = bf16[2,3,2,32,512]{4,3,2,1,0:T(8,128)(2,1)S(1)} collective-permute-done((bf16[2,3,2,32,512]{4,3,2,1,0:T(8,128)(2,1)S(1)}, bf16[2,3,2,32,512]{4,3,2,1,0:T(8,128)(2,1)S(1)}, u32[]{:S(2)}, u32[]{:S(2)}) %collective-permute-start.15) | collective-permute-done | bytes 393248 | tf_op jit(solution)/shard_map/ppermute | solution.py:53
  46.3 3.0 %collective-permute-start.16 = (bf16[4,3,2,32,512]{4,3,2,0,1:T(8,128)(2,1)S(1)}, bf16[4,3,2,32,512]{4,3,2,0,1:T(8,128)(2,1)S(1)}, u32[]{:S(2)}, u32[]{:S(2)}) collective-permute-start(bf16[4,3,2,32,512]{4,3,2,0,1:T(8,128)(2,1)S(1)} %copy.13), channel_id=1, source_target_pairs={{0,12},{1,13},{2,14},{3,15},{4,8},{5,9},{6,10},{7,11},{8,4},{9,5},... | collective-permute-start | bytes 2359304 | tf_op jit(solution)/shard_map/ppermute | solution.py:53
  49.5 2.1 %collective-permute-start.13 = (bf16[4,3,2,32,512]{4,3,2,0,1:T(8,128)(2,1)S(1)}, bf16[4,3,2,32,512]{4,3,2,0,1:T(8,128)(2,1)S(1)}, u32[]{:S(2)}, u32[]{:S(2)}) collective-permute-start(bf16[4,3,2,32,512]{4,3,2,0,1:T(8,128)(2,1)S(1)} %pad_maximum_fusion.3), channel_id=1, source_target_pairs={{0,4},{1,5},{2,6},{3,7},{4,0},{5,1},{6,2},{7,3},{8,12},{9,13},{10,... | collective-permute-start | bytes 2359304 | tf_op jit(solution)/shard_map/ppermute | solution.py:53
  53.1 10.2 %collective-permute-done.16 = bf16[4,3,2,32,512]{4,3,2,0,1:T(8,128)(2,1)S(1)} collective-permute-done((bf16[4,3,2,32,512]{4,3,2,0,1:T(8,128)(2,1)S(1)}, bf16[4,3,2,32,512]{4,3,2,0,1:T(8,128)(2,1)S(1)}, u32[]{:S(2)}, u32[]{:S(2)}) %collective-permute-start.16) | collective-permute-done | bytes 786464 | tf_op jit(solution)/shard_map/ppermute | solution.py:53
  65.1 7.9 %collective-permute-start.25 = (bf16[2,8,2,32,512]{4,3,2,1,0:T(8,128)(2,1)S(1)}, bf16[2,8,2,32,512]{4,3,2,1,0:T(8,128)(2,1)S(1)}, u32[]{:S(2)}, u32[]{:S(2)}) collective-permute-start(bf16[2,8,2,32,512]{4,3,2,1,0:T(8,128)(2,1)S(1)} %pad_maximum_fusion.2.refs_7_), channel_id=1, source_target_pairs={{0,16},{1,17},{2,18},{3,19},{4,20},{5,21},{6,22},{7,23},{8,24},{9,... | collective-permute-start | bytes 3145736 | tf_op jit(solution)/shard_map/ppermute | solution.py:53
  73.1 2.2 %collective-permute-start.17 = (bf16[8,2,32,512]{3,2,1,0:T(8,128)(2,1)S(1)}, bf16[8,2,32,512]{3,2,1,0:T(8,128)(2,1)}, u32[]{:S(2)}, u32[]{:S(2)}) collective-permute-start(bf16[8,2,32,512]{3,2,1,0:T(8,128)(2,1)S(1)} %get-tuple-element.44), channel_id=1, source_target_pairs={{0,12},{1,13},{2,14},{3,15},{4,8},{5,9},{6,10},{7,11},{8,4},{9,5},... | collective-permute-start | bytes 1572872 | tf_op jit(solution)/shard_map/ppermute | solution.py:53
  79.5 2.0 %collective-permute-done.19.refs_9_ = bf16[8,2,32,512]{3,2,1,0:T(8,128)(2,1)} collective-permute-done((bf16[8,2,32,512]{3,2,1,0:T(8,128)(2,1)S(1)}, bf16[8,2,32,512]{3,2,1,0:T(8,128)(2,1)}, u32[]{:S(2)}, u32[]{:S(2)}) %collective-permute-start.19) | collective-permute-done | bytes 524320 | tf_op jit(solution)/shard_map/ppermute | solution.py:53
  81.5 2.2 %collective-permute-start.22 = (bf16[8,2,32,512]{3,2,1,0:T(8,128)(2,1)}, bf16[8,2,32,512]{3,2,1,0:T(8,128)(2,1)}, u32[]{:S(2)}, u32[]{:S(2)}) collective-permute-start(bf16[8,2,32,512]{3,2,1,0:T(8,128)(2,1)} %get-tuple-element.49), channel_id=1, source_target_pairs={{0,12},{1,13},{2,14},{3,15},{4,8},{5,9},{6,10},{7,11},{8,4},{9,5},... | collective-permute-start | bytes 1572872 | tf_op jit(solution)/shard_map/ppermute | solution.py:53
  85.2 1.9 %pad_maximum_fusion.8 = (bf16[8,2,32,512]{3,2,1,0:T(8,128)(2,1)}, bf16[1,8,2,32,512]{4,3,2,1,0:T(8,128)(2,1)S(1)}) fusion(bf16[4,2,32,512]{3,2,1,0:T(8,128)(2,1)} %get-tuple-element.42, bf16[4,2,32,512]{3,2,1,0:T(8,128)(2,1)} %get-tuple-element.39), kind=kLoop, calls=%fused_computation.8 | loop fusion | flops 262144 | bytes 1572864 | tf_op jit(solution)/shard_map/concatenate | solution.py:286
  87.1 1.9 %pad_maximum_fusion.7 = (bf16[8,2,32,512]{3,2,1,0:T(8,128)(2,1)}, bf16[1,8,2,32,512]{4,3,2,1,0:T(8,128)(2,1)S(1)}) fusion(bf16[4,2,32,512]{3,2,1,0:T(8,128)(2,1)} %get-tuple-element.36, bf16[4,2,32,512]{3,2,1,0:T(8,128)(2,1)} %get-tuple-element.33), kind=kLoop, calls=%fused_computation.7 | loop fusion | flops 262144 | bytes 1572864 | tf_op jit(solution)/shard_map/concatenate | solution.py:286
  92.5 11.8 %transform.3.refs_13_ = bf16[32,2,3,16,2,512]{5,4,3,2,1,0:T(2,128)(2,1)} custom-call(s32[2]{0:T(128)S(1)} %copy-done.4, f32[16]{0:T(128)S(1)} %squeeze.60.refs_1_, bf16[256,512]{1,0:T(8,128)(2,1)S(1)} %bitcast.53, bf16[8,2,32,512]{3,2,1,0:T(8,128)(2,1)S(1)} %pad_maximum_fusion.5.refs_3_, bf16[8,2,32,512]{3,2,1,0:T(8,128)(2,1)S(1)} %pad_maximum_fusion.6.refs_4_, ...), custom_call_target="tpu_custom_call" | custom-call | flops 1000000 | bytes 1000000 | tf_op jit(solution)/shard_map/transform/pallas_call | solution.py:211
  105.1 2.2 %collective-permute-start.18 = (bf16[8,2,32,512]{3,2,1,0:T(8,128)(2,1)}, bf16[8,2,32,512]{3,2,1,0:T(8,128)(2,1)}, u32[]{:S(2)}, u32[]{:S(2)}) collective-permute-start(bf16[8,2,32,512]{3,2,1,0:T(8,128)(2,1)} %get-tuple-element.25), channel_id=1, source_target_pairs={{0,12},{1,13},{2,14},{3,15},{4,8},{5,9},{6,10},{7,11},{8,4},{9,5},... | collective-permute-start | bytes 1572872 | tf_op jit(solution)/shard_map/ppermute | solution.py:53
  107.4 11.1 %transform.4.refs_13_ = bf16[32,2,3,16,2,512]{5,4,3,2,1,0:T(2,128)(2,1)} custom-call(s32[2]{0:T(128)S(1)} %copy-done.4, f32[16]{0:T(128)S(1)} %squeeze.55.refs_1_, bf16[256,512]{1,0:T(8,128)(2,1)S(1)} %bitcast.54, bf16[8,2,32,512]{3,2,1,0:T(8,128)(2,1)S(1)} %pad_maximum_fusion.5.refs_3_, ...), custom_call_target="tpu_custom_call", output_to_operand_aliasing={{}: (13, {})} | custom-call | flops 1000000 | bytes 1000000 | tf_op jit(solution)/shard_map/transform/pallas_call | solution.py:211
  121.6 11.1 %transform.5 = bf16[32,2,3,16,2,512]{5,4,3,2,1,0:T(2,128)(2,1)} custom-call(s32[2]{0:T(128)S(1)} %copy-done.4, f32[16]{0:T(128)S(1)} %squeeze.46.refs_1_, bf16[256,512]{1,0:T(8,128)(2,1)S(1)} %bitcast.55, bf16[8,2,32,512]{3,2,1,0:T(8,128)(2,1)S(1)} %pad_maximum_fusion.5.refs_3_, ...), custom_call_target="tpu_custom_call", output_to_operand_aliasing={{}: (13, {})} | custom-call | flops 1000000 | bytes 1000000 | tf_op jit(solution)/shard_map/transform/pallas_call | solution.py:211
  (101 shorter events, 31.4 us)
Async XLA Ops:
  3.5 8.5 %collective-permute-start.8 = (bf16[3,4,32,512]{3,2,1,0:T(8,128)(2,1)}, bf16[3,4,32,512]{3,2,1,0:T(8,128)(2,1)S(1)}, u32[]{:S(2)}, u32[]{:S(2)}) collective-permute-start(bf16[3,4,32,512]{3,2,1,0:T(8,128)(2,1)} %get-tuple-element.19), channel_id=1, source_target_pairs={{0,16},{1,17},{2,18},{3,19},{4,20},{5,21},{6,22},{7,23},{8,24},{9,... | collective-permute-start | bytes 1179656 | tf_op jit(solution)/shard_map/ppermute | solution.py:53
  13.1 10.5 %collective-permute-start.9 = (bf16[3,4,32,512]{3,2,1,0:T(8,128)(2,1)S(1)}, bf16[3,4,32,512]{3,2,1,0:T(8,128)(2,1)S(1)}, u32[]{:S(2)}, u32[]{:S(2)}) collective-permute-start(bf16[3,4,32,512]{3,2,1,0:T(8,128)(2,1)S(1)} %broadcast_select_fusion), channel_id=1, source_target_pairs={{0,32},{1,33},{2,34},{3,35},{4,36},{5,37},{6,38},{7,39},{8,40},{9,... | collective-permute-start | bytes 1179656 | tf_op jit(solution)/shard_map/ppermute | solution.py:53
  17.9 5.7 %collective-permute-start.1 = (bf16[2,2,32,512]{3,2,1,0:T(8,128)(2,1)S(1)}, bf16[2,2,32,512]{3,2,1,0:T(8,128)(2,1)S(1)}, u32[]{:S(2)}, u32[]{:S(2)}) collective-permute-start(bf16[2,2,32,512]{3,2,1,0:T(8,128)(2,1)S(1)} %pad_maximum_fusion.20), channel_id=1, source_target_pairs={{0,3},{1,2},{2,1},{3,0},{4,7},{5,6},{6,5},{7,4},{8,11},{9,10},{10,... | collective-permute-start | bytes 393224 | tf_op jit(solution)/shard_map/ppermute | solution.py:53
  21.1 6.8 %collective-permute-start.5 = (bf16[4,2,32,512]{3,2,1,0:T(8,128)(2,1)S(1)}, bf16[4,2,32,512]{3,2,1,0:T(8,128)(2,1)S(1)}, u32[]{:S(2)}, u32[]{:S(2)}) collective-permute-start(bf16[4,2,32,512]{3,2,1,0:T(8,128)(2,1)S(1)} %pad_maximum_fusion.17), channel_id=1, source_target_pairs={{0,12},{1,13},{2,14},{3,15},{4,8},{5,9},{6,10},{7,11},{8,4},{9,5},... | collective-permute-start | bytes 786440 | tf_op jit(solution)/shard_map/ppermute | solution.py:53
  23.7 7.0 %collective-permute-start.10 = (bf16[3,4,32,512]{3,2,1,0:T(8,128)(2,1)S(1)}, bf16[3,4,32,512]{3,2,1,0:T(8,128)(2,1)S(1)}, u32[]{:S(2)}, u32[]{:S(2)}) collective-permute-start(bf16[3,4,32,512]{3,2,1,0:T(8,128)(2,1)S(1)} %broadcast_select_fusion.1), channel_id=1, source_target_pairs={{0,96},{1,97},{2,98},{3,99},{4,100},{5,101},{6,102},{7,103},{8,104... | collective-permute-start | bytes 1179656 | tf_op jit(solution)/shard_map/ppermute | solution.py:53
  23.8 5.6 %collective-permute-start.2 = (bf16[4,2,32,512]{3,2,1,0:T(8,128)(2,1)S(1)}, bf16[4,2,32,512]{3,2,1,0:T(8,128)(2,1)S(1)}, u32[]{:S(2)}, u32[]{:S(2)}) collective-permute-start(bf16[4,2,32,512]{3,2,1,0:T(8,128)(2,1)S(1)} %pad_maximum_fusion.16), channel_id=1, source_target_pairs={{0,4},{1,5},{2,6},{3,7},{4,0},{5,1},{6,2},{7,3},{8,12},{9,13},{10,... | collective-permute-start | bytes 786440 | tf_op jit(solution)/shard_map/ppermute | solution.py:53
  30.9 5.8 %collective-permute-start.14 = (bf16[1,3,2,32,512]{4,3,2,1,0:T(8,128)(2,1)S(1)}, bf16[1,3,2,32,512]{4,3,2,1,0:T(8,128)(2,1)S(1)}, u32[]{:S(2)}, u32[]{:S(2)}) collective-permute-start(bf16[1,3,2,32,512]{4,3,2,1,0:T(8,128)(2,1)S(1)} %get-tuple-element.56), channel_id=1, source_target_pairs={{0,3},{1,2},{2,1},{3,0},{4,7},{5,6},{6,5},{7,4},{8,11},{9,10},{10,... | collective-permute-start | bytes 589832 | tf_op jit(solution)/shard_map/ppermute | solution.py:53
  32.6 6.5 %collective-permute-start.11 = (bf16[1,3,2,32,512]{4,3,2,0,1:T(8,128)(2,1)S(1)}, bf16[1,3,2,32,512]{4,3,2,0,1:T(8,128)(2,1)S(1)}, u32[]{:S(2)}, u32[]{:S(2)}) collective-permute-start(bf16[1,3,2,32,512]{4,3,2,0,1:T(8,128)(2,1)S(1)} %get-tuple-element.55), channel_id=1, source_target_pairs={{0,1},{1,0},{2,3},{3,2},{4,5},{5,4},{6,7},{7,6},{8,9},{9,8},{10,11... | collective-permute-start | bytes 589832 | tf_op jit(solution)/shard_map/ppermute | solution.py:53
  36.7 8.6 %collective-permute-start.15 = (bf16[2,3,2,32,512]{4,3,2,1,0:T(8,128)(2,1)S(1)}, bf16[2,3,2,32,512]{4,3,2,1,0:T(8,128)(2,1)S(1)}, u32[]{:S(2)}, u32[]{:S(2)}) collective-permute-start(bf16[2,3,2,32,512]{4,3,2,1,0:T(8,128)(2,1)S(1)} %pad_maximum_fusion.14), channel_id=1, source_target_pairs={{0,4},{1,5},{2,6},{3,7},{4,0},{5,1},{6,2},{7,3},{8,12},{9,13},{10,... | collective-permute-start | bytes 1179656 | tf_op jit(solution)/shard_map/ppermute | solution.py:53
  36.8 9.2 %collective-permute-start.7 = (bf16[8,2,32,512]{3,2,1,0:T(8,128)(2,1)S(1)}, bf16[8,2,32,512]{3,2,1,0:T(8,128)(2,1)S(1)}, u32[]{:S(2)}, u32[]{:S(2)}) collective-permute-start(bf16[8,2,32,512]{3,2,1,0:T(8,128)(2,1)S(1)} %pad_maximum_fusion.6.refs_4_), channel_id=1, source_target_pairs={{0,1},{1,0},{2,3},{3,2},{4,5},{5,4},{6,7},{7,6},{8,9},{9,8},{10,11... | collective-permute-start | bytes 1572872 | tf_op jit(solution)/shard_map/ppermute | solution.py:53
  36.9 9.3 %collective-permute-start.6 = (bf16[8,2,32,512]{3,2,1,0:T(8,128)(2,1)S(1)}, bf16[8,2,32,512]{3,2,1,0:T(8,128)(2,1)S(1)}, u32[]{:S(2)}, u32[]{:S(2)}) collective-permute-start(bf16[8,2,32,512]{3,2,1,0:T(8,128)(2,1)S(1)} %pad_maximum_fusion.5.refs_3_), channel_id=1, source_target_pairs={{0,12},{1,13},{2,14},{3,15},{4,8},{5,9},{6,10},{7,11},{8,4},{9,5},... | collective-permute-start | bytes 1572872 | tf_op jit(solution)/shard_map/ppermute | solution.py:53
  39.2 10.2 %collective-permute-start.12 = (bf16[2,3,2,32,512]{4,3,2,0,1:T(8,128)(2,1)S(1)}, bf16[2,3,2,32,512]{4,3,2,0,1:T(8,128)(2,1)S(1)}, u32[]{:S(2)}, u32[]{:S(2)}) collective-permute-start(bf16[2,3,2,32,512]{4,3,2,0,1:T(8,128)(2,1)S(1)} %pad_maximum_fusion.13), channel_id=1, source_target_pairs={{0,3},{1,2},{2,1},{3,0},{4,7},{5,6},{6,5},{7,4},{8,11},{9,10},{10,... | collective-permute-start | bytes 1179656 | tf_op jit(solution)/shard_map/ppermute | solution.py:53
  46.3 16.9 %collective-permute-start.16 = (bf16[4,3,2,32,512]{4,3,2,0,1:T(8,128)(2,1)S(1)}, bf16[4,3,2,32,512]{4,3,2,0,1:T(8,128)(2,1)S(1)}, u32[]{:S(2)}, u32[]{:S(2)}) collective-permute-start(bf16[4,3,2,32,512]{4,3,2,0,1:T(8,128)(2,1)S(1)} %copy.13), channel_id=1, source_target_pairs={{0,12},{1,13},{2,14},{3,15},{4,8},{5,9},{6,10},{7,11},{8,4},{9,5},... | collective-permute-start | bytes 2359304 | tf_op jit(solution)/shard_map/ppermute | solution.py:53
  49.5 14.7 %collective-permute-start.13 = (bf16[4,3,2,32,512]{4,3,2,0,1:T(8,128)(2,1)S(1)}, bf16[4,3,2,32,512]{4,3,2,0,1:T(8,128)(2,1)S(1)}, u32[]{:S(2)}, u32[]{:S(2)}) collective-permute-start(bf16[4,3,2,32,512]{4,3,2,0,1:T(8,128)(2,1)S(1)} %pad_maximum_fusion.3), channel_id=1, source_target_pairs={{0,4},{1,5},{2,6},{3,7},{4,0},{5,1},{6,2},{7,3},{8,12},{9,13},{10,... | collective-permute-start | bytes 2359304 | tf_op jit(solution)/shard_map/ppermute | solution.py:53
  65.1 18.6 %collective-permute-start.25 = (bf16[2,8,2,32,512]{4,3,2,1,0:T(8,128)(2,1)S(1)}, bf16[2,8,2,32,512]{4,3,2,1,0:T(8,128)(2,1)S(1)}, u32[]{:S(2)}, u32[]{:S(2)}) collective-permute-start(bf16[2,8,2,32,512]{4,3,2,1,0:T(8,128)(2,1)S(1)} %pad_maximum_fusion.2.refs_7_), channel_id=1, source_target_pairs={{0,16},{1,17},{2,18},{3,19},{4,20},{5,21},{6,22},{7,23},{8,24},{9,... | collective-permute-start | bytes 3145736 | tf_op jit(solution)/shard_map/ppermute | solution.py:53
  73.0 8.5 %collective-permute-start.19 = (bf16[8,2,32,512]{3,2,1,0:T(8,128)(2,1)S(1)}, bf16[8,2,32,512]{3,2,1,0:T(8,128)(2,1)}, u32[]{:S(2)}, u32[]{:S(2)}) collective-permute-start(bf16[8,2,32,512]{3,2,1,0:T(8,128)(2,1)S(1)} %get-tuple-element.46), channel_id=1, source_target_pairs={{0,1},{1,0},{2,3},{3,2},{4,5},{5,4},{6,7},{7,6},{8,9},{9,8},{10,11... | collective-permute-start | bytes 1572872 | tf_op jit(solution)/shard_map/ppermute | solution.py:53
  73.1 10.6 %collective-permute-start.17 = (bf16[8,2,32,512]{3,2,1,0:T(8,128)(2,1)S(1)}, bf16[8,2,32,512]{3,2,1,0:T(8,128)(2,1)}, u32[]{:S(2)}, u32[]{:S(2)}) collective-permute-start(bf16[8,2,32,512]{3,2,1,0:T(8,128)(2,1)S(1)} %get-tuple-element.44), channel_id=1, source_target_pairs={{0,12},{1,13},{2,14},{3,15},{4,8},{5,9},{6,10},{7,11},{8,4},{9,5},... | collective-permute-start | bytes 1572872 | tf_op jit(solution)/shard_map/ppermute | solution.py:53
  77.2 30.1 %collective-permute-start.24 = (bf16[2,8,2,32,512]{4,3,2,1,0:T(8,128)(2,1)S(1)}, bf16[2,8,2,32,512]{4,3,2,1,0:T(8,128)(2,1)}, u32[]{:S(2)}, u32[]{:S(2)}) collective-permute-start(bf16[2,8,2,32,512]{4,3,2,1,0:T(8,128)(2,1)S(1)} %pad_maximum_fusion.1.refs_7_), channel_id=1, source_target_pairs={{0,16},{1,17},{2,18},{3,19},{4,20},{5,21},{6,22},{7,23},{8,24},{9,... | collective-permute-start | bytes 3145736 | tf_op jit(solution)/shard_map/ppermute | solution.py:53
  78.0 26.3 %collective-permute-start.23 = (bf16[8,2,32,512]{3,2,1,0:T(8,128)(2,1)}, bf16[8,2,32,512]{3,2,1,0:T(8,128)(2,1)}, u32[]{:S(2)}, u32[]{:S(2)}) collective-permute-start(bf16[8,2,32,512]{3,2,1,0:T(8,128)(2,1)} %get-tuple-element.47), channel_id=1, source_target_pairs={{0,1},{1,0},{2,3},{3,2},{4,5},{5,4},{6,7},{7,6},{8,9},{9,8},{10,11... | collective-permute-start | bytes 1572872 | tf_op jit(solution)/shard_map/ppermute | solution.py:53
  81.5 23.0 %collective-permute-start.22 = (bf16[8,2,32,512]{3,2,1,0:T(8,128)(2,1)}, bf16[8,2,32,512]{3,2,1,0:T(8,128)(2,1)}, u32[]{:S(2)}, u32[]{:S(2)}) collective-permute-start(bf16[8,2,32,512]{3,2,1,0:T(8,128)(2,1)} %get-tuple-element.49), channel_id=1, source_target_pairs={{0,12},{1,13},{2,14},{3,15},{4,8},{5,9},{6,10},{7,11},{8,4},{9,5},... | collective-permute-start | bytes 1572872 | tf_op jit(solution)/shard_map/ppermute | solution.py:53
  83.6 6.4 %collective-permute-start.27 = (bf16[8,2,32,512]{3,2,1,0:T(8,128)(2,1)}, bf16[8,2,32,512]{3,2,1,0:T(8,128)(2,1)}, u32[]{:S(2)}, u32[]{:S(2)}) collective-permute-start(bf16[8,2,32,512]{3,2,1,0:T(8,128)(2,1)} %collective-permute-done.19.refs_9_), channel_id=1, source_target_pairs={{0,16},{1,17},{2,18},{3,19},{4,20},{5,21},{6,22},{7,23},{8,24},{9,... | collective-permute-start | bytes 1572872 | tf_op jit(solution)/shard_map/ppermute | solution.py:53
  104.9 13.6 %collective-permute-start.20 = (bf16[8,2,32,512]{3,2,1,0:T(8,128)(2,1)}, bf16[8,2,32,512]{3,2,1,0:T(8,128)(2,1)}, u32[]{:S(2)}, u32[]{:S(2)}) collective-permute-start(bf16[8,2,32,512]{3,2,1,0:T(8,128)(2,1)} %get-tuple-element.26), channel_id=1, source_target_pairs={{0,1},{1,0},{2,3},{3,2},{4,5},{5,4},{6,7},{7,6},{8,9},{9,8},{10,11... | collective-permute-start | bytes 1572872 | tf_op jit(solution)/shard_map/ppermute | solution.py:53
  105.1 14.0 %collective-permute-start.18 = (bf16[8,2,32,512]{3,2,1,0:T(8,128)(2,1)}, bf16[8,2,32,512]{3,2,1,0:T(8,128)(2,1)}, u32[]{:S(2)}, u32[]{:S(2)}) collective-permute-start(bf16[8,2,32,512]{3,2,1,0:T(8,128)(2,1)} %get-tuple-element.25), channel_id=1, source_target_pairs={{0,12},{1,13},{2,14},{3,15},{4,8},{5,9},{6,10},{7,11},{8,4},{9,5},... | collective-permute-start | bytes 1572872 | tf_op jit(solution)/shard_map/ppermute | solution.py:53
  107.3 12.2 %collective-permute-start.21 = (bf16[2,8,2,32,512]{4,3,2,1,0:T(8,128)(2,1)}, bf16[2,8,2,32,512]{4,3,2,1,0:T(8,128)(2,1)}, u32[]{:S(2)}, u32[]{:S(2)}) collective-permute-start(bf16[2,8,2,32,512]{4,3,2,1,0:T(8,128)(2,1)} %pad_maximum_fusion.refs_7_), channel_id=1, source_target_pairs={{0,16},{1,17},{2,18},{3,19},{4,20},{5,21},{6,22},{7,23},{8,24},{9,... | collective-permute-start | bytes 3145736 | tf_op jit(solution)/shard_map/ppermute | solution.py:53
  (15 other events, 100.3 us)

commit v2 on v1

v2 whole, which is shorter than its diff:
```python
import jax
import jax.numpy as jnp
import numpy as np
from jax import lax
from jax.experimental import pallas as pl
from jax.experimental.pallas import tpu as pltpu
from jax.sharding import PartitionSpec as P

RUN = 3
G = 512
ROWS = 32
PLANES = 2

CLASSES = (((1, 3, 4, 12), (3, 4, 12, 1)), ((4, 12, 1, 3), (12, 1, 3, 4)))
ZCLASSES = ((2, 6), (6, 2))

PAIRS = ((0, 1), (0, 2), (0, 3), (1, 2), (1, 3), (2, 3))


def term(a, b):
    return 8 * (a // 2) + 4 * (b // 2) + 2 * (a % 2) + b % 2


def block_masks():
    table = np.zeros((2, 2, 16), np.int32)
    for core in range(2):
        for half in range(2):
            for block in range(16):
                for step in range(4):
                    if block >> step & 1:
                        table[core, half, block] ^= CLASSES[core][half][step]
    return table


MASKS = block_masks()


def exchange(value, wa_mask, grid_mask):
    perm = []
    for wa in range(8):
        for grid in range(16):
            core = wa % 2
            perm.append((wa * 16 + grid, (wa ^ wa_mask(core)) * 16 + (grid ^ grid_mask(core))))
    return lax.ppermute(value, ("wa", "grid"), perm)


def swap_core(value):
    return exchange(value, lambda core: 1, lambda core: 0)


def swap_z(value, step):
    return exchange(value, lambda core: ZCLASSES[core][step], lambda core: 0)


def swap_grid(value, half, step):
    return exchange(value, lambda core: 0, lambda core: CLASSES[core][half][step])


def pick_kernel(ids, owner, jones, mine, other, semaphore):
    core = ids[0]
    copies = []
    for index in range(RUN):
        slot = owner[index] & 3
        for entry in range(4):
            for part, target in ((core, mine), (1 - core, other)):
                copies.append(
                    pltpu.make_async_copy(
                        jones.at[slot, entry, part], target.at[index, entry], semaphore.at[len(copies)]
                    )
                )
    for copy in copies:
        copy.start()
    for copy in copies:
        copy.wait()


def pick(ids, owner, jones):
    shape = jax.ShapeDtypeStruct((RUN, 4, ROWS, G), jnp.bfloat16)
    scalars = pl.BlockSpec(memory_space=pltpu.SMEM)
    return pl.pallas_call(
        pick_kernel,
        out_shape=(shape, shape),
        in_specs=[scalars, scalars, pl.BlockSpec(memory_space=pl.ANY)],
        out_specs=(pl.BlockSpec(memory_space=pltpu.VMEM), pl.BlockSpec(memory_space=pltpu.VMEM)),
        scratch_shapes=[pltpu.SemaphoreType.DMA((RUN * 8,))],
        compiler_params=pltpu.CompilerParams(vmem_limit_bytes=60 * 1024 * 1024),
        name="pick",
    )(ids, owner, jones)


def transform_kernel(index, *refs):
    ids, keep, ku = refs[:3]
    gathered = refs[3:5]
    own = (refs[5:7], refs[7:9])
    far = (refs[9:11], refs[11:13])
    out, fields, operator, products, left, staged, field_sem, operator_sem, out_sem = refs[-9:]
    core, grid = ids[0], ids[1]

    def placed(half, block, near):
        masks = (int(MASKS[0, half, block]), int(MASKS[1, half, block]))
        chosen = jnp.where(core == 0, masks[0], masks[1]) if near else jnp.where(core == 0, masks[1], masks[0])
        return pl.ds(pl.multiple_of((grid ^ chosen) * ROWS, ROWS), ROWS)

    for half in range(2):
        for block in range(16):
            for near, source, part in ((True, own, core), (False, far, 1 - core)):
                pltpu.make_async_copy(
                    source[block // 8][half].at[block % 8],
                    fields.at[part, pl.ds(2 * half, 2), placed(half, block, near)],
                    field_sem,
                ).start()
    for block in range(16):
        pltpu.make_async_copy(
            gathered[block // 8].at[block % 8], operator.at[:, :, placed(0, block, True)], operator_sem
        ).start()

    def multiply(columns):
        for start in range(0, G, 16):
            rows = slice(start, start + 16)
            re = [fields[0, entry, rows, columns].astype(jnp.float32) for entry in range(4)]
            im = [fields[1, entry, rows, columns].astype(jnp.float32) for entry in range(4)]
            for a in range(4):
                products[a, rows, columns] = (re[a] * re[a] + im[a] * im[a]).astype(jnp.bfloat16)
            for at, (a, b) in enumerate(PAIRS):
                products[4 + 2 * at, rows, columns] = (re[a] * re[b] + im[a] * im[b]).astype(jnp.bfloat16)
                products[5 + 2 * at, rows, columns] = (im[a] * re[b] - re[a] * im[b]).astype(jnp.bfloat16)

    def put(plane, entry, columns, value, turned):
        rows = slice(entry * 64, entry * 64 + 64)
        left[plane, rows, columns] = value.astype(jnp.bfloat16)
        left[plane, rows, slice(columns.start + G, columns.stop + G)] = turned.astype(jnp.bfloat16)

    def first_pass(columns):
        def apply(field):
            return jnp.dot(ku[...], products[field, :, columns], preferred_element_type=jnp.float32)

        for a in range(4):
            whole = apply(a)
            for plane in range(PLANES):
                at = plane * 128
                put(plane, term(a, a), columns, whole[at : at + 64], whole[at + 64 : at + 128])
        for pair, (a, b) in enumerate(PAIRS):
            real, imag = apply(4 + 2 * pair), apply(5 + 2 * pair)
            for plane in range(PLANES):
                at = plane * 128
                xa, ya = real[at : at + 64], real[at + 64 : at + 128]
                xb, yb = imag[at : at + 64], imag[at + 64 : at + 128]
                put(plane, term(a, b), columns, xa + yb, ya - xb)
                put(plane, term(b, a), columns, xa - yb, ya + xb)

    chunks = [slice(start, start + 256) for start in range(0, G, 256)]
    pltpu.make_async_copy(fields, fields, field_sem).wait()
    multiply(chunks[0])
    for step, chunk in enumerate(chunks):
        if step + 1 < len(chunks):
            multiply(chunks[step + 1])
        first_pass(chunk)
    for entry in range(16):

        @pl.when(keep[entry] == 0)
        def _(entry=entry):
            left[:, entry * 64 : entry * 64 + 64] = jnp.zeros((PLANES, 64, 2 * G), jnp.bfloat16)

    pltpu.make_async_copy(operator, operator, operator_sem).wait()
    contract = (((1,), (1,)), ((), ()))
    for plane in range(PLANES):
        for group in range(4):
            rows = slice(group * 256, group * 256 + 256)
            total = lax.dot_general(
                left[plane, rows, 0:G], operator[plane, 0], contract, preferred_element_type=jnp.float32
            ) + lax.dot_general(
                left[plane, rows, G : 2 * G], operator[plane, 1], contract, preferred_element_type=jnp.float32
            )
            staged[plane, group * 4 : group * 4 + 4] = total.astype(jnp.bfloat16).reshape(4, ROWS, 2, G)
            for entry in range(group * 4, group * 4 + 4):
                pltpu.make_async_copy(
                    staged.at[plane, entry], out.at[:, plane, index, entry], out_sem
                ).start()
    pltpu.make_async_copy(staged, staged, out_sem).wait()


def transform(index, ids, keep, ku, operators, own, far, previous):
    anywhere = pl.BlockSpec(memory_space=pl.ANY)
    scalars = pl.BlockSpec(memory_space=pltpu.SMEM)
    operands = [ids, keep, ku, *operators, *own, *far]
    specs = [scalars, scalars, pl.BlockSpec(memory_space=pltpu.VMEM)] + [anywhere] * 10
    aliases = {}
    if previous is not None:
        aliases = {len(operands): 0}
        operands.append(previous)
        specs.append(anywhere)

    def kernel(*refs):
        transform_kernel(index, *refs)

    return pl.pallas_call(
        kernel,
        out_shape=jax.ShapeDtypeStruct((ROWS, PLANES, RUN, 16, 2, G), jnp.bfloat16),
        in_specs=specs,
        out_specs=anywhere,
        input_output_aliases=aliases,
        scratch_shapes=[
            pltpu.VMEM((2, 4, G, G), jnp.bfloat16),
            pltpu.VMEM((PLANES, 2, G, G), jnp.bfloat16),
            pltpu.VMEM((16, G, G), jnp.bfloat16),
            pltpu.VMEM((PLANES, 16 * 64, 2 * G), jnp.bfloat16),
            pltpu.VMEM((PLANES, 16, ROWS, 2, G), jnp.bfloat16),
            pltpu.SemaphoreType.DMA,
            pltpu.SemaphoreType.DMA,
            pltpu.SemaphoreType.DMA,
        ],
        compiler_params=pltpu.CompilerParams(vmem_limit_bytes=26 * 1024 * 1024),
        cost_estimate=pl.CostEstimate(flops=1_000_000, bytes_accessed=1_000_000, transcendentals=0),
        name="transform",
    )(*operands)


def after(value, *others):
    return lax.optimization_barrier((value, *others))[0]


def choose(flags, yes, no):
    return jnp.where(flags[:, None, None, None], yes, no)


def body(jones, owner, mask, w_operator):
    wa = lax.axis_index("wa")
    grid = lax.axis_index("grid")
    core = wa & 1
    ids = jnp.stack([core, grid]).astype(jnp.int32)
    mine, other = pick(ids, owner, jones)

    blocks = w_operator[None]
    blocks = jnp.concatenate([blocks, swap_grid(blocks, 0, 0)], 0)

    holder = owner[:RUN] >> 2
    rows = choose((holder & 1) == core, mine, swap_core(other))
    first = ZCLASSES[0][0] + core * (ZCLASSES[1][0] - ZCLASSES[0][0])
    apart = (holder ^ wa) & 6
    rows = after(rows, blocks)
    blocks = jnp.concatenate([blocks, swap_grid(blocks, 0, 1)], 0)
    rows = choose(apart == 0, rows, swap_z(rows, 0))
    rows = after(rows, blocks)
    blocks = jnp.concatenate([blocks, swap_grid(blocks, 0, 2)], 0)
    rows = choose((apart == 0) | (apart == first), rows, swap_z(rows, 1))
    rows = after(rows, blocks)
    operators = (blocks, swap_grid(blocks, 0, 3))

    streams = []
    for half in range(2):
        stream = rows[None, :, 2 * half : 2 * half + 2]
        for step in range(2):
            stream = jnp.concatenate([stream, swap_grid(stream, half, step)], 0)
        stream = after(stream, *operators)
        streams.append((stream, swap_grid(stream, half, 2)))

    kr, ki = w_operator[:, 0], w_operator[:, 1]
    plain = jnp.stack([kr, ki], 2).reshape(PLANES, 2 * ROWS, G)
    turned = jnp.stack([-ki, kr], 2).reshape(PLANES, 2 * ROWS, G)
    ku = jnp.concatenate([plain, turned], 1).reshape(PLANES * 4 * ROWS, G)
    keep = mask.reshape(RUN, 16)

    own = []
    for index in range(RUN):
        low = [jnp.concatenate([near[:, index], far[:, index]], 0) for near, far in streams]
        send = low
        if index == 2:
            send = [after(send[half], own[0][2 + half]) for half in range(2)]
        own.append((*low, *[swap_grid(send[half], half, 3) for half in range(2)]))
    result = None
    for index in range(RUN):
        sent = own[index]
        if result is not None:
            sent = [*sent[:2], *[after(one, result) for one in sent[2:]]]
        far = [swap_core(one) for one in sent]
        result = transform(index, ids, keep[index], ku, operators, own[index], far, result)
    return result


def solution(mesh):
    return jax.shard_map(
        body,
        mesh=mesh,
        in_specs=(P("wa", None, None, "grid", None), P(), P(), P("wa", None, "grid", None)),
        out_specs=P("grid", "wa", None, None, None, None),
        check_vma=False,
    )
```

time: 134 us -> 130 us (0.970)
  Pallas kernels: 36.8 us -> 31.5 us
  starting transfers between devices: 43.5 us -> 45.2 us
    pallas_call x3, Pallas kernels: 34 us -> 28.7 us  [transform(): pl.pallas_call(kernel, out_shape=jax.ShapeDtypeStruct((ROWS, PLANES, RUN,...]
    concatenate x10 -> x7, other arithmetic: 0.42 us -> 3.13 us  [the longest x1 1.01 us: body(): blocks = jnp.concatenate([blocks, swap_grid(blocks, 0, 2)], 0)]
    ppermute x32 -> x31, starting transfers between devices: 43.5 us -> 45.2 us  [exchange(): return lax.ppermute(value, ('wa', 'grid'), perm)]
    concatenate x4 -> x6, other arithmetic: 5.53 us -> 3.97 us  [body(): jnp.concatenate([near[:, index], far[:, index]], 0)]
    another operation x5 -> x0, other arithmetic: 1.39 us -> none  [body(): jnp.stack([jnp.concatenate([near[:, index], far[:, index]], 0) for near,...]
    unnamed x14 -> x22, local copies, waits for them, and re-layouts: 3.44 us -> 4.47 us
    ppermute x32 -> x31, waiting for transfers between devices: 33.6 us -> 34.2 us  [exchange(): return lax.ppermute(value, ('wa', 'grid'), perm)]
  transfers between devices with their start and end apart: 32 -> 31, of which waited for: 13 -> 9; matrix products, arithmetic and copies ran while one was open for 9% -> 10% of each run, Pallas kernels for 17% -> 15%
where the time goes in v2:
time: 130 us
  starting transfers between devices  45.2 us (35%)
  waiting for transfers between devices  34.2 us (26%)
  Pallas kernels  31.5 us (24%)
  other arithmetic  10.1 us (8%)
  local copies, waits for them, and re-layouts  8.25 us (6%)
    ppermute x31, starting transfers between devices, exchange(): return lax.ppermute(value, ('wa', 'grid'), perm)  45.2 us
    ppermute x31, waiting for transfers between devices, exchange(): return lax.ppermute(value, ('wa', 'grid'), perm)  34.2 us
    pallas_call x3, Pallas kernels, transform(): pl.pallas_call(kernel, out_shape=jax.ShapeDtypeStruct((ROWS, PLANES, RUN,...  28.7 us
    unnamed x22, local copies, waits for them, and re-layouts  4.47 us
    concatenate x6, other arithmetic, body(): jnp.concatenate([near[:, index], far[:, index]], 0)  3.97 us
    pallas_call x1, Pallas kernels, pick(): pl.pallas_call(pick_kernel, out_shape=(shape, shape), in_specs=[scalars,...  2.84 us
  transfers between devices with their start and end apart: 31, of which 9 were waited for; matrix products, arithmetic and copies ran while one was open for 10% of the time, Pallas kernels for 15%

profile of v2, /device:TPU:1, one launch (start us, length us, event | category | flops | bytes accessed | tf_op | source)
XLA Modules:
  0.0 129.7 jit_solution(4038903644647897917)
XLA Ops:
  0.7 2.8 %pick.1 = (bf16[3,4,32,512]{3,2,1,0:T(8,128)(2,1)}, bf16[3,4,32,512]{3,2,1,0:T(8,128)(2,1)}) custom-call(s32[2]{0:T(128)} %pad_add_fusion.ids.refs_0_, s32[32]{0:T(128)} %owner.1, bf16[4,4,2,32,512]{4,3,2,1,0:T(8,128)(2,1)} %jones.1), custom_call_target="tpu_custom_call" | custom-call | tf_op jit(solution)/shard_map/pick/pallas_call | solution.py:80
  7.1 2.3 %collective-permute-done = bf16[1,2,2,32,512]{4,3,2,1,0:T(8,128)(2,1)S(1)} collective-permute-done((bf16[1,2,2,32,512]{4,3,2,1,0:T(8,128)(2,1)}, bf16[1,2,2,32,512]{4,3,2,1,0:T(8,128)(2,1)S(1)}, u32[]{:S(2)}, u32[]{:S(2)}) %collective-permute-start) | collective-permute-done | bytes 131104 | tf_op jit(solution)/shard_map/ppermute | solution.py:44
  10.3 2.9 %collective-permute-start.1 = (bf16[2,2,2,32,512]{4,3,2,1,0:T(8,128)(2,1)S(1)}, bf16[2,2,2,32,512]{4,3,2,1,0:T(8,128)(2,1)S(1)}, u32[]{:S(2)}, u32[]{:S(2)}) collective-permute-start(bf16[2,2,2,32,512]{4,3,2,1,0:T(8,128)(2,1)S(1)} %pad_maximum_fusion.13), channel_id=1, source_target_pairs={{0,3},{1,2},{2,1},{3,0},{4,7},{5,6},{6,5},{7,4},{8,11},{9,10},{10,... | collective-permute-start | bytes 786440 | tf_op jit(solution)/shard_map/ppermute | solution.py:44
  14.3 3.8 %collective-permute-start.5 = (bf16[3,4,32,512]{3,2,1,0:T(8,128)(2,1)S(1)}, bf16[3,4,32,512]{3,2,1,0:T(8,128)(2,1)S(1)}, u32[]{:S(2)}, u32[]{:S(2)}) collective-permute-start(bf16[3,4,32,512]{3,2,1,0:T(8,128)(2,1)S(1)} %broadcast_select_fusion), channel_id=1, source_target_pairs={{0,32},{1,33},{2,34},{3,35},{4,36},{5,37},{6,38},{7,39},{8,40},{9,... | collective-permute-start | bytes 1179656 | tf_op jit(solution)/shard_map/ppermute | solution.py:44
  20.4 2.9 %collective-permute-done.5 = bf16[3,4,32,512]{3,2,1,0:T(8,128)(2,1)S(1)} collective-permute-done((bf16[3,4,32,512]{3,2,1,0:T(8,128)(2,1)S(1)}, bf16[3,4,32,512]{3,2,1,0:T(8,128)(2,1)S(1)}, u32[]{:S(2)}, u32[]{:S(2)}) %collective-permute-start.5) | collective-permute-done | bytes 393248 | tf_op jit(solution)/shard_map/ppermute | solution.py:44
  23.5 4.0 %collective-permute-done.2 = bf16[4,2,2,32,512]{4,3,2,1,0:T(8,128)(2,1)S(1)} collective-permute-done((bf16[4,2,2,32,512]{4,3,2,1,0:T(8,128)(2,1)S(1)}, bf16[4,2,2,32,512]{4,3,2,1,0:T(8,128)(2,1)S(1)}, u32[]{:S(2)}, u32[]{:S(2)}) %collective-permute-start.2) | collective-permute-done | bytes 524320 | tf_op jit(solution)/shard_map/ppermute | solution.py:44
  28.5 2.6 %collective-permute-start.3 = (bf16[8,2,2,32,512]{4,3,2,1,0:T(8,128)(2,1)S(1)}, bf16[8,2,2,32,512]{4,3,2,1,0:T(8,128)(2,1)S(1)}, u32[]{:S(2)}, u32[]{:S(2)}) collective-permute-start(bf16[8,2,2,32,512]{4,3,2,1,0:T(8,128)(2,1)S(1)} %pad_maximum_fusion.refs_3_), channel_id=1, source_target_pairs={{0,12},{1,13},{2,14},{3,15},{4,8},{5,9},{6,10},{7,11},{8,4},{9,5},... | collective-permute-start | bytes 3145736 | tf_op jit(solution)/shard_map/ppermute | solution.py:44
  31.2 1.9 %collective-permute-start.10 = (bf16[1,3,2,32,512]{4,3,2,0,1:T(8,128)(2,1)S(1)}, bf16[1,3,2,32,512]{4,3,2,0,1:T(8,128)(2,1)S(1)}, u32[]{:S(2)}, u32[]{:S(2)}) collective-permute-start(bf16[1,3,2,32,512]{4,3,2,0,1:T(8,128)(2,1)S(1)} %get-tuple-element.42), channel_id=1, source_target_pairs={{0,3},{1,2},{2,1},{3,0},{4,7},{5,6},{6,5},{7,4},{8,11},{9,10},{10,... | collective-permute-start | bytes 589832 | tf_op jit(solution)/shard_map/ppermute | solution.py:44
  33.1 6.3 %collective-permute-done.10 = bf16[1,3,2,32,512]{4,3,2,0,1:T(8,128)(2,1)S(1)} collective-permute-done((bf16[1,3,2,32,512]{4,3,2,0,1:T(8,128)(2,1)S(1)}, bf16[1,3,2,32,512]{4,3,2,0,1:T(8,128)(2,1)S(1)}, u32[]{:S(2)}, u32[]{:S(2)}) %collective-permute-start.10) | collective-permute-done | bytes 196640 | tf_op jit(solution)/shard_map/ppermute | solution.py:44
  41.1 5.2 %collective-permute-done.11 = bf16[2,3,2,32,512]{4,3,2,0,1:T(8,128)(2,1)S(1)} collective-permute-done((bf16[2,3,2,32,512]{4,3,2,0,1:T(8,128)(2,1)S(1)}, bf16[2,3,2,32,512]{4,3,2,0,1:T(8,128)(2,1)S(1)}, u32[]{:S(2)}, u32[]{:S(2)}) %collective-permute-start.11) | collective-permute-done | bytes 393248 | tf_op jit(solution)/shard_map/ppermute | solution.py:44
  46.5 1.8 %collective-permute-start.12 = (bf16[4,3,2,32,512]{4,3,2,0,1:T(8,128)(2,1)S(1)}, bf16[4,3,2,32,512]{4,3,2,0,1:T(8,128)(2,1)S(1)}, u32[]{:S(2)}, u32[]{:S(2)}) collective-permute-start(bf16[4,3,2,32,512]{4,3,2,0,1:T(8,128)(2,1)S(1)} %pad_maximum_fusion.2), channel_id=1, source_target_pairs={{0,12},{1,13},{2,14},{3,15},{4,8},{5,9},{6,10},{7,11},{8,4},{9,5},... | collective-permute-start | bytes 2359304 | tf_op jit(solution)/shard_map/ppermute | solution.py:44
  48.3 3.8 %collective-permute-done.8 = bf16[2,3,2,32,512]{4,3,2,1,0:T(8,128)(2,1)S(1)} collective-permute-done((bf16[2,3,2,32,512]{4,3,2,1,0:T(8,128)(2,1)S(1)}, bf16[2,3,2,32,512]{4,3,2,1,0:T(8,128)(2,1)S(1)}, u32[]{:S(2)}, u32[]{:S(2)}) %collective-permute-start.8) | collective-permute-done | bytes 393248 | tf_op jit(solution)/shard_map/ppermute | solution.py:44
  53.9 7.3 %collective-permute-done.12 = bf16[4,3,2,32,512]{4,3,2,0,1:T(8,128)(2,1)S(1)} collective-permute-done((bf16[4,3,2,32,512]{4,3,2,0,1:T(8,128)(2,1)S(1)}, bf16[4,3,2,32,512]{4,3,2,0,1:T(8,128)(2,1)S(1)}, u32[]{:S(2)}, u32[]{:S(2)}) %collective-permute-start.12) | collective-permute-done | bytes 786464 | tf_op jit(solution)/shard_map/ppermute | solution.py:44
  62.2 4.0 %collective-permute-start.24 = (bf16[8,2,32,512]{3,2,1,0:T(8,128)(2,1)S(1)}, bf16[8,2,32,512]{3,2,1,0:T(8,128)(2,1)S(1)}, u32[]{:S(2)}, u32[]{:S(2)}) collective-permute-start(bf16[8,2,32,512]{3,2,1,0:T(8,128)(2,1)S(1)} %pad_maximum_fusion.7.refs_6_), channel_id=1, source_target_pairs={{0,16},{1,17},{2,18},{3,19},{4,20},{5,21},{6,22},{7,23},{8,24},{9,... | collective-permute-start | bytes 1572872 | tf_op jit(solution)/shard_map/ppermute | solution.py:44
  67.1 3.0 %collective-permute-start.13 = (bf16[8,2,32,512]{3,2,1,0:T(8,128)(2,1)S(1)}, bf16[8,2,32,512]{3,2,1,0:T(8,128)(2,1)}, u32[]{:S(2)}, u32[]{:S(2)}) collective-permute-start(bf16[8,2,32,512]{3,2,1,0:T(8,128)(2,1)S(1)} %pad_maximum_fusion.6.refs_5_), channel_id=1, source_target_pairs={{0,12},{1,13},{2,14},{3,15},{4,8},{5,9},{6,10},{7,11},{8,4},{9,5},... | collective-permute-start | bytes 1572872 | tf_op jit(solution)/shard_map/ppermute | solution.py:44
  70.1 7.1 %collective-permute-start.23 = (bf16[8,2,32,512]{3,2,1,0:T(8,128)(2,1)S(1)}, bf16[8,2,32,512]{3,2,1,0:T(8,128)(2,1)S(1)}, u32[]{:S(2)}, u32[]{:S(2)}) collective-permute-start(bf16[8,2,32,512]{3,2,1,0:T(8,128)(2,1)S(1)} %pad_maximum_fusion.6.refs_5_), channel_id=1, source_target_pairs={{0,16},{1,17},{2,18},{3,19},{4,20},{5,21},{6,22},{7,23},{8,24},{9,... | collective-permute-start | bytes 1572872 | tf_op jit(solution)/shard_map/ppermute | solution.py:44
  77.6 1.7 %collective-permute-start.20 = (bf16[8,2,32,512]{3,2,1,0:T(8,128)(2,1)S(1)}, bf16[8,2,32,512]{3,2,1,0:T(8,128)(2,1)}, u32[]{:S(2)}, u32[]{:S(2)}) collective-permute-start(bf16[8,2,32,512]{3,2,1,0:T(8,128)(2,1)S(1)} %pad_maximum_fusion.9.refs_6_), channel_id=1, source_target_pairs={{0,1},{1,0},{2,3},{3,2},{4,5},{5,4},{6,7},{7,6},{8,9},{9,8},{10,11... | collective-permute-start | bytes 1572872 | tf_op jit(solution)/shard_map/ppermute | solution.py:44
  79.5 4.9 %collective-permute-start.26 = (bf16[8,2,32,512]{3,2,1,0:T(8,128)(2,1)}, bf16[8,2,32,512]{3,2,1,0:T(8,128)(2,1)}, u32[]{:S(2)}, u32[]{:S(2)}) collective-permute-start(bf16[8,2,32,512]{3,2,1,0:T(8,128)(2,1)} %collective-permute-done.15.refs_8_), channel_id=1, source_target_pairs={{0,16},{1,17},{2,18},{3,19},{4,20},{5,21},{6,22},{7,23},{8,24},{9,... | collective-permute-start | bytes 1572872 | tf_op jit(solution)/shard_map/ppermute | solution.py:44
  85.3 1.9 %pad_maximum_fusion.5.refs_6_ = bf16[8,2,32,512]{3,2,1,0:T(8,128)(2,1)} fusion(bf16[4,2,32,512]{3,2,1,0:T(8,128)(2,1)} %get-tuple-element.36, bf16[4,2,32,512]{3,2,1,0:T(8,128)(2,1)} %get-tuple-element.33), kind=kLoop, calls=%fused_computation.5 | loop fusion | flops 262144 | bytes 1048576 | tf_op jit(solution)/shard_map/concatenate | solution.py:265
  87.2 1.9 %pad_maximum_fusion.4.refs_5_ = bf16[8,2,32,512]{3,2,1,0:T(8,128)(2,1)} fusion(bf16[4,2,32,512]{3,2,1,0:T(8,128)(2,1)} %get-tuple-element.39, bf16[4,2,32,512]{3,2,1,0:T(8,128)(2,1)} %get-tuple-element.41), kind=kLoop, calls=%fused_computation.4 | loop fusion | flops 262144 | bytes 1048576 | tf_op jit(solution)/shard_map/concatenate | solution.py:265
  93.5 9.9 %transform.3.refs_13_ = bf16[32,2,3,16,2,512]{5,4,3,2,1,0:T(2,128)(2,1)} custom-call(s32[2]{0:T(128)S(1)} %copy-done.8, s32[16]{0:T(128)S(1)} %squeeze.60.refs_1_, bf16[256,512]{1,0:T(8,128)(2,1)S(1)} %bitcast.42, bf16[8,2,2,32,512]{4,3,2,1,0:T(8,128)(2,1)S(1)} %pad_maximum_fusion.refs_3_, bf16[8,2,2,32,512]{4,3,2,1,0:T(8,128)(2,1)S(1)} %collective-permute-done.3.refs_4_, ...), custom_call_target="tpu_custom_call" | custom-call | flops 1000000 | bytes 1000000 | tf_op jit(solution)/shard_map/transform/pallas_call | solution.py:196
  104.0 1.6 %collective-permute-start.16 = (bf16[8,2,32,512]{3,2,1,0:T(8,128)(2,1)}, bf16[8,2,32,512]{3,2,1,0:T(8,128)(2,1)}, u32[]{:S(2)}, u32[]{:S(2)}) collective-permute-start(bf16[8,2,32,512]{3,2,1,0:T(8,128)(2,1)} %pad_maximum_fusion.5.refs_6_), channel_id=1, source_target_pairs={{0,1},{1,0},{2,3},{3,2},{4,5},{5,4},{6,7},{7,6},{8,9},{9,8},{10,11... | collective-permute-start | bytes 1572872 | tf_op jit(solution)/shard_map/ppermute | solution.py:44
  107.8 9.6 %transform.4.refs_13_ = bf16[32,2,3,16,2,512]{5,4,3,2,1,0:T(2,128)(2,1)} custom-call(s32[2]{0:T(128)S(1)} %copy-done.8, s32[16]{0:T(128)S(1)} %squeeze.55.refs_1_, bf16[256,512]{1,0:T(8,128)(2,1)S(1)} %bitcast.43, bf16[8,2,2,32,512]{4,3,2,1,0:T(8,128)(2,1)S(1)} %pad_maximum_fusion.refs_3_, ...), custom_call_target="tpu_custom_call", output_to_operand_aliasing={{}: (13, {})} | custom-call | flops 1000000 | bytes 1000000 | tf_op jit(solution)/shard_map/transform/pallas_call | solution.py:196
  120.3 9.2 %transform.5 = bf16[32,2,3,16,2,512]{5,4,3,2,1,0:T(2,128)(2,1)} custom-call(s32[2]{0:T(128)S(1)} %copy-done.8, s32[16]{0:T(128)S(1)} %squeeze.46.refs_1_, bf16[256,512]{1,0:T(8,128)(2,1)S(1)} %bitcast.44, bf16[8,2,2,32,512]{4,3,2,1,0:T(8,128)(2,1)S(1)} %pad_maximum_fusion.refs_3_, ...), custom_call_target="tpu_custom_call", output_to_operand_aliasing={{}: (13, {})} | custom-call | flops 1000000 | bytes 1000000 | tf_op jit(solution)/shard_map/transform/pallas_call | solution.py:196
  (100 shorter events, 26.8 us)
Async XLA Ops:
  3.5 9.7 %collective-permute-start.4 = (bf16[3,4,32,512]{3,2,1,0:T(8,128)(2,1)}, bf16[3,4,32,512]{3,2,1,0:T(8,128)(2,1)S(1)}, u32[]{:S(2)}, u32[]{:S(2)}) collective-permute-start(bf16[3,4,32,512]{3,2,1,0:T(8,128)(2,1)} %get-tuple-element.19), channel_id=1, source_target_pairs={{0,16},{1,17},{2,18},{3,19},{4,20},{5,21},{6,22},{7,23},{8,24},{9,... | collective-permute-start | bytes 1179656 | tf_op jit(solution)/shard_map/ppermute | solution.py:44
  10.3 7.8 %collective-permute-start.1 = (bf16[2,2,2,32,512]{4,3,2,1,0:T(8,128)(2,1)S(1)}, bf16[2,2,2,32,512]{4,3,2,1,0:T(8,128)(2,1)S(1)}, u32[]{:S(2)}, u32[]{:S(2)}) collective-permute-start(bf16[2,2,2,32,512]{4,3,2,1,0:T(8,128)(2,1)S(1)} %pad_maximum_fusion.13), channel_id=1, source_target_pairs={{0,3},{1,2},{2,1},{3,0},{4,7},{5,6},{6,5},{7,4},{8,11},{9,10},{10,... | collective-permute-start | bytes 786440 | tf_op jit(solution)/shard_map/ppermute | solution.py:44
  14.3 9.0 %collective-permute-start.5 = (bf16[3,4,32,512]{3,2,1,0:T(8,128)(2,1)S(1)}, bf16[3,4,32,512]{3,2,1,0:T(8,128)(2,1)S(1)}, u32[]{:S(2)}, u32[]{:S(2)}) collective-permute-start(bf16[3,4,32,512]{3,2,1,0:T(8,128)(2,1)S(1)} %broadcast_select_fusion), channel_id=1, source_target_pairs={{0,32},{1,33},{2,34},{3,35},{4,36},{5,37},{6,38},{7,39},{8,40},{9,... | collective-permute-start | bytes 1179656 | tf_op jit(solution)/shard_map/ppermute | solution.py:44
  19.1 8.4 %collective-permute-start.2 = (bf16[4,2,2,32,512]{4,3,2,1,0:T(8,128)(2,1)S(1)}, bf16[4,2,2,32,512]{4,3,2,1,0:T(8,128)(2,1)S(1)}, u32[]{:S(2)}, u32[]{:S(2)}) collective-permute-start(bf16[4,2,2,32,512]{4,3,2,1,0:T(8,128)(2,1)S(1)} %pad_maximum_fusion.3), channel_id=1, source_target_pairs={{0,4},{1,5},{2,6},{3,7},{4,0},{5,1},{6,2},{7,3},{8,12},{9,13},{10,... | collective-permute-start | bytes 1572872 | tf_op jit(solution)/shard_map/ppermute | solution.py:44
  23.4 7.7 %collective-permute-start.6 = (bf16[3,4,32,512]{3,2,1,0:T(8,128)(2,1)S(1)}, bf16[3,4,32,512]{3,2,1,0:T(8,128)(2,1)S(1)}, u32[]{:S(2)}, u32[]{:S(2)}) collective-permute-start(bf16[3,4,32,512]{3,2,1,0:T(8,128)(2,1)S(1)} %broadcast_select_fusion.1), channel_id=1, source_target_pairs={{0,96},{1,97},{2,98},{3,99},{4,100},{5,101},{6,102},{7,103},{8,104... | collective-permute-start | bytes 1179656 | tf_op jit(solution)/shard_map/ppermute | solution.py:44
  28.5 18.0 %collective-permute-start.3 = (bf16[8,2,2,32,512]{4,3,2,1,0:T(8,128)(2,1)S(1)}, bf16[8,2,2,32,512]{4,3,2,1,0:T(8,128)(2,1)S(1)}, u32[]{:S(2)}, u32[]{:S(2)}) collective-permute-start(bf16[8,2,2,32,512]{4,3,2,1,0:T(8,128)(2,1)S(1)} %pad_maximum_fusion.refs_3_), channel_id=1, source_target_pairs={{0,12},{1,13},{2,14},{3,15},{4,8},{5,9},{6,10},{7,11},{8,4},{9,5},... | collective-permute-start | bytes 3145736 | tf_op jit(solution)/shard_map/ppermute | solution.py:44
  31.2 8.2 %collective-permute-start.10 = (bf16[1,3,2,32,512]{4,3,2,0,1:T(8,128)(2,1)S(1)}, bf16[1,3,2,32,512]{4,3,2,0,1:T(8,128)(2,1)S(1)}, u32[]{:S(2)}, u32[]{:S(2)}) collective-permute-start(bf16[1,3,2,32,512]{4,3,2,0,1:T(8,128)(2,1)S(1)} %get-tuple-element.42), channel_id=1, source_target_pairs={{0,3},{1,2},{2,1},{3,0},{4,7},{5,6},{6,5},{7,4},{8,11},{9,10},{10,... | collective-permute-start | bytes 589832 | tf_op jit(solution)/shard_map/ppermute | solution.py:44
  33.1 7.0 %collective-permute-start.7 = (bf16[1,3,2,32,512]{4,3,2,1,0:T(8,128)(2,1)S(1)}, bf16[1,3,2,32,512]{4,3,2,1,0:T(8,128)(2,1)S(1)}, u32[]{:S(2)}, u32[]{:S(2)}) collective-permute-start(bf16[1,3,2,32,512]{4,3,2,1,0:T(8,128)(2,1)S(1)} %get-tuple-element.43), channel_id=1, source_target_pairs={{0,1},{1,0},{2,3},{3,2},{4,5},{5,4},{6,7},{7,6},{8,9},{9,8},{10,11... | collective-permute-start | bytes 589832 | tf_op jit(solution)/shard_map/ppermute | solution.py:44
  40.1 12.0 %collective-permute-start.8 = (bf16[2,3,2,32,512]{4,3,2,1,0:T(8,128)(2,1)S(1)}, bf16[2,3,2,32,512]{4,3,2,1,0:T(8,128)(2,1)S(1)}, u32[]{:S(2)}, u32[]{:S(2)}) collective-permute-start(bf16[2,3,2,32,512]{4,3,2,1,0:T(8,128)(2,1)S(1)} %pad_maximum_fusion.10), channel_id=1, source_target_pairs={{0,3},{1,2},{2,1},{3,0},{4,7},{5,6},{6,5},{7,4},{8,11},{9,10},{10,... | collective-permute-start | bytes 1179656 | tf_op jit(solution)/shard_map/ppermute | solution.py:44
  46.5 14.7 %collective-permute-start.12 = (bf16[4,3,2,32,512]{4,3,2,0,1:T(8,128)(2,1)S(1)}, bf16[4,3,2,32,512]{4,3,2,0,1:T(8,128)(2,1)S(1)}, u32[]{:S(2)}, u32[]{:S(2)}) collective-permute-start(bf16[4,3,2,32,512]{4,3,2,0,1:T(8,128)(2,1)S(1)} %pad_maximum_fusion.2), channel_id=1, source_target_pairs={{0,12},{1,13},{2,14},{3,15},{4,8},{5,9},{6,10},{7,11},{8,4},{9,5},... | collective-permute-start | bytes 2359304 | tf_op jit(solution)/shard_map/ppermute | solution.py:44
  52.3 14.0 %collective-permute-start.9 = (bf16[4,3,2,32,512]{4,3,2,0,1:T(8,128)(2,1)S(1)}, bf16[4,3,2,32,512]{4,3,2,0,1:T(8,128)(2,1)S(1)}, u32[]{:S(2)}, u32[]{:S(2)}) collective-permute-start(bf16[4,3,2,32,512]{4,3,2,0,1:T(8,128)(2,1)S(1)} %copy.15), channel_id=1, source_target_pairs={{0,4},{1,5},{2,6},{3,7},{4,0},{5,1},{6,2},{7,3},{8,12},{9,13},{10,... | collective-permute-start | bytes 2359304 | tf_op jit(solution)/shard_map/ppermute | solution.py:44
  62.1 17.3 %collective-permute-start.15 = (bf16[8,2,32,512]{3,2,1,0:T(8,128)(2,1)S(1)}, bf16[8,2,32,512]{3,2,1,0:T(8,128)(2,1)}, u32[]{:S(2)}, u32[]{:S(2)}) collective-permute-start(bf16[8,2,32,512]{3,2,1,0:T(8,128)(2,1)S(1)} %pad_maximum_fusion.7.refs_6_), channel_id=1, source_target_pairs={{0,1},{1,0},{2,3},{3,2},{4,5},{5,4},{6,7},{7,6},{8,9},{9,8},{10,11... | collective-permute-start | bytes 1572872 | tf_op jit(solution)/shard_map/ppermute | solution.py:44
  62.2 17.2 %collective-permute-start.24 = (bf16[8,2,32,512]{3,2,1,0:T(8,128)(2,1)S(1)}, bf16[8,2,32,512]{3,2,1,0:T(8,128)(2,1)S(1)}, u32[]{:S(2)}, u32[]{:S(2)}) collective-permute-start(bf16[8,2,32,512]{3,2,1,0:T(8,128)(2,1)S(1)} %pad_maximum_fusion.7.refs_6_), channel_id=1, source_target_pairs={{0,16},{1,17},{2,18},{3,19},{4,20},{5,21},{6,22},{7,23},{8,24},{9,... | collective-permute-start | bytes 1572872 | tf_op jit(solution)/shard_map/ppermute | solution.py:44
  67.1 12.4 %collective-permute-start.13 = (bf16[8,2,32,512]{3,2,1,0:T(8,128)(2,1)S(1)}, bf16[8,2,32,512]{3,2,1,0:T(8,128)(2,1)}, u32[]{:S(2)}, u32[]{:S(2)}) collective-permute-start(bf16[8,2,32,512]{3,2,1,0:T(8,128)(2,1)S(1)} %pad_maximum_fusion.6.refs_5_), channel_id=1, source_target_pairs={{0,12},{1,13},{2,14},{3,15},{4,8},{5,9},{6,10},{7,11},{8,4},{9,5},... | collective-permute-start | bytes 1572872 | tf_op jit(solution)/shard_map/ppermute | solution.py:44
  70.1 14.3 %collective-permute-start.23 = (bf16[8,2,32,512]{3,2,1,0:T(8,128)(2,1)S(1)}, bf16[8,2,32,512]{3,2,1,0:T(8,128)(2,1)S(1)}, u32[]{:S(2)}, u32[]{:S(2)}) collective-permute-start(bf16[8,2,32,512]{3,2,1,0:T(8,128)(2,1)S(1)} %pad_maximum_fusion.6.refs_5_), channel_id=1, source_target_pairs={{0,16},{1,17},{2,18},{3,19},{4,20},{5,21},{6,22},{7,23},{8,24},{9,... | collective-permute-start | bytes 1572872 | tf_op jit(solution)/shard_map/ppermute | solution.py:44
  77.6 25.8 %collective-permute-start.20 = (bf16[8,2,32,512]{3,2,1,0:T(8,128)(2,1)S(1)}, bf16[8,2,32,512]{3,2,1,0:T(8,128)(2,1)}, u32[]{:S(2)}, u32[]{:S(2)}) collective-permute-start(bf16[8,2,32,512]{3,2,1,0:T(8,128)(2,1)S(1)} %pad_maximum_fusion.9.refs_6_), channel_id=1, source_target_pairs={{0,1},{1,0},{2,3},{3,2},{4,5},{5,4},{6,7},{7,6},{8,9},{9,8},{10,11... | collective-permute-start | bytes 1572872 | tf_op jit(solution)/shard_map/ppermute | solution.py:44
  79.3 26.3 %collective-permute-start.22 = (bf16[8,2,32,512]{3,2,1,0:T(8,128)(2,1)S(1)}, bf16[8,2,32,512]{3,2,1,0:T(8,128)(2,1)}, u32[]{:S(2)}, u32[]{:S(2)}) collective-permute-start(bf16[8,2,32,512]{3,2,1,0:T(8,128)(2,1)S(1)} %pad_maximum_fusion.9.refs_6_), channel_id=1, source_target_pairs={{0,16},{1,17},{2,18},{3,19},{4,20},{5,21},{6,22},{7,23},{8,24},{9,... | collective-permute-start | bytes 1572872 | tf_op jit(solution)/shard_map/ppermute | solution.py:44
  79.4 24.4 %collective-permute-start.19 = (bf16[8,2,32,512]{3,2,1,0:T(8,128)(2,1)S(1)}, bf16[8,2,32,512]{3,2,1,0:T(8,128)(2,1)}, u32[]{:S(2)}, u32[]{:S(2)}) collective-permute-start(bf16[8,2,32,512]{3,2,1,0:T(8,128)(2,1)S(1)} %pad_maximum_fusion.8.refs_5_), channel_id=1, source_target_pairs={{0,12},{1,13},{2,14},{3,15},{4,8},{5,9},{6,10},{7,11},{8,4},{9,5},... | collective-permute-start | bytes 1572872 | tf_op jit(solution)/shard_map/ppermute | solution.py:44
  79.5 9.6 %collective-permute-start.26 = (bf16[8,2,32,512]{3,2,1,0:T(8,128)(2,1)}, bf16[8,2,32,512]{3,2,1,0:T(8,128)(2,1)}, u32[]{:S(2)}, u32[]{:S(2)}) collective-permute-start(bf16[8,2,32,512]{3,2,1,0:T(8,128)(2,1)} %collective-permute-done.15.refs_8_), channel_id=1, source_target_pairs={{0,16},{1,17},{2,18},{3,19},{4,20},{5,21},{6,22},{7,23},{8,24},{9,... | collective-permute-start | bytes 1572872 | tf_op jit(solution)/shard_map/ppermute | solution.py:44
  89.1 17.2 %collective-permute-start.21 = (bf16[8,2,32,512]{3,2,1,0:T(8,128)(2,1)S(1)}, bf16[8,2,32,512]{3,2,1,0:T(8,128)(2,1)}, u32[]{:S(2)}, u32[]{:S(2)}) collective-permute-start(bf16[8,2,32,512]{3,2,1,0:T(8,128)(2,1)S(1)} %pad_maximum_fusion.8.refs_5_), channel_id=1, source_target_pairs={{0,16},{1,17},{2,18},{3,19},{4,20},{5,21},{6,22},{7,23},{8,24},{9,... | collective-permute-start | bytes 1572872 | tf_op jit(solution)/shard_map/ppermute | solution.py:44
  104.0 13.4 %collective-permute-start.16 = (bf16[8,2,32,512]{3,2,1,0:T(8,128)(2,1)}, bf16[8,2,32,512]{3,2,1,0:T(8,128)(2,1)}, u32[]{:S(2)}, u32[]{:S(2)}) collective-permute-start(bf16[8,2,32,512]{3,2,1,0:T(8,128)(2,1)} %pad_maximum_fusion.5.refs_6_), channel_id=1, source_target_pairs={{0,1},{1,0},{2,3},{3,2},{4,5},{5,4},{6,7},{7,6},{8,9},{9,8},{10,11... | collective-permute-start | bytes 1572872 | tf_op jit(solution)/shard_map/ppermute | solution.py:44
  105.6 12.2 %collective-permute-start.14 = (bf16[8,2,32,512]{3,2,1,0:T(8,128)(2,1)}, bf16[8,2,32,512]{3,2,1,0:T(8,128)(2,1)}, u32[]{:S(2)}, u32[]{:S(2)}) collective-permute-start(bf16[8,2,32,512]{3,2,1,0:T(8,128)(2,1)} %pad_maximum_fusion.4.refs_5_), channel_id=1, source_target_pairs={{0,12},{1,13},{2,14},{3,15},{4,8},{5,9},{6,10},{7,11},{8,4},{9,5},... | collective-permute-start | bytes 1572872 | tf_op jit(solution)/shard_map/ppermute | solution.py:44
  106.3 11.7 %collective-permute-start.18 = (bf16[8,2,32,512]{3,2,1,0:T(8,128)(2,1)}, bf16[8,2,32,512]{3,2,1,0:T(8,128)(2,1)}, u32[]{:S(2)}, u32[]{:S(2)}) collective-permute-start(bf16[8,2,32,512]{3,2,1,0:T(8,128)(2,1)} %pad_maximum_fusion.5.refs_6_), channel_id=1, source_target_pairs={{0,16},{1,17},{2,18},{3,19},{4,20},{5,21},{6,22},{7,23},{8,24},{9,... | collective-permute-start | bytes 1572872 | tf_op jit(solution)/shard_map/ppermute | solution.py:44
  107.7 10.4 %collective-permute-start.17 = (bf16[8,2,32,512]{3,2,1,0:T(8,128)(2,1)}, bf16[8,2,32,512]{3,2,1,0:T(8,128)(2,1)}, u32[]{:S(2)}, u32[]{:S(2)}) collective-permute-start(bf16[8,2,32,512]{3,2,1,0:T(8,128)(2,1)} %pad_maximum_fusion.4.refs_5_), channel_id=1, source_target_pairs={{0,16},{1,17},{2,18},{3,19},{4,20},{5,21},{6,22},{7,23},{8,24},{9,... | collective-permute-start | bytes 1572872 | tf_op jit(solution)/shard_map/ppermute | solution.py:44
  (18 other events, 189.8 us)

commit v3 on v2

--- a/solution.py
+++ b/solution.py
@@ -13,6 +13,8 @@
 
 CLASSES = (((1, 3, 4, 12), (3, 4, 12, 1)), ((4, 12, 1, 3), (12, 1, 3, 4)))
 ZCLASSES = ((2, 6), (6, 2))
+
+MEMBERS = (0, 2, 3)
 
 PAIRS = ((0, 1), (0, 2), (0, 3), (1, 2), (1, 3), (2, 3))
 
@@ -61,13 +63,10 @@
     copies = []
     for index in range(RUN):
         slot = owner[index] & 3
-        for entry in range(4):
-            for part, target in ((core, mine), (1 - core, other)):
-                copies.append(
-                    pltpu.make_async_copy(
-                        jones.at[slot, entry, part], target.at[index, entry], semaphore.at[len(copies)]
-                    )
-                )
+        for part, target in ((core, mine), (1 - core, other)):
+            copies.append(
+                pltpu.make_async_copy(jones.at[slot, :, part], target.at[index], semaphore.at[len(copies)])
+            )
     for copy in copies:
         copy.start()
     for copy in copies:
@@ -82,7 +81,7 @@
         out_shape=(shape, shape),
         in_specs=[scalars, scalars, pl.BlockSpec(memory_space=pl.ANY)],
         out_specs=(pl.BlockSpec(memory_space=pltpu.VMEM), pl.BlockSpec(memory_space=pltpu.VMEM)),
-        scratch_shapes=[pltpu.SemaphoreType.DMA((RUN * 8,))],
+        scratch_shapes=[pltpu.SemaphoreType.DMA((RUN * 2,))],
         compiler_params=pltpu.CompilerParams(vmem_limit_bytes=60 * 1024 * 1024),
         name="pick",
     )(ids, owner, jones)
@@ -90,9 +89,10 @@
 
 def transform_kernel(index, *refs):
     ids, keep, ku = refs[:3]
-    gathered = refs[3:5]
-    own = (refs[5:7], refs[7:9])
-    far = (refs[9:11], refs[11:13])
+    own = (refs[3:5], refs[5:7], refs[7:9])
+    far = (refs[9:11], refs[11:13], refs[13:15])
+    lasts = refs[15:17]
+    member = MEMBERS[index]
     out, fields, operator, products, left, staged, field_sem, operator_sem, out_sem = refs[-9:]
     core, grid = ids[0], ids[1]
 
@@ -101,18 +101,23 @@
         chosen = jnp.where(core == 0, masks[0], masks[1]) if near else jnp.where(core == 0, masks[1], masks[0])
         return pl.ds(pl.multiple_of((grid ^ chosen) * ROWS, ROWS), ROWS)
 
+    def block_of(group, half, block, at):
+        if block < 8:
+            return group[block // 4][half].at[block % 4, at]
+        return group[2][half].at[block - 8, 0]
+
     for half in range(2):
         for block in range(16):
             for near, source, part in ((True, own, core), (False, far, 1 - core)):
                 pltpu.make_async_copy(
-                    source[block // 8][half].at[block % 8],
+                    block_of(source, half, block, member),
                     fields.at[part, pl.ds(2 * half, 2), placed(half, block, near)],
                     field_sem,
                 ).start()
-    for block in range(16):
-        pltpu.make_async_copy(
-            gathered[block // 8].at[block % 8], operator.at[:, :, placed(0, block, True)], operator_sem
-        ).start()
+    for half in range(2):
+        for block in range(16):
+            source = block_of(own, half, block, 1) if block < 8 else lasts[half].at[block - 8, 1]
+            pltpu.make_async_copy(source, operator.at[half, :, placed(half, block, True)], operator_sem).start()
 
     def multiply(columns):
         for start in range(0, G, 16):
@@ -179,11 +184,11 @@
     pltpu.make_async_copy(staged, staged, out_sem).wait()
 
 
-def transform(index, ids, keep, ku, operators, own, far, previous):
+def transform(index, ids, keep, ku, own, far, lasts, previous):
     anywhere = pl.BlockSpec(memory_space=pl.ANY)
     scalars = pl.BlockSpec(memory_space=pltpu.SMEM)
-    operands = [ids, keep, ku, *operators, *own, *far]
-    specs = [scalars, scalars, pl.BlockSpec(memory_space=pltpu.VMEM)] + [anywhere] * 10
+    operands = [ids, keep, ku, *own, *far, *lasts]
+    specs = [scalars, scalars, pl.BlockSpec(memory_space=pltpu.VMEM)] + [anywhere] * 14
     aliases = {}
     if previous is not None:
         aliases = {len(operands): 0}
@@ -230,29 +235,23 @@
     ids = jnp.stack([core, grid]).astype(jnp.int32)
     mine, other = pick(ids, owner, jones)
 
-    blocks = w_operator[None]
-    blocks = jnp.concatenate([blocks, swap_grid(blocks, 0, 0)], 0)
-
     holder = owner[:RUN] >> 2
     rows = choose((holder & 1) == core, mine, swap_core(other))
     first = ZCLASSES[0][0] + core * (ZCLASSES[1][0] - ZCLASSES[0][0])
     apart = (holder ^ wa) & 6
-    rows = after(rows, blocks)
-    blocks = jnp.concatenate([blocks, swap_grid(blocks, 0, 1)], 0)
     rows = choose(apart == 0, rows, swap_z(rows, 0))
-    rows = after(rows, blocks)
-    blocks = jnp.concatenate([blocks, swap_grid(blocks, 0, 2)], 0)
     rows = choose((apart == 0) | (apart == first), rows, swap_z(rows, 1))
-    rows = after(rows, blocks)
-    operators = (blocks, swap_grid(blocks, 0, 3))
-
-    streams = []
+
+    near, next_blocks = [], []
     for half in range(2):
-        stream = rows[None, :, 2 * half : 2 * half + 2]
+        of_types = rows[:, 2 * half : 2 * half + 2]
+        stream = jnp.concatenate([of_types[:1], w_operator[half : half + 1], of_types[1:]], 0)[None]
         for step in range(2):
             stream = jnp.concatenate([stream, swap_grid(stream, half, step)], 0)
-        stream = after(stream, *operators)
-        streams.append((stream, swap_grid(stream, half, 2)))
+        near.append(stream)
+        next_blocks.append(swap_grid(stream, half, 2))
+    far_near = [swap_core(one) for one in near]
+    far_next = [swap_core(one) for one in next_blocks]
 
     kr, ki = w_operator[:, 0], w_operator[:, 1]
     plain = jnp.stack([kr, ki], 2).reshape(PLANES, 2 * ROWS, G)
@@ -260,20 +259,22 @@
     ku = jnp.concatenate([plain, turned], 1).reshape(PLANES * 4 * ROWS, G)
     keep = mask.reshape(RUN, 16)
 
-    own = []
+    lasts = []
     for index in range(RUN):
-        low = [jnp.concatenate([near[:, index], far[:, index]], 0) for near, far in streams]
-        send = low
+        members = slice(0, 2) if index == 0 else slice(MEMBERS[index], MEMBERS[index] + 1)
+        send = [jnp.concatenate([near[half][:, members], next_blocks[half][:, members]], 0) for half in range(2)]
         if index == 2:
-            send = [after(send[half], own[0][2 + half]) for half in range(2)]
-        own.append((*low, *[swap_grid(send[half], half, 3) for half in range(2)]))
+            send = [after(send[half], lasts[0][half]) for half in range(2)]
+        lasts.append([swap_grid(send[half], half, 3) for half in range(2)])
     result = None
     for index in range(RUN):
-        sent = own[index]
+        sent = [last[:, :1] for last in lasts[index]]
         if result is not None:
-            sent = [*sent[:2], *[after(one, result) for one in sent[2:]]]
-        far = [swap_core(one) for one in sent]
-        result = transform(index, ids, keep[index], ku, operators, own[index], far, result)
+            sent = [after(one, result) for one in sent]
+        far_last = [swap_core(one) for one in sent]
+        own = (*near, *next_blocks, *lasts[index])
+        far = (*far_near, *far_next, *far_last)
+        result = transform(index, ids, keep[index], ku, own, far, lasts[0], result)
     return result
 
 

time: 130 us -> 158 us (1.22)
  local copies, waits for them, and re-layouts: 8.25 us -> 30.3 us
  waiting for transfers between devices: 34.2 us -> 41.2 us
  starting transfers between devices: 45.2 us -> 40.9 us
  Pallas kernels: 31.5 us -> 33.7 us
    unnamed x22 -> x46, local copies, waits for them, and re-layouts: 4.47 us -> 21.3 us
    slice x1 -> x14, local copies, waits for them, and re-layouts: 0.01 us -> 7.83 us  [the longest x4 3.64 us: body(): next_blocks[half][:, members]]
    ppermute x31 -> x25, waiting for transfers between devices: 34.2 us -> 41.2 us  [exchange(): return lax.ppermute(value, ('wa', 'grid'), perm)]
    ppermute x31 -> x25, starting transfers between devices: 45.2 us -> 40.9 us  [exchange(): return lax.ppermute(value, ('wa', 'grid'), perm)]
    squeeze x8 -> x3, local copies, waits for them, and re-layouts: 3.37 us -> 0.25 us  [body(): result = transform(index, ids, keep[index], ku, own, far, lasts[0], result)]
    pallas_call x3, Pallas kernels: 28.7 us -> 30.8 us  [transform(): pl.pallas_call(kernel, out_shape=jax.ShapeDtypeStruct((ROWS, PLANES, RUN,...]
    concatenate x9 -> x6, other arithmetic: 6.86 us -> 5.7 us  [body(): jnp.concatenate([near[half][:, members], next_blocks[half][:, members]], 0)]
  transfers between devices with their start and end apart: 31 -> 25, of which waited for: 9 -> 12; matrix products, arithmetic and copies ran while one was open for 10% -> 11% of each run, Pallas kernels for 15% -> 13%
where the time goes in v3:
time: 158 us; the launch traced here: 157 us
  waiting for transfers between devices  41.2 us (26%)
  starting transfers between devices  40.9 us (26%)
  Pallas kernels  33.7 us (21%)
  local copies, waits for them, and re-layouts  30.3 us (19%)
  other arithmetic  9.91 us (6%)
    ppermute x25, waiting for transfers between devices, exchange(): return lax.ppermute(value, ('wa', 'grid'), perm)  41.2 us
    ppermute x25, starting transfers between devices, exchange(): return lax.ppermute(value, ('wa', 'grid'), perm)  40.9 us
    pallas_call x3, Pallas kernels, transform(): pl.pallas_call(kernel, out_shape=jax.ShapeDtypeStruct((ROWS, PLANES, RUN,...  30.8 us
    unnamed x46, local copies, waits for them, and re-layouts  21.3 us
    concatenate x6, other arithmetic, body(): jnp.concatenate([near[half][:, members], next_blocks[half][:, members]], 0)  5.7 us
    slice x4, local copies, waits for them, and re-layouts, body(): next_blocks[half][:, members]  3.64 us
  transfers between devices with their start and end apart: 25, of which 12 were waited for; matrix products, arithmetic and copies ran while one was open for 11% of the time, Pallas kernels for 13%

profile of v3, /device:TPU:1, one launch (start us, length us, event | category | flops | bytes accessed | tf_op | source)
XLA Modules:
  0.0 156.5 jit_solution(2107317511806833485)
XLA Ops:
  0.6 2.9 %pick.1 = (bf16[3,4,32,512]{3,2,1,0:T(8,128)(2,1)}, bf16[3,4,32,512]{3,2,1,0:T(8,128)(2,1)}) custom-call(s32[2]{0:T(128)} %pad_add_fusion.ids.refs_0_, s32[32]{0:T(128)} %owner.1, bf16[4,4,2,32,512]{4,3,2,1,0:T(8,128)(2,1)} %jones.1), custom_call_target="tpu_custom_call" | custom-call | tf_op jit(solution)/shard_map/pick/pallas_call | solution.py:79
  3.5 1.5 collective-permute-start
  7.7 3.9 %collective-permute-start.1 = (bf16[3,4,32,512]{3,2,1,0:T(8,128)(2,1)S(1)}, bf16[3,4,32,512]{3,2,1,0:T(8,128)(2,1)S(1)}, u32[]{:S(2)}, u32[]{:S(2)}) collective-permute-start(bf16[3,4,32,512]{3,2,1,0:T(8,128)(2,1)S(1)} %broadcast_select_fusion), channel_id=1, source_target_pairs={{0,32},{1,33},{2,34},{3,35},{4,36},{5,37},{6,38},{7,39},{8,40},{9,... | collective-permute-start | bytes 1179656 | tf_op jit(solution)/shard_map/ppermute | solution.py:46
  11.6 5.2 %collective-permute-done.1 = bf16[3,4,32,512]{3,2,1,0:T(8,128)(2,1)S(1)} collective-permute-done((bf16[3,4,32,512]{3,2,1,0:T(8,128)(2,1)S(1)}, bf16[3,4,32,512]{3,2,1,0:T(8,128)(2,1)S(1)}, u32[]{:S(2)}, u32[]{:S(2)}) %collective-permute-start.1) | collective-permute-done | bytes 393248 | tf_op jit(solution)/shard_map/ppermute | solution.py:46
  17.9 6.0 %collective-permute-done.2 = bf16[3,4,32,512]{3,2,1,0:T(8,128)(2,1)S(1)} collective-permute-done((bf16[3,4,32,512]{3,2,1,0:T(8,128)(2,1)S(1)}, bf16[3,4,32,512]{3,2,1,0:T(8,128)(2,1)S(1)}, u32[]{:S(2)}, u32[]{:S(2)}) %collective-permute-start.2) | collective-permute-done | bytes 393248 | tf_op jit(solution)/shard_map/ppermute | solution.py:46
  24.1 2.8 %collective-permute-start.5 = (bf16[1,4,2,32,512]{4,3,2,1,0:T(8,128)(2,1)S(1)}, bf16[1,4,2,32,512]{4,3,2,1,0:T(8,128)(2,1)S(1)}, u32[]{:S(2)}, u32[]{:S(2)}) collective-permute-start(bf16[1,4,2,32,512]{4,3,2,1,0:T(8,128)(2,1)S(1)} %maximum_bitcast_fusion.1), channel_id=1, source_target_pairs={{0,3},{1,2},{2,1},{3,0},{4,7},{5,6},{6,5},{7,4},{8,11},{9,10},{10,... | collective-permute-start | bytes 786440 | tf_op jit(solution)/shard_map/ppermute | solution.py:46
  27.0 3.9 %collective-permute-done.5 = bf16[1,4,2,32,512]{4,3,2,1,0:T(8,128)(2,1)S(1)} collective-permute-done((bf16[1,4,2,32,512]{4,3,2,1,0:T(8,128)(2,1)S(1)}, bf16[1,4,2,32,512]{4,3,2,1,0:T(8,128)(2,1)S(1)}, u32[]{:S(2)}, u32[]{:S(2)}) %collective-permute-start.5) | collective-permute-done | bytes 262176 | tf_op jit(solution)/shard_map/ppermute | solution.py:46
  32.6 2.2 %collective-permute-start.4 = (bf16[2,4,2,32,512]{4,3,2,1,0:T(8,128)(2,1)S(1)}, bf16[2,4,2,32,512]{4,3,2,1,0:T(8,128)(2,1)S(1)}, u32[]{:S(2)}, u32[]{:S(2)}) collective-permute-start(bf16[2,4,2,32,512]{4,3,2,1,0:T(8,128)(2,1)S(1)} %pad_maximum_fusion.4), channel_id=1, source_target_pairs={{0,3},{1,2},{2,1},{3,0},{4,7},{5,6},{6,5},{7,4},{8,11},{9,10},{10,... | collective-permute-start | bytes 1572872 | tf_op jit(solution)/shard_map/ppermute | solution.py:46
  34.8 5.9 %collective-permute-done.6 = bf16[2,4,2,32,512]{4,3,2,1,0:T(8,128)(2,1)S(1)} collective-permute-done((bf16[2,4,2,32,512]{4,3,2,1,0:T(8,128)(2,1)S(1)}, bf16[2,4,2,32,512]{4,3,2,1,0:T(8,128)(2,1)S(1)}, u32[]{:S(2)}, u32[]{:S(2)}) %collective-permute-start.6) | collective-permute-done | bytes 524320 | tf_op jit(solution)/shard_map/ppermute | solution.py:46
  40.8 1.2 collective-permute-start.8
  44.0 14.1 %collective-permute-done.8.refs_6_ = bf16[4,4,2,32,512]{4,3,2,1,0:T(8,128)(2,1)S(1)} collective-permute-done((bf16[4,4,2,32,512]{4,3,2,1,0:T(8,128)(2,1)S(1)}, bf16[4,4,2,32,512]{4,3,2,1,0:T(8,128)(2,1)S(1)}, u32[]{:S(2)}, u32[]{:S(2)}) %collective-permute-start.8) | collective-permute-done | bytes 1048608 | tf_op jit(solution)/shard_map/ppermute | solution.py:46
  58.3 2.6 %collective-permute-start.11 = (bf16[8,2,2,32,512]{4,3,2,1,0:T(8,128)(2,1)S(1)}, bf16[8,2,2,32,512]{4,3,2,1,0:T(8,128)(2,1)S(1)}, u32[]{:S(2)}, u32[]{:S(2)}) collective-permute-start(bf16[8,2,2,32,512]{4,3,2,1,0:T(8,128)(2,1)S(1)} %pad_maximum_fusion.3), channel_id=1, source_target_pairs={{0,1},{1,0},{2,3},{3,2},{4,5},{5,4},{6,7},{7,6},{8,9},{9,8},{10,11... | collective-permute-start | bytes 3145736 | tf_op jit(solution)/shard_map/ppermute | solution.py:46
  63.6 11.2 %collective-permute-start.16 = (bf16[4,4,2,32,512]{4,3,2,1,0:T(8,128)(2,1)S(1)}, bf16[4,4,2,32,512]{4,3,2,1,0:T(8,128)(2,1)S(1)}, u32[]{:S(2)}, u32[]{:S(2)}) collective-permute-start(bf16[4,4,2,32,512]{4,3,2,1,0:T(8,128)(2,1)S(1)} %collective-permute-done.8.refs_6_), channel_id=1, source_target_pairs={{0,16},{1,17},{2,18},{3,19},{4,20},{5,21},{6,22},{7,23},{8,24},{9,... | collective-permute-start | bytes 3145736 | tf_op jit(solution)/shard_map/ppermute | solution.py:46
  78.0 1.8 %fusion.4 = (bf16[4,1,2,32,512]{4,3,2,1,0:T(8,128)(2,1)S(1)}, bf16[4,1,2,32,512]{4,3,2,1,0:T(8,128)(2,1)}) fusion(bf16[4,4,2,32,512]{4,3,2,1,0:T(8,128)(2,1)} %collective-permute-done.7.refs_5_), kind=kLoop, calls=%fused_computation.30 | loop fusion | bytes 1048576 | tf_op jit(solution)/shard_map/slice | solution.py:265
  81.5 1.5 collective-permute-start.18
  85.8 7.9 %collective-permute-start.20 = (bf16[8,1,2,32,512]{4,3,2,1,0:T(8,128)(2,1)}, bf16[8,1,2,32,512]{4,3,2,1,0:T(8,128)(2,1)}, u32[]{:S(2)}, u32[]{:S(2)}) collective-permute-start(bf16[8,1,2,32,512]{4,3,2,1,0:T(8,128)(2,1)} %slice.130), channel_id=1, source_target_pairs={{0,16},{1,17},{2,18},{3,19},{4,20},{5,21},{6,22},{7,23},{8,24},{9,... | collective-permute-start | bytes 1572872 | tf_op jit(solution)/shard_map/ppermute | solution.py:46
  96.4 1.9 %pad_maximum_fusion.7 = bf16[8,1,2,32,512]{4,3,2,1,0:T(8,128)(2,1)} fusion(bf16[4,1,2,32,512]{4,3,2,1,0:T(8,128)(2,1)} %get-tuple-element.24, bf16[4,1,2,32,512]{4,3,2,1,0:T(8,128)(2,1)} %get-tuple-element.22), kind=kLoop, calls=%fused_computation.7 | loop fusion | flops 262144 | bytes 1048576 | tf_op jit(solution)/shard_map/concatenate | solution.py:265
  98.3 1.9 %pad_maximum_fusion.6 = bf16[8,1,2,32,512]{4,3,2,1,0:T(8,128)(2,1)} fusion(bf16[4,1,2,32,512]{4,3,2,1,0:T(8,128)(2,1)} %get-tuple-element.28, bf16[4,1,2,32,512]{4,3,2,1,0:T(8,128)(2,1)} %get-tuple-element.26), kind=kLoop, calls=%fused_computation.6 | loop fusion | flops 262144 | bytes 1048576 | tf_op jit(solution)/shard_map/concatenate | solution.py:265
  103.9 1.2 copy-done.13
  106.3 10.9 %transform.3.refs_17_ = bf16[32,2,3,16,2,512]{5,4,3,2,1,0:T(2,128)(2,1)} custom-call(s32[2]{0:T(128)S(1)} %copy-done.20, s32[16]{0:T(128)S(1)} %squeeze.12.refs_1_, bf16[256,512]{1,0:T(8,128)(2,1)S(1)} %bitcast.17, bf16[4,4,2,32,512]{4,3,2,1,0:T(8,128)(2,1)S(1)} %pad_maximum_fusion.refs_3_, bf16[4,4,2,32,512]{4,3,2,1,0:T(8,128)(2,1)S(1)} %pad_maximum_fusion.1.refs_4_, ...), custom_call_target="tpu_custom_call" | custom-call | flops 1000000 | bytes 1000000 | tf_op jit(solution)/shard_map/transform/pallas_call | solution.py:201
  118.2 1.5 collective-permute-done.21.refs_13_
  126.6 10.0 %transform.4.refs_17_ = bf16[32,2,3,16,2,512]{5,4,3,2,1,0:T(2,128)(2,1)} custom-call(s32[2]{0:T(128)S(1)} %copy-done.20, s32[16]{0:T(128)S(1)} %squeeze.11.refs_1_, bf16[256,512]{1,0:T(8,128)(2,1)S(1)} %bitcast.18, bf16[4,4,2,32,512]{4,3,2,1,0:T(8,128)(2,1)S(1)} %pad_maximum_fusion.refs_3_, ...), custom_call_target="tpu_custom_call", output_to_operand_aliasing={{}: (17, {})} | custom-call | flops 1000000 | bytes 1000000 | tf_op jit(solution)/shard_map/transform/pallas_call | solution.py:201
  138.1 1.5 collective-permute-done.23.refs_13_
  146.4 9.9 %transform.5 = bf16[32,2,3,16,2,512]{5,4,3,2,1,0:T(2,128)(2,1)} custom-call(s32[2]{0:T(128)S(1)} %copy-done.20, s32[16]{0:T(128)S(1)} %squeeze.10.refs_1_, bf16[256,512]{1,0:T(8,128)(2,1)S(1)} %bitcast.19, bf16[4,4,2,32,512]{4,3,2,1,0:T(8,128)(2,1)S(1)} %pad_maximum_fusion.refs_3_, ...), custom_call_target="tpu_custom_call", output_to_operand_aliasing={{}: (17, {})} | custom-call | flops 1000000 | bytes 1000000 | tf_op jit(solution)/shard_map/transform/pallas_call | solution.py:201
  (117 shorter events, 42.3 us)
Async XLA Ops:
  3.5 3.1 %collective-permute-start = (bf16[3,4,32,512]{3,2,1,0:T(8,128)(2,1)}, bf16[3,4,32,512]{3,2,1,0:T(8,128)(2,1)S(1)}, u32[]{:S(2)}, u32[]{:S(2)}) collective-permute-start(bf16[3,4,32,512]{3,2,1,0:T(8,128)(2,1)} %get-tuple-element.14), channel_id=1, source_target_pairs={{0,16},{1,17},{2,18},{3,19},{4,20},{5,21},{6,22},{7,23},{8,24},{9,... | collective-permute-start | bytes 1179656 | tf_op jit(solution)/shard_map/ppermute | solution.py:46
  7.7 9.1 %collective-permute-start.1 = (bf16[3,4,32,512]{3,2,1,0:T(8,128)(2,1)S(1)}, bf16[3,4,32,512]{3,2,1,0:T(8,128)(2,1)S(1)}, u32[]{:S(2)}, u32[]{:S(2)}) collective-permute-start(bf16[3,4,32,512]{3,2,1,0:T(8,128)(2,1)S(1)} %broadcast_select_fusion), channel_id=1, source_target_pairs={{0,32},{1,33},{2,34},{3,35},{4,36},{5,37},{6,38},{7,39},{8,40},{9,... | collective-permute-start | bytes 1179656 | tf_op jit(solution)/shard_map/ppermute | solution.py:46
  16.9 7.0 %collective-permute-start.2 = (bf16[3,4,32,512]{3,2,1,0:T(8,128)(2,1)S(1)}, bf16[3,4,32,512]{3,2,1,0:T(8,128)(2,1)S(1)}, u32[]{:S(2)}, u32[]{:S(2)}) collective-permute-start(bf16[3,4,32,512]{3,2,1,0:T(8,128)(2,1)S(1)} %broadcast_select_fusion.1), channel_id=1, source_target_pairs={{0,96},{1,97},{2,98},{3,99},{4,100},{5,101},{6,102},{7,103},{8,104... | collective-permute-start | bytes 1179656 | tf_op jit(solution)/shard_map/ppermute | solution.py:46
  24.1 6.9 %collective-permute-start.5 = (bf16[1,4,2,32,512]{4,3,2,1,0:T(8,128)(2,1)S(1)}, bf16[1,4,2,32,512]{4,3,2,1,0:T(8,128)(2,1)S(1)}, u32[]{:S(2)}, u32[]{:S(2)}) collective-permute-start(bf16[1,4,2,32,512]{4,3,2,1,0:T(8,128)(2,1)S(1)} %maximum_bitcast_fusion.1), channel_id=1, source_target_pairs={{0,3},{1,2},{2,1},{3,0},{4,7},{5,6},{6,5},{7,4},{8,11},{9,10},{10,... | collective-permute-start | bytes 786440 | tf_op jit(solution)/shard_map/ppermute | solution.py:46
  26.9 5.6 %collective-permute-start.3 = (bf16[1,4,2,32,512]{4,3,2,1,0:T(8,128)(2,1)S(1)}, bf16[1,4,2,32,512]{4,3,2,1,0:T(8,128)(2,1)S(1)}, u32[]{:S(2)}, u32[]{:S(2)}) collective-permute-start(bf16[1,4,2,32,512]{4,3,2,1,0:T(8,128)(2,1)S(1)} %maximum_bitcast_fusion), channel_id=1, source_target_pairs={{0,1},{1,0},{2,3},{3,2},{4,5},{5,4},{6,7},{7,6},{8,9},{9,8},{10,11... | collective-permute-start | bytes 786440 | tf_op jit(solution)/shard_map/ppermute | solution.py:46
  31.0 9.7 %collective-permute-start.6 = (bf16[2,4,2,32,512]{4,3,2,1,0:T(8,128)(2,1)S(1)}, bf16[2,4,2,32,512]{4,3,2,1,0:T(8,128)(2,1)S(1)}, u32[]{:S(2)}, u32[]{:S(2)}) collective-permute-start(bf16[2,4,2,32,512]{4,3,2,1,0:T(8,128)(2,1)S(1)} %pad_maximum_fusion.5), channel_id=1, source_target_pairs={{0,4},{1,5},{2,6},{3,7},{4,0},{5,1},{6,2},{7,3},{8,12},{9,13},{10,... | collective-permute-start | bytes 1572872 | tf_op jit(solution)/shard_map/ppermute | solution.py:46
  32.6 9.6 %collective-permute-start.4 = (bf16[2,4,2,32,512]{4,3,2,1,0:T(8,128)(2,1)S(1)}, bf16[2,4,2,32,512]{4,3,2,1,0:T(8,128)(2,1)S(1)}, u32[]{:S(2)}, u32[]{:S(2)}) collective-permute-start(bf16[2,4,2,32,512]{4,3,2,1,0:T(8,128)(2,1)S(1)} %pad_maximum_fusion.4), channel_id=1, source_target_pairs={{0,3},{1,2},{2,1},{3,0},{4,7},{5,6},{6,5},{7,4},{8,11},{9,10},{10,... | collective-permute-start | bytes 1572872 | tf_op jit(solution)/shard_map/ppermute | solution.py:46
  40.8 17.3 %collective-permute-start.8 = (bf16[4,4,2,32,512]{4,3,2,1,0:T(8,128)(2,1)S(1)}, bf16[4,4,2,32,512]{4,3,2,1,0:T(8,128)(2,1)S(1)}, u32[]{:S(2)}, u32[]{:S(2)}) collective-permute-start(bf16[4,4,2,32,512]{4,3,2,1,0:T(8,128)(2,1)S(1)} %pad_maximum_fusion.1.refs_4_), channel_id=1, source_target_pairs={{0,12},{1,13},{2,14},{3,15},{4,8},{5,9},{6,10},{7,11},{8,4},{9,5},... | collective-permute-start | bytes 3145736 | tf_op jit(solution)/shard_map/ppermute | solution.py:46
  42.3 19.2 %collective-permute-start.7 = (bf16[4,4,2,32,512]{4,3,2,1,0:T(8,128)(2,1)S(1)}, bf16[4,4,2,32,512]{4,3,2,1,0:T(8,128)(2,1)}, u32[]{:S(2)}, u32[]{:S(2)}) collective-permute-start(bf16[4,4,2,32,512]{4,3,2,1,0:T(8,128)(2,1)S(1)} %pad_maximum_fusion.refs_3_), channel_id=1, source_target_pairs={{0,4},{1,5},{2,6},{3,7},{4,0},{5,1},{6,2},{7,3},{8,12},{9,13},{10,... | collective-permute-start | bytes 3145736 | tf_op jit(solution)/shard_map/ppermute | solution.py:46
  58.3 19.7 %collective-permute-start.11 = (bf16[8,2,2,32,512]{4,3,2,1,0:T(8,128)(2,1)S(1)}, bf16[8,2,2,32,512]{4,3,2,1,0:T(8,128)(2,1)S(1)}, u32[]{:S(2)}, u32[]{:S(2)}) collective-permute-start(bf16[8,2,2,32,512]{4,3,2,1,0:T(8,128)(2,1)S(1)} %pad_maximum_fusion.3), channel_id=1, source_target_pairs={{0,1},{1,0},{2,3},{3,2},{4,5},{5,4},{6,7},{7,6},{8,9},{9,8},{10,11... | collective-permute-start | bytes 3145736 | tf_op jit(solution)/shard_map/ppermute | solution.py:46
  61.0 22.9 %collective-permute-start.14 = (bf16[4,4,2,32,512]{4,3,2,1,0:T(8,128)(2,1)S(1)}, bf16[4,4,2,32,512]{4,3,2,1,0:T(8,128)(2,1)S(1)}, u32[]{:S(2)}, u32[]{:S(2)}) collective-permute-start(bf16[4,4,2,32,512]{4,3,2,1,0:T(8,128)(2,1)S(1)} %pad_maximum_fusion.1.refs_4_), channel_id=1, source_target_pairs={{0,16},{1,17},{2,18},{3,19},{4,20},{5,21},{6,22},{7,23},{8,24},{9,... | collective-permute-start | bytes 3145736 | tf_op jit(solution)/shard_map/ppermute | solution.py:46
  61.1 23.8 %collective-permute-start.13 = (bf16[4,4,2,32,512]{4,3,2,1,0:T(8,128)(2,1)S(1)}, bf16[4,4,2,32,512]{4,3,2,1,0:T(8,128)(2,1)S(1)}, u32[]{:S(2)}, u32[]{:S(2)}) collective-permute-start(bf16[4,4,2,32,512]{4,3,2,1,0:T(8,128)(2,1)S(1)} %pad_maximum_fusion.refs_3_), channel_id=1, source_target_pairs={{0,16},{1,17},{2,18},{3,19},{4,20},{5,21},{6,22},{7,23},{8,24},{9,... | collective-permute-start | bytes 3145736 | tf_op jit(solution)/shard_map/ppermute | solution.py:46
  62.7 18.7 %collective-permute-start.9 = (bf16[8,2,2,32,512]{4,3,2,1,0:T(8,128)(2,1)S(1)}, bf16[8,2,2,32,512]{4,3,2,1,0:T(8,128)(2,1)S(1)}, u32[]{:S(2)}, u32[]{:S(2)}) collective-permute-start(bf16[8,2,2,32,512]{4,3,2,1,0:T(8,128)(2,1)S(1)} %pad_maximum_fusion.2), channel_id=1, source_target_pairs={{0,12},{1,13},{2,14},{3,15},{4,8},{5,9},{6,10},{7,11},{8,4},{9,5},... | collective-permute-start | bytes 3145736 | tf_op jit(solution)/shard_map/ppermute | solution.py:46
  63.6 30.1 %collective-permute-start.16 = (bf16[4,4,2,32,512]{4,3,2,1,0:T(8,128)(2,1)S(1)}, bf16[4,4,2,32,512]{4,3,2,1,0:T(8,128)(2,1)S(1)}, u32[]{:S(2)}, u32[]{:S(2)}) collective-permute-start(bf16[4,4,2,32,512]{4,3,2,1,0:T(8,128)(2,1)S(1)} %collective-permute-done.8.refs_6_), channel_id=1, source_target_pairs={{0,16},{1,17},{2,18},{3,19},{4,20},{5,21},{6,22},{7,23},{8,24},{9,... | collective-permute-start | bytes 3145736 | tf_op jit(solution)/shard_map/ppermute | solution.py:46
  78.0 22.2 %collective-permute-start.15 = (bf16[4,4,2,32,512]{4,3,2,1,0:T(8,128)(2,1)}, bf16[4,4,2,32,512]{4,3,2,1,0:T(8,128)(2,1)}, u32[]{:S(2)}, u32[]{:S(2)}) collective-permute-start(bf16[4,4,2,32,512]{4,3,2,1,0:T(8,128)(2,1)} %collective-permute-done.7.refs_5_), channel_id=1, source_target_pairs={{0,16},{1,17},{2,18},{3,19},{4,20},{5,21},{6,22},{7,23},{8,24},{9,... | collective-permute-start | bytes 3145736 | tf_op jit(solution)/shard_map/ppermute | solution.py:46
  81.5 35.8 %collective-permute-start.18 = (bf16[8,1,2,32,512]{4,3,2,1,0:T(8,128)(2,1)}, bf16[8,1,2,32,512]{4,3,2,1,0:T(8,128)(2,1)}, u32[]{:S(2)}, u32[]{:S(2)}) collective-permute-start(bf16[8,1,2,32,512]{4,3,2,1,0:T(8,128)(2,1)} %pad_maximum_fusion.9), channel_id=1, source_target_pairs={{0,1},{1,0},{2,3},{3,2},{4,5},{5,4},{6,7},{7,6},{8,9},{9,8},{10,11... | collective-permute-start | bytes 1572872 | tf_op jit(solution)/shard_map/ppermute | solution.py:46
  84.8 32.5 %collective-permute-start.17 = (bf16[8,1,2,32,512]{4,3,2,1,0:T(8,128)(2,1)}, bf16[8,1,2,32,512]{4,3,2,1,0:T(8,128)(2,1)}, u32[]{:S(2)}, u32[]{:S(2)}) collective-permute-start(bf16[8,1,2,32,512]{4,3,2,1,0:T(8,128)(2,1)} %pad_maximum_fusion.8), channel_id=1, source_target_pairs={{0,12},{1,13},{2,14},{3,15},{4,8},{5,9},{6,10},{7,11},{8,4},{9,5},... | collective-permute-start | bytes 1572872 | tf_op jit(solution)/shard_map/ppermute | solution.py:46
  85.8 14.4 %collective-permute-start.20 = (bf16[8,1,2,32,512]{4,3,2,1,0:T(8,128)(2,1)}, bf16[8,1,2,32,512]{4,3,2,1,0:T(8,128)(2,1)}, u32[]{:S(2)}, u32[]{:S(2)}) collective-permute-start(bf16[8,1,2,32,512]{4,3,2,1,0:T(8,128)(2,1)} %slice.130), channel_id=1, source_target_pairs={{0,16},{1,17},{2,18},{3,19},{4,20},{5,21},{6,22},{7,23},{8,24},{9,... | collective-permute-start | bytes 1572872 | tf_op jit(solution)/shard_map/ppermute | solution.py:46
  94.7 5.5 %collective-permute-start.19 = (bf16[8,1,2,32,512]{4,3,2,1,0:T(8,128)(2,1)}, bf16[8,1,2,32,512]{4,3,2,1,0:T(8,128)(2,1)}, u32[]{:S(2)}, u32[]{:S(2)}) collective-permute-start(bf16[8,1,2,32,512]{4,3,2,1,0:T(8,128)(2,1)} %slice.129), channel_id=1, source_target_pairs={{0,16},{1,17},{2,18},{3,19},{4,20},{5,21},{6,22},{7,23},{8,24},{9,... | collective-permute-start | bytes 1572872 | tf_op jit(solution)/shard_map/ppermute | solution.py:46
  117.9 2.6 %collective-permute-start.22 = (bf16[8,1,2,32,512]{4,3,2,1,0:T(8,128)(2,1)}, bf16[8,1,2,32,512]{4,3,2,1,0:T(8,128)(2,1)}, u32[]{:S(2)}, u32[]{:S(2)}) collective-permute-start(bf16[8,1,2,32,512]{4,3,2,1,0:T(8,128)(2,1)} %collective-permute-done.18.refs_8_), channel_id=1, source_target_pairs={{0,16},{1,17},{2,18},{3,19},{4,20},{5,21},{6,22},{7,23},{8,24},{9,... | collective-permute-start | bytes 1572872 | tf_op jit(solution)/shard_map/ppermute | solution.py:46
  117.9 18.6 %collective-permute-start.12 = (bf16[8,1,2,32,512]{4,3,2,1,0:T(8,128)(2,1)}, bf16[8,1,2,32,512]{4,3,2,1,0:T(8,128)(2,1)}, u32[]{:S(2)}, u32[]{:S(2)}) collective-permute-start(bf16[8,1,2,32,512]{4,3,2,1,0:T(8,128)(2,1)} %pad_maximum_fusion.7), channel_id=1, source_target_pairs={{0,1},{1,0},{2,3},{3,2},{4,5},{5,4},{6,7},{7,6},{8,9},{9,8},{10,11... | collective-permute-start | bytes 1572872 | tf_op jit(solution)/shard_map/ppermute | solution.py:46
  118.2 18.4 %collective-permute-start.10 = (bf16[8,1,2,32,512]{4,3,2,1,0:T(8,128)(2,1)}, bf16[8,1,2,32,512]{4,3,2,1,0:T(8,128)(2,1)}, u32[]{:S(2)}, u32[]{:S(2)}) collective-permute-start(bf16[8,1,2,32,512]{4,3,2,1,0:T(8,128)(2,1)} %pad_maximum_fusion.6), channel_id=1, source_target_pairs={{0,12},{1,13},{2,14},{3,15},{4,8},{5,9},{6,10},{7,11},{8,4},{9,5},... | collective-permute-start | bytes 1572872 | tf_op jit(solution)/shard_map/ppermute | solution.py:46
  136.6 2.9 %collective-permute-start.23 = (bf16[8,1,2,32,512]{4,3,2,1,0:T(8,128)(2,1)}, bf16[8,1,2,32,512]{4,3,2,1,0:T(8,128)(2,1)}, u32[]{:S(2)}, u32[]{:S(2)}) collective-permute-start(bf16[8,1,2,32,512]{4,3,2,1,0:T(8,128)(2,1)} %collective-permute-done.10.refs_7_), channel_id=1, source_target_pairs={{0,16},{1,17},{2,18},{3,19},{4,20},{5,21},{6,22},{7,23},{8,24},{9,... | collective-permute-start | bytes 1572872 | tf_op jit(solution)/shard_map/ppermute | solution.py:46
  137.7 2.6 %collective-permute-start.24 = (bf16[8,1,2,32,512]{4,3,2,1,0:T(8,128)(2,1)}, bf16[8,1,2,32,512]{4,3,2,1,0:T(8,128)(2,1)}, u32[]{:S(2)}, u32[]{:S(2)}) collective-permute-start(bf16[8,1,2,32,512]{4,3,2,1,0:T(8,128)(2,1)} %collective-permute-done.12.refs_8_), channel_id=1, source_target_pairs={{0,16},{1,17},{2,18},{3,19},{4,20},{5,21},{6,22},{7,23},{8,24},{9,... | collective-permute-start | bytes 1572872 | tf_op jit(solution)/shard_map/ppermute | solution.py:46
  (24 other events, 162.8 us)

commit v4 on v3

v4 whole, which is shorter than its diff:
```python
import jax
import jax.numpy as jnp
import numpy as np
from jax import lax
from jax.experimental import pallas as pl
from jax.experimental.pallas import tpu as pltpu
from jax.sharding import PartitionSpec as P

RUN = 3
G = 512
ROWS = 32
PLANES = 2

CLASSES = (((1, 3, 4, 12), (1, 3, 12, 4)), ((4, 12, 1, 3), (4, 12, 3, 1)))
ZCLASSES = ((2, 6), (6, 2))

MEMBERS = (0, 2, 3)

PAIRS = ((0, 1), (0, 2), (0, 3), (1, 2), (1, 3), (2, 3))


def term(a, b):
    return 8 * (a // 2) + 4 * (b // 2) + 2 * (a % 2) + b % 2


def block_masks():
    table = np.zeros((2, 2, 16), np.int32)
    for core in range(2):
        for half in range(2):
            for block in range(16):
                for step in range(4):
                    if block >> step & 1:
                        table[core, half, block] ^= CLASSES[core][half][step]
    return table


MASKS = block_masks()


def exchange(value, wa_mask, grid_mask):
    perm = []
    for wa in range(8):
        for grid in range(16):
            core = wa % 2
            perm.append((wa * 16 + grid, (wa ^ wa_mask(core)) * 16 + (grid ^ grid_mask(core))))
    return lax.ppermute(value, ("wa", "grid"), perm)


def swap_core(value):
    return exchange(value, lambda core: 1, lambda core: 0)


def swap_z(value, step):
    return exchange(value, lambda core: ZCLASSES[core][step], lambda core: 0)


def swap_grid(value, half, step):
    return exchange(value, lambda core: 0, lambda core: CLASSES[core][half][step])


def swap_ring(value, turn):
    masks = [(one[0][0], one[0][1], one[0][0] ^ one[0][1])[turn] for one in CLASSES]
    return exchange(value, lambda core: 0, lambda core: masks[core])


def pick_kernel(ids, owner, jones, mine, other, semaphore):
    core = ids[0]
    copies = []
    for index in range(RUN):
        slot = owner[index] & 3
        for part, target in ((core, mine), (1 - core, other)):
            copies.append(
                pltpu.make_async_copy(jones.at[slot, :, part], target.at[index], semaphore.at[len(copies)])
            )
    for copy in copies:
        copy.start()
    for copy in copies:
        copy.wait()


def pick(ids, owner, jones):
    shape = jax.ShapeDtypeStruct((RUN, 4, ROWS, G), jnp.bfloat16)
    scalars = pl.BlockSpec(memory_space=pltpu.SMEM)
    return pl.pallas_call(
        pick_kernel,
        out_shape=(shape, shape),
        in_specs=[scalars, scalars, pl.BlockSpec(memory_space=pl.ANY)],
        out_specs=(pl.BlockSpec(memory_space=pltpu.VMEM), pl.BlockSpec(memory_space=pltpu.VMEM)),
        scratch_shapes=[pltpu.SemaphoreType.DMA((RUN * 2,))],
        compiler_params=pltpu.CompilerParams(vmem_limit_bytes=60 * 1024 * 1024),
        name="pick",
    )(ids, owner, jones)


def transform_kernel(types, *refs):
    ids, keep, ku = refs[:3]
    own = (refs[3:5], refs[5:7], refs[11:13])
    far = (refs[7:9], refs[9:11], refs[13:15])
    lasts = refs[15:17] if len(types) > 1 else refs[11:13]
    out, fields, operator, products, left, staged, field_sems, operator_sem, out_sems = refs[-9:]
    core, grid = ids[0], ids[1]

    def placed(half, block, near):
        masks = (int(MASKS[0, half, block]), int(MASKS[1, half, block]))
        chosen = jnp.where(core == 0, masks[0], masks[1]) if near else jnp.where(core == 0, masks[1], masks[0])
        return pl.ds(pl.multiple_of((grid ^ chosen) * ROWS, ROWS), ROWS)

    def block_of(group, half, block, member, last_member):
        if block < 8:
            return group[block // 4][half].at[block % 4, member]
        return group[2][half].at[block - 8, last_member]

    def load(turn):
        for half in range(2):
            for block in range(16):
                for near, source, part in ((True, own, core), (False, far, 1 - core)):
                    pltpu.make_async_copy(
                        block_of(source, half, block, MEMBERS[types[turn]], turn),
                        fields.at[turn, part, pl.ds(2 * half, 2), placed(half, block, near)],
                        field_sems.at[turn],
                    ).start()

    load(0)
    for half in range(2):
        for block in range(16):
            source = block_of(own, half, block, 1, 0) if block < 8 else lasts[half].at[block - 8, 1]
            pltpu.make_async_copy(source, operator.at[half, :, placed(half, block, True)], operator_sem).start()
    for turn in range(1, len(types)):
        load(turn)

    def multiply(turn, columns):
        for start in range(0, G, 16):
            rows = slice(start, start + 16)
            re = [fields[turn, 0, entry, rows, columns].astype(jnp.float32) for entry in range(4)]
            im = [fields[turn, 1, entry, rows, columns].astype(jnp.float32) for entry in range(4)]
            for a in range(4):
                products[a, rows, columns] = (re[a] * re[a] + im[a] * im[a]).astype(jnp.bfloat16)
            for at, (a, b) in enumerate(PAIRS):
                products[4 + 2 * at, rows, columns] = (re[a] * re[b] + im[a] * im[b]).astype(jnp.bfloat16)
                products[5 + 2 * at, rows, columns] = (im[a] * re[b] - re[a] * im[b]).astype(jnp.bfloat16)

    def put(plane, entry, columns, value, turned):
        rows = slice(entry * 64, entry * 64 + 64)
        left[plane, rows, columns] = value.astype(jnp.bfloat16)
        left[plane, rows, slice(columns.start + G, columns.stop + G)] = turned.astype(jnp.bfloat16)

    def first_pass(columns):
        def apply(field):
            return jnp.dot(ku[...], products[field, :, columns], preferred_element_type=jnp.float32)

        for a in range(4):
            whole = apply(a)
            for plane in range(PLANES):
                at = plane * 128
                put(plane, term(a, a), columns, whole[at : at + 64], whole[at + 64 : at + 128])
        for pair, (a, b) in enumerate(PAIRS):
            real, imag = apply(4 + 2 * pair), apply(5 + 2 * pair)
            for plane in range(PLANES):
                at = plane * 128
                xa, ya = real[at : at + 64], real[at + 64 : at + 128]
                xb, yb = imag[at : at + 64], imag[at + 64 : at + 128]
                put(plane, term(a, b), columns, xa + yb, ya - xb)
                put(plane, term(b, a), columns, xa - yb, ya + xb)

    chunks = [slice(start, start + 256) for start in range(0, G, 256)]
    contract = (((1,), (1,)), ((), ()))
    for turn, index in enumerate(types):
        pltpu.make_async_copy(fields.at[turn], fields.at[turn], field_sems.at[turn]).wait()
        multiply(turn, chunks[0])
        for step, chunk in enumerate(chunks):
            if step + 1 < len(chunks):
                multiply(turn, chunks[step + 1])
            first_pass(chunk)
        for entry in range(16):

            @pl.when(keep[index * 16 + entry] == 0)
            def _(entry=entry):
                left[:, entry * 64 : entry * 64 + 64] = jnp.zeros((PLANES, 64, 2 * G), jnp.bfloat16)

        if turn == 0:
            pltpu.make_async_copy(operator, operator, operator_sem).wait()
        for plane in range(PLANES):
            for group in range(4):
                rows = slice(group * 256, group * 256 + 256)
                total = lax.dot_general(
                    left[plane, rows, 0:G], operator[plane, 0], contract, preferred_element_type=jnp.float32
                ) + lax.dot_general(
                    left[plane, rows, G : 2 * G], operator[plane, 1], contract, preferred_element_type=jnp.float32
                )
                staged[turn, plane, group * 4 : group * 4 + 4] = total.astype(jnp.bfloat16).reshape(4, ROWS, 2, G)
                for entry in range(group * 4, group * 4 + 4):
                    pltpu.make_async_copy(
                        staged.at[turn, plane, entry], out.at[:, plane, index, entry], out_sems.at[turn]
                    ).start()
    for turn in range(len(types)):
        pltpu.make_async_copy(staged.at[turn], staged.at[turn], out_sems.at[turn]).wait()


def transform(types, ids, keep, ku, shared, own_last, far_last, lasts, previous):
    anywhere = pl.BlockSpec(memory_space=pl.ANY)
    in_hbm = pl.BlockSpec(memory_space=pltpu.HBM)
    scalars = pl.BlockSpec(memory_space=pltpu.SMEM)
    operands = [ids, keep, ku, *shared, *own_last, *far_last, *lasts]
    specs = [scalars, scalars, pl.BlockSpec(memory_space=pltpu.VMEM)] + [in_hbm] * (len(operands) - 3)
    aliases = {}
    if previous is not None:
        aliases = {len(operands): 0}
        operands.append(previous)
        specs.append(anywhere)

    def kernel(*refs):
        transform_kernel(types, *refs)

    count = len(types)
    return pl.pallas_call(
        kernel,
        out_shape=jax.ShapeDtypeStruct((ROWS, PLANES, RUN, 16, 2, G), jnp.bfloat16),
        in_specs=specs,
        out_specs=anywhere,
        input_output_aliases=aliases,
        scratch_shapes=[
            pltpu.VMEM((count, 2, 4, G, G), jnp.bfloat16),
            pltpu.VMEM((PLANES, 2, G, G), jnp.bfloat16),
            pltpu.VMEM((16, G, G), jnp.bfloat16),
            pltpu.VMEM((PLANES, 16 * 64, 2 * G), jnp.bfloat16),
            pltpu.VMEM((count, PLANES, 16, ROWS, 2, G), jnp.bfloat16),
            pltpu.SemaphoreType.DMA((count,)),
            pltpu.SemaphoreType.DMA,
            pltpu.SemaphoreType.DMA((count,)),
        ],
        compiler_params=pltpu.CompilerParams(vmem_limit_bytes=60 * 1024 * 1024),
        cost_estimate=pl.CostEstimate(flops=1_000_000, bytes_accessed=1_000_000, transcendentals=0),
        name="transform",
    )(*operands)


def after(value, *others):
    return lax.optimization_barrier((value, *others))[0]


def together(values):
    return list(lax.optimization_barrier(tuple(values)))


def choose(flags, yes, no):
    return jnp.where(flags[:, None, None, None], yes, no)


def body(jones, owner, mask, w_operator):
    wa = lax.axis_index("wa")
    grid = lax.axis_index("grid")
    core = wa & 1
    ids = jnp.stack([core, grid]).astype(jnp.int32)
    mine, other = pick(ids, owner, jones)

    kr, ki = w_operator[:, 0], w_operator[:, 1]
    plain = jnp.stack([kr, ki], 2).reshape(PLANES, 2 * ROWS, G)
    turned = jnp.stack([-ki, kr], 2).reshape(PLANES, 2 * ROWS, G)
    ku = jnp.concatenate([plain, turned], 1).reshape(PLANES * 4 * ROWS, G)
    keep = mask.reshape(RUN * 16)

    holder = owner[:RUN] >> 2
    rows = choose((holder & 1) == core, mine, swap_core(other))
    first = ZCLASSES[0][0] + core * (ZCLASSES[1][0] - ZCLASSES[0][0])
    apart = (holder ^ wa) & 6
    rows = choose(apart == 0, rows, swap_z(rows, 0))
    rows = choose((apart == 0) | (apart == first), rows, swap_z(rows, 1))
    rows, ku, keep, ids = together((rows, ku, keep, ids))

    halves = []
    for half in range(2):
        of_types = rows[:, 2 * half : 2 * half + 2]
        halves.append(jnp.concatenate([of_types[:1], w_operator[half : half + 1], of_types[1:]], 0))
    held = jnp.stack(halves)
    ring = [held, *together([swap_ring(held, turn) for turn in range(3)])]
    near = [jnp.stack([one[half] for one in ring]) for half in range(2)]
    next_blocks = together([swap_grid(near[half], half, 2) for half in range(2)])
    far_near = [swap_core(one) for one in near]
    far_next = [swap_core(one) for one in next_blocks]

    def send(members):
        return [jnp.concatenate([near[half][:, members], next_blocks[half][:, members]], 0) for half in range(2)]

    last = [swap_grid(one, half, 3) for half, one in enumerate(send(slice(0, 2)))]
    rest = send(slice(2, 4))
    moved = together((*last, *rest, *near, *next_blocks, *far_near, *far_next))
    lasts, rest, shared = [moved[:2]], moved[2:4], tuple(moved[4:])
    far_last = together([swap_core(last[:, :1]) for last in lasts[0]])
    lasts.append(together([swap_grid(one, half, 3) for half, one in enumerate(rest)]))
    result = transform((0,), ids, keep, ku, shared, lasts[0], far_last, (), None)
    far_last = [swap_core(after(last, result)) for last in lasts[1]]
    result = transform((1, 2), ids, keep, ku, shared, lasts[1], far_last, lasts[0], result)
    return result


def solution(mesh):
    return jax.shard_map(
        body,
        mesh=mesh,
        in_specs=(P("wa", None, None, "grid", None), P(), P(), P("wa", None, "grid", None)),
        out_specs=P("grid", "wa", None, None, None, None),
        check_vma=False,
    )
```

time: 158 us -> 116 us (0.73)
  local copies, waits for them, and re-layouts: 30.3 us -> 5.4 us
  starting transfers between devices: 40.9 us -> 28.5 us
  Pallas kernels: 33.7 us -> 28.7 us
  waiting for transfers between devices: 41.2 us -> 45.9 us
  other arithmetic: 9.91 us -> 6.69 us
    unnamed x46 -> x28, local copies, waits for them, and re-layouts: 21.3 us -> 0.84 us
    ppermute x25 -> x20, starting transfers between devices: 40.9 us -> 28.5 us  [exchange(): return lax.ppermute(value, ('wa', 'grid'), perm)]
    slice x11 -> x9, local copies, waits for them, and re-layouts: 6.92 us -> 0.5 us  [the longest x2 0.17 us: send(): next_blocks[half][:, members]]
    pallas_call x3 -> x2, Pallas kernels: 30.8 us -> 25.9 us  [transform(): pl.pallas_call(kernel, out_shape=jax.ShapeDtypeStruct((ROWS, PLANES, RUN,...]
    ppermute x25 -> x20, waiting for transfers between devices: 41.2 us -> 45.9 us  [exchange(): return lax.ppermute(value, ('wa', 'grid'), perm)]
    concatenate x10 -> x4, other arithmetic: 6.01 us -> 2.48 us  [send(): jnp.concatenate([near[half][:, members], next_blocks[half][:, members]], 0)]
  transfers between devices with their start and end apart: 25 -> 20, of which waited for: 12 -> 15; matrix products, arithmetic and copies ran while one was open for 11% -> 8% of each run, Pallas kernels for 13% -> 9%
where the time goes in v4:
time: 116 us
  waiting for transfers between devices  45.9 us (40%)
  Pallas kernels  28.7 us (25%)
  starting transfers between devices  28.5 us (25%)
  other arithmetic  6.69 us (6%)
  local copies, waits for them, and re-layouts  5.4 us (5%)
    ppermute x20, waiting for transfers between devices, exchange(): return lax.ppermute(value, ('wa', 'grid'), perm)  45.9 us
    ppermute x20, starting transfers between devices, exchange(): return lax.ppermute(value, ('wa', 'grid'), perm)  28.5 us
    pallas_call x2, Pallas kernels, transform(): pl.pallas_call(kernel, out_shape=jax.ShapeDtypeStruct((ROWS, PLANES, RUN,...  25.9 us
    pallas_call x1, Pallas kernels, pick(): pl.pallas_call(pick_kernel, out_shape=(shape, shape), in_specs=[scalars,...  2.8 us
    concatenate x4, other arithmetic, send(): jnp.concatenate([near[half][:, members], next_blocks[half][:, members]], 0)  2.48 us
  transfers between devices with their start and end apart: 20, of which 15 were waited for; matrix products, arithmetic and copies ran while one was open for 8% of the time, Pallas kernels for 9%

profile of v4, /device:TPU:1, one launch (start us, length us, event | category | flops | bytes accessed | tf_op | source)
XLA Modules:
  0.0 115.7 jit_solution(10911414220656227337)
XLA Ops:
  0.7 2.8 %pick.1 = (bf16[3,4,32,512]{3,2,1,0:T(8,128)(2,1)}, bf16[3,4,32,512]{3,2,1,0:T(8,128)(2,1)}) custom-call(s32[2]{0:T(128)} %pad_add_fusion.ids.refs_0_, s32[32]{0:T(128)} %owner.1, bf16[4,4,2,32,512]{4,3,2,1,0:T(8,128)(2,1)} %jones.1), custom_call_target="tpu_custom_call" | custom-call | tf_op jit(solution)/shard_map/pick/pallas_call | solution.py:84
  3.5 1.5 %collective-permute-start = (bf16[3,4,32,512]{3,2,1,0:T(8,128)(2,1)}, bf16[3,4,32,512]{3,2,1,0:T(8,128)(2,1)S(1)}, u32[]{:S(2)}, u32[]{:S(2)}) collective-permute-start(bf16[3,4,32,512]{3,2,1,0:T(8,128)(2,1)} %get-tuple-element.35), channel_id=1, source_target_pairs={{0,16},{1,17},{2,18},{3,19},{4,20},{5,21},{6,22},{7,23},{8,24},{9,... | collective-permute-start | bytes 1179656 | tf_op jit(solution)/shard_map/ppermute | solution.py:46
  7.6 3.9 %collective-permute-start.1 = (bf16[3,4,32,512]{3,2,1,0:T(8,128)(2,1)S(1)}, bf16[3,4,32,512]{3,2,1,0:T(8,128)(2,1)S(1)}, u32[]{:S(2)}, u32[]{:S(2)}) collective-permute-start(bf16[3,4,32,512]{3,2,1,0:T(8,128)(2,1)S(1)} %broadcast_select_fusion), channel_id=1, source_target_pairs={{0,32},{1,33},{2,34},{3,35},{4,36},{5,37},{6,38},{7,39},{8,40},{9,... | collective-permute-start | bytes 1179656 | tf_op jit(solution)/shard_map/ppermute | solution.py:46
  13.3 3.4 %collective-permute-done.1 = bf16[3,4,32,512]{3,2,1,0:T(8,128)(2,1)S(1)} collective-permute-done((bf16[3,4,32,512]{3,2,1,0:T(8,128)(2,1)S(1)}, bf16[3,4,32,512]{3,2,1,0:T(8,128)(2,1)S(1)}, u32[]{:S(2)}, u32[]{:S(2)}) %collective-permute-start.1) | collective-permute-done | bytes 393248 | tf_op jit(solution)/shard_map/ppermute | solution.py:46
  16.9 1.3 %reshape.28.refs_1_ = s32[48]{0:T(128)} reshape(s32[3,4,4]{2,1,0:T(4,128)} %param.6) | data formatting | bytes 384 | tf_op jit(solution)/shard_map/reshape | solution.py:260
  20.5 3.4 %collective-permute-done.2 = bf16[3,4,32,512]{3,2,1,0:T(8,128)(2,1)S(1)} collective-permute-done((bf16[3,4,32,512]{3,2,1,0:T(8,128)(2,1)S(1)}, bf16[3,4,32,512]{3,2,1,0:T(8,128)(2,1)S(1)}, u32[]{:S(2)}, u32[]{:S(2)}) %collective-permute-start.2) | collective-permute-done | bytes 393248 | tf_op jit(solution)/shard_map/ppermute | solution.py:46
  24.1 3.0 %collective-permute-start.5 = (bf16[2,4,2,32,512]{4,3,2,1,0:T(8,128)(2,1)S(1)}, bf16[2,4,2,32,512]{4,3,2,1,0:T(8,128)(2,1)S(1)}, u32[]{:S(2)}, u32[]{:S(2)}) collective-permute-start(bf16[2,4,2,32,512]{4,3,2,1,0:T(8,128)(2,1)S(1)} %pad_maximum_fusion.6), channel_id=1, source_target_pairs={{0,2},{1,3},{2,0},{3,1},{4,6},{5,7},{6,4},{7,5},{8,10},{9,11},{10,... | collective-permute-start | bytes 1572872 | tf_op jit(solution)/shard_map/ppermute | solution.py:46
  27.9 6.2 %collective-permute-done.5 = bf16[2,4,2,32,512]{4,3,2,1,0:T(8,128)(2,1)S(1)} collective-permute-done((bf16[2,4,2,32,512]{4,3,2,1,0:T(8,128)(2,1)S(1)}, bf16[2,4,2,32,512]{4,3,2,1,0:T(8,128)(2,1)S(1)}, u32[]{:S(2)}, u32[]{:S(2)}) %collective-permute-start.5) | collective-permute-done | bytes 524320 | tf_op jit(solution)/shard_map/ppermute | solution.py:46
  34.1 5.6 %collective-permute-done.4 = bf16[2,4,2,32,512]{4,3,2,1,0:T(8,128)(2,1)S(1)} collective-permute-done((bf16[2,4,2,32,512]{4,3,2,1,0:T(8,128)(2,1)S(1)}, bf16[2,4,2,32,512]{4,3,2,1,0:T(8,128)(2,1)S(1)}, u32[]{:S(2)}, u32[]{:S(2)}) %collective-permute-start.4) | collective-permute-done | bytes 524320 | tf_op jit(solution)/shard_map/ppermute | solution.py:46
  40.3 1.3 %collective-permute-start.6 = (bf16[4,4,2,32,512]{4,3,2,1,0:T(8,128)(2,1)S(1)}, bf16[4,4,2,32,512]{4,3,2,1,0:T(8,128)(2,1)S(1)}, u32[]{:S(2)}, u32[]{:S(2)}) collective-permute-start(bf16[4,4,2,32,512]{4,3,2,1,0:T(8,128)(2,1)S(1)} %pad_maximum_fusion.refs_3_), channel_id=1, source_target_pairs={{0,4},{1,5},{2,6},{3,7},{4,0},{5,1},{6,2},{7,3},{8,12},{9,13},{10,... | collective-permute-start | bytes 3145736 | tf_op jit(solution)/shard_map/ppermute | solution.py:46
  41.7 1.9 %collective-permute-start.7 = (bf16[4,4,2,32,512]{4,3,2,1,0:T(8,128)(2,1)S(1)}, bf16[4,4,2,32,512]{4,3,2,1,0:T(8,128)(2,1)S(1)}, u32[]{:S(2)}, u32[]{:S(2)}) collective-permute-start(bf16[4,4,2,32,512]{4,3,2,1,0:T(8,128)(2,1)S(1)} %pad_maximum_fusion.1.refs_4_), channel_id=1, source_target_pairs={{0,12},{1,13},{2,14},{3,15},{4,8},{5,9},{6,10},{7,11},{8,4},{9,5},... | collective-permute-start | bytes 3145736 | tf_op jit(solution)/shard_map/ppermute | solution.py:46
  43.6 3.7 %collective-permute-start.10 = (bf16[4,4,2,32,512]{4,3,2,1,0:T(8,128)(2,1)S(1)}, bf16[4,4,2,32,512]{4,3,2,1,0:T(8,128)(2,1)S(1)}, u32[]{:S(2)}, u32[]{:S(2)}) collective-permute-start(bf16[4,4,2,32,512]{4,3,2,1,0:T(8,128)(2,1)S(1)} %pad_maximum_fusion.refs_3_), channel_id=1, source_target_pairs={{0,16},{1,17},{2,18},{3,19},{4,20},{5,21},{6,22},{7,23},{8,24},{9,... | collective-permute-start | bytes 3145736 | tf_op jit(solution)/shard_map/ppermute | solution.py:46
  47.5 6.8 %collective-permute-done.6.refs_5_ = bf16[4,4,2,32,512]{4,3,2,1,0:T(8,128)(2,1)S(1)} collective-permute-done((bf16[4,4,2,32,512]{4,3,2,1,0:T(8,128)(2,1)S(1)}, bf16[4,4,2,32,512]{4,3,2,1,0:T(8,128)(2,1)S(1)}, u32[]{:S(2)}, u32[]{:S(2)}) %collective-permute-start.6) | collective-permute-done | bytes 1048608 | tf_op jit(solution)/shard_map/ppermute | solution.py:46
  54.3 2.6 %collective-permute-done.7.refs_6_ = bf16[4,4,2,32,512]{4,3,2,1,0:T(8,128)(2,1)S(1)} collective-permute-done((bf16[4,4,2,32,512]{4,3,2,1,0:T(8,128)(2,1)S(1)}, bf16[4,4,2,32,512]{4,3,2,1,0:T(8,128)(2,1)S(1)}, u32[]{:S(2)}, u32[]{:S(2)}) %collective-permute-start.7) | collective-permute-done | bytes 1048608 | tf_op jit(solution)/shard_map/ppermute | solution.py:46
  57.3 4.0 %collective-permute-start.12 = (bf16[4,4,2,32,512]{4,3,2,1,0:T(8,128)(2,1)S(1)}, bf16[4,4,2,32,512]{4,3,2,1,0:T(8,128)(2,1)S(1)}, u32[]{:S(2)}, u32[]{:S(2)}) collective-permute-start(bf16[4,4,2,32,512]{4,3,2,1,0:T(8,128)(2,1)S(1)} %collective-permute-done.6.refs_5_), channel_id=1, source_target_pairs={{0,16},{1,17},{2,18},{3,19},{4,20},{5,21},{6,22},{7,23},{8,24},{9,... | collective-permute-start | bytes 3145736 | tf_op jit(solution)/shard_map/ppermute | solution.py:46
  61.5 2.4 %collective-permute-start.8 = (bf16[8,2,2,32,512]{4,3,2,1,0:T(8,128)(2,1)S(1)}, bf16[8,2,2,32,512]{4,3,2,1,0:T(8,128)(2,1)S(1)}, u32[]{:S(2)}, u32[]{:S(2)}) collective-permute-start(bf16[8,2,2,32,512]{4,3,2,1,0:T(8,128)(2,1)S(1)} %pad_maximum_fusion.2), channel_id=1, source_target_pairs={{0,12},{1,13},{2,14},{3,15},{4,8},{5,9},{6,10},{7,11},{8,4},{9,5},... | collective-permute-start | bytes 3145736 | tf_op jit(solution)/shard_map/ppermute | solution.py:46
  66.4 4.8 %collective-permute-done.9.refs_12_.refs_16_ = bf16[8,2,2,32,512]{4,3,2,1,0:T(8,128)(2,1)S(1)} collective-permute-done((bf16[8,2,2,32,512]{4,3,2,1,0:T(8,128)(2,1)S(1)}, bf16[8,2,2,32,512]{4,3,2,1,0:T(8,128)(2,1)S(1)}, u32[]{:S(2)}, u32[]{:S(2)}) %collective-permute-start.9) | collective-permute-done | bytes 1048608 | tf_op jit(solution)/shard_map/ppermute | solution.py:46
  71.2 5.5 %collective-permute-done.8.refs_11_.refs_15_ = bf16[8,2,2,32,512]{4,3,2,1,0:T(8,128)(2,1)S(1)} collective-permute-done((bf16[8,2,2,32,512]{4,3,2,1,0:T(8,128)(2,1)S(1)}, bf16[8,2,2,32,512]{4,3,2,1,0:T(8,128)(2,1)S(1)}, u32[]{:S(2)}, u32[]{:S(2)}) %collective-permute-start.8) | collective-permute-done | bytes 1048608 | tf_op jit(solution)/shard_map/ppermute | solution.py:46
  76.7 2.4 %collective-permute-start.14 = (bf16[8,2,2,32,512]{4,3,2,1,0:T(8,128)(2,1)}, bf16[8,2,2,32,512]{4,3,2,1,0:T(8,128)(2,1)S(1)}, u32[]{:S(2)}, u32[]{:S(2)}) collective-permute-start(bf16[8,2,2,32,512]{4,3,2,1,0:T(8,128)(2,1)} %pad_maximum_fusion.4), channel_id=1, source_target_pairs={{0,12},{1,13},{2,14},{3,15},{4,8},{5,9},{6,10},{7,11},{8,4},{9,5},... | collective-permute-start | bytes 3145736 | tf_op jit(solution)/shard_map/ppermute | solution.py:46
  80.6 1.4 %collective-permute-done.17.refs_14_ = bf16[8,1,2,32,512]{4,3,2,1,0:T(8,128)(2,1)S(1)} collective-permute-done((bf16[8,1,2,32,512]{4,3,2,1,0:T(8,128)(2,1)S(1)}, bf16[8,1,2,32,512]{4,3,2,1,0:T(8,128)(2,1)S(1)}, u32[]{:S(2)}, u32[]{:S(2)}) %collective-permute-start.17) | collective-permute-done | bytes 524320 | tf_op jit(solution)/shard_map/ppermute | solution.py:46
  82.9 10.3 %transform.2.refs_17_ = bf16[32,2,3,16,2,512]{5,4,3,2,1,0:T(2,128)(2,1)} custom-call(s32[2]{0:T(128)} %pad_add_fusion.ids.refs_0_, s32[48]{0:T(128)} %reshape.28.refs_1_, bf16[256,512]{1,0:T(8,128)(2,1)} %bitcast.17, bf16[4,4,2,32,512]{4,3,2,1,0:T(8,128)(2,1)} %copy-done, bf16[4,4,2,32,512]{4,3,2,1,0:T(8,128)(2,1)} %copy-done.1, ...), custom_call_target="tpu_custom_call" | custom-call | flops 1000000 | bytes 1000000 | tf_op jit(solution)/shard_map/transform/pallas_call | solution.py:215
  93.3 1.9 %collective-permute-start.18 = (bf16[8,2,2,32,512]{4,3,2,1,0:T(8,128)(2,1)S(1)}, bf16[8,2,2,32,512]{4,3,2,1,0:T(8,128)(2,1)S(1)}, u32[]{:S(2)}, u32[]{:S(2)}) collective-permute-start(bf16[8,2,2,32,512]{4,3,2,1,0:T(8,128)(2,1)S(1)} %collective-permute-done.14.refs_11_), channel_id=1, source_target_pairs={{0,16},{1,17},{2,18},{3,19},{4,20},{5,21},{6,22},{7,23},{8,24},{9,... | collective-permute-start | bytes 3145736 | tf_op jit(solution)/shard_map/ppermute | solution.py:46
  95.2 3.7 %collective-permute-done.18.refs_13_ = bf16[8,2,2,32,512]{4,3,2,1,0:T(8,128)(2,1)S(1)} collective-permute-done((bf16[8,2,2,32,512]{4,3,2,1,0:T(8,128)(2,1)S(1)}, bf16[8,2,2,32,512]{4,3,2,1,0:T(8,128)(2,1)S(1)}, u32[]{:S(2)}, u32[]{:S(2)}) %collective-permute-start.18) | collective-permute-done | bytes 1048608 | tf_op jit(solution)/shard_map/ppermute | solution.py:46
  99.9 15.6 %transform.3 = bf16[32,2,3,16,2,512]{5,4,3,2,1,0:T(2,128)(2,1)} custom-call(s32[2]{0:T(128)} %pad_add_fusion.ids.refs_0_, s32[48]{0:T(128)} %reshape.28.refs_1_, bf16[256,512]{1,0:T(8,128)(2,1)} %bitcast.18, bf16[4,4,2,32,512]{4,3,2,1,0:T(8,128)(2,1)} %copy-done, bf16[4,4,2,32,512]{4,3,2,1,0:T(8,128)(2,1)} %copy-done.1, ...), custom_call_target="tpu_custom_call", output_to_operand_aliasing={{}: (17, {})} | custom-call | flops 1000000 | bytes 1000000 | tf_op jit(solution)/shard_map/transform/pallas_call | solution.py:215
  (80 shorter events, 15.6 us)
Async XLA Ops:
  3.5 3.1 %collective-permute-start = (bf16[3,4,32,512]{3,2,1,0:T(8,128)(2,1)}, bf16[3,4,32,512]{3,2,1,0:T(8,128)(2,1)S(1)}, u32[]{:S(2)}, u32[]{:S(2)}) collective-permute-start(bf16[3,4,32,512]{3,2,1,0:T(8,128)(2,1)} %get-tuple-element.35), channel_id=1, source_target_pairs={{0,16},{1,17},{2,18},{3,19},{4,20},{5,21},{6,22},{7,23},{8,24},{9,... | collective-permute-start | bytes 1179656 | tf_op jit(solution)/shard_map/ppermute | solution.py:46
  7.6 9.1 %collective-permute-start.1 = (bf16[3,4,32,512]{3,2,1,0:T(8,128)(2,1)S(1)}, bf16[3,4,32,512]{3,2,1,0:T(8,128)(2,1)S(1)}, u32[]{:S(2)}, u32[]{:S(2)}) collective-permute-start(bf16[3,4,32,512]{3,2,1,0:T(8,128)(2,1)S(1)} %broadcast_select_fusion), channel_id=1, source_target_pairs={{0,32},{1,33},{2,34},{3,35},{4,36},{5,37},{6,38},{7,39},{8,40},{9,... | collective-permute-start | bytes 1179656 | tf_op jit(solution)/shard_map/ppermute | solution.py:46
  16.8 7.0 %collective-permute-start.2 = (bf16[3,4,32,512]{3,2,1,0:T(8,128)(2,1)S(1)}, bf16[3,4,32,512]{3,2,1,0:T(8,128)(2,1)S(1)}, u32[]{:S(2)}, u32[]{:S(2)}) collective-permute-start(bf16[3,4,32,512]{3,2,1,0:T(8,128)(2,1)S(1)} %broadcast_select_fusion.1), channel_id=1, source_target_pairs={{0,96},{1,97},{2,98},{3,99},{4,100},{5,101},{6,102},{7,103},{8,104... | collective-permute-start | bytes 1179656 | tf_op jit(solution)/shard_map/ppermute | solution.py:46
  24.1 10.0 %collective-permute-start.5 = (bf16[2,4,2,32,512]{4,3,2,1,0:T(8,128)(2,1)S(1)}, bf16[2,4,2,32,512]{4,3,2,1,0:T(8,128)(2,1)S(1)}, u32[]{:S(2)}, u32[]{:S(2)}) collective-permute-start(bf16[2,4,2,32,512]{4,3,2,1,0:T(8,128)(2,1)S(1)} %pad_maximum_fusion.6), channel_id=1, source_target_pairs={{0,2},{1,3},{2,0},{3,1},{4,6},{5,7},{6,4},{7,5},{8,10},{9,11},{10,... | collective-permute-start | bytes 1572872 | tf_op jit(solution)/shard_map/ppermute | solution.py:46
  27.1 12.5 %collective-permute-start.4 = (bf16[2,4,2,32,512]{4,3,2,1,0:T(8,128)(2,1)S(1)}, bf16[2,4,2,32,512]{4,3,2,1,0:T(8,128)(2,1)S(1)}, u32[]{:S(2)}, u32[]{:S(2)}) collective-permute-start(bf16[2,4,2,32,512]{4,3,2,1,0:T(8,128)(2,1)S(1)} %pad_maximum_fusion.6), channel_id=1, source_target_pairs={{0,3},{1,2},{2,1},{3,0},{4,7},{5,6},{6,5},{7,4},{8,11},{9,10},{10,... | collective-permute-start | bytes 1572872 | tf_op jit(solution)/shard_map/ppermute | solution.py:46
  27.9 12.1 %collective-permute-start.3 = (bf16[2,4,2,32,512]{4,3,2,1,0:T(8,128)(2,1)S(1)}, bf16[2,4,2,32,512]{4,3,2,1,0:T(8,128)(2,1)S(1)}, u32[]{:S(2)}, u32[]{:S(2)}) collective-permute-start(bf16[2,4,2,32,512]{4,3,2,1,0:T(8,128)(2,1)S(1)} %pad_maximum_fusion.6), channel_id=1, source_target_pairs={{0,1},{1,0},{2,3},{3,2},{4,5},{5,4},{6,7},{7,6},{8,9},{9,8},{10,11... | collective-permute-start | bytes 1572872 | tf_op jit(solution)/shard_map/ppermute | solution.py:46
  40.3 21.1 %copy-start = (bf16[4,4,2,32,512]{4,3,2,1,0:T(8,128)(2,1)}, bf16[4,4,2,32,512]{4,3,2,1,0:T(8,128)(2,1)S(1)}, u32[]{:S(2)}) copy-start(bf16[4,4,2,32,512]{4,3,2,1,0:T(8,128)(2,1)S(1)} %pad_maximum_fusion.refs_3_) | copy-start | bytes 3145732
  40.3 14.0 %collective-permute-start.6 = (bf16[4,4,2,32,512]{4,3,2,1,0:T(8,128)(2,1)S(1)}, bf16[4,4,2,32,512]{4,3,2,1,0:T(8,128)(2,1)S(1)}, u32[]{:S(2)}, u32[]{:S(2)}) collective-permute-start(bf16[4,4,2,32,512]{4,3,2,1,0:T(8,128)(2,1)S(1)} %pad_maximum_fusion.refs_3_), channel_id=1, source_target_pairs={{0,4},{1,5},{2,6},{3,7},{4,0},{5,1},{6,2},{7,3},{8,12},{9,13},{10,... | collective-permute-start | bytes 3145736 | tf_op jit(solution)/shard_map/ppermute | solution.py:46
  41.7 19.7 %copy-start.1 = (bf16[4,4,2,32,512]{4,3,2,1,0:T(8,128)(2,1)}, bf16[4,4,2,32,512]{4,3,2,1,0:T(8,128)(2,1)S(1)}, u32[]{:S(2)}) copy-start(bf16[4,4,2,32,512]{4,3,2,1,0:T(8,128)(2,1)S(1)} %pad_maximum_fusion.1.refs_4_) | copy-start | bytes 3145732
  41.7 15.2 %collective-permute-start.7 = (bf16[4,4,2,32,512]{4,3,2,1,0:T(8,128)(2,1)S(1)}, bf16[4,4,2,32,512]{4,3,2,1,0:T(8,128)(2,1)S(1)}, u32[]{:S(2)}, u32[]{:S(2)}) collective-permute-start(bf16[4,4,2,32,512]{4,3,2,1,0:T(8,128)(2,1)S(1)} %pad_maximum_fusion.1.refs_4_), channel_id=1, source_target_pairs={{0,12},{1,13},{2,14},{3,15},{4,8},{5,9},{6,10},{7,11},{8,4},{9,5},... | collective-permute-start | bytes 3145736 | tf_op jit(solution)/shard_map/ppermute | solution.py:46
  43.6 20.3 %collective-permute-start.10 = (bf16[4,4,2,32,512]{4,3,2,1,0:T(8,128)(2,1)S(1)}, bf16[4,4,2,32,512]{4,3,2,1,0:T(8,128)(2,1)S(1)}, u32[]{:S(2)}, u32[]{:S(2)}) collective-permute-start(bf16[4,4,2,32,512]{4,3,2,1,0:T(8,128)(2,1)S(1)} %pad_maximum_fusion.refs_3_), channel_id=1, source_target_pairs={{0,16},{1,17},{2,18},{3,19},{4,20},{5,21},{6,22},{7,23},{8,24},{9,... | collective-permute-start | bytes 3145736 | tf_op jit(solution)/shard_map/ppermute | solution.py:46
  47.4 19.0 %collective-permute-start.11 = (bf16[4,4,2,32,512]{4,3,2,1,0:T(8,128)(2,1)S(1)}, bf16[4,4,2,32,512]{4,3,2,1,0:T(8,128)(2,1)S(1)}, u32[]{:S(2)}, u32[]{:S(2)}) collective-permute-start(bf16[4,4,2,32,512]{4,3,2,1,0:T(8,128)(2,1)S(1)} %pad_maximum_fusion.1.refs_4_), channel_id=1, source_target_pairs={{0,16},{1,17},{2,18},{3,19},{4,20},{5,21},{6,22},{7,23},{8,24},{9,... | collective-permute-start | bytes 3145736 | tf_op jit(solution)/shard_map/ppermute | solution.py:46
  57.2 14.0 %collective-permute-start.9 = (bf16[8,2,2,32,512]{4,3,2,1,0:T(8,128)(2,1)S(1)}, bf16[8,2,2,32,512]{4,3,2,1,0:T(8,128)(2,1)S(1)}, u32[]{:S(2)}, u32[]{:S(2)}) collective-permute-start(bf16[8,2,2,32,512]{4,3,2,1,0:T(8,128)(2,1)S(1)} %pad_maximum_fusion.3), channel_id=1, source_target_pairs={{0,4},{1,5},{2,6},{3,7},{4,0},{5,1},{6,2},{7,3},{8,12},{9,13},{10,... | collective-permute-start | bytes 3145736 | tf_op jit(solution)/shard_map/ppermute | solution.py:46
  57.3 19.4 %collective-permute-start.12 = (bf16[4,4,2,32,512]{4,3,2,1,0:T(8,128)(2,1)S(1)}, bf16[4,4,2,32,512]{4,3,2,1,0:T(8,128)(2,1)S(1)}, u32[]{:S(2)}, u32[]{:S(2)}) collective-permute-start(bf16[4,4,2,32,512]{4,3,2,1,0:T(8,128)(2,1)S(1)} %collective-permute-done.6.refs_5_), channel_id=1, source_target_pairs={{0,16},{1,17},{2,18},{3,19},{4,20},{5,21},{6,22},{7,23},{8,24},{9,... | collective-permute-start | bytes 3145736 | tf_op jit(solution)/shard_map/ppermute | solution.py:46
  61.5 15.2 %collective-permute-start.8 = (bf16[8,2,2,32,512]{4,3,2,1,0:T(8,128)(2,1)S(1)}, bf16[8,2,2,32,512]{4,3,2,1,0:T(8,128)(2,1)S(1)}, u32[]{:S(2)}, u32[]{:S(2)}) collective-permute-start(bf16[8,2,2,32,512]{4,3,2,1,0:T(8,128)(2,1)S(1)} %pad_maximum_fusion.2), channel_id=1, source_target_pairs={{0,12},{1,13},{2,14},{3,15},{4,8},{5,9},{6,10},{7,11},{8,4},{9,5},... | collective-permute-start | bytes 3145736 | tf_op jit(solution)/shard_map/ppermute | solution.py:46
  63.9 16.6 %copy-start.6 = (bf16[4,4,2,32,512]{4,3,2,1,0:T(8,128)(2,1)}, bf16[4,4,2,32,512]{4,3,2,1,0:T(8,128)(2,1)S(1)}, u32[]{:S(2)}) copy-start(bf16[4,4,2,32,512]{4,3,2,1,0:T(8,128)(2,1)S(1)} %collective-permute-done.10.refs_7_) | copy-start | bytes 3145732
  63.9 12.8 %collective-permute-start.13 = (bf16[4,4,2,32,512]{4,3,2,1,0:T(8,128)(2,1)S(1)}, bf16[4,4,2,32,512]{4,3,2,1,0:T(8,128)(2,1)S(1)}, u32[]{:S(2)}, u32[]{:S(2)}) collective-permute-start(bf16[4,4,2,32,512]{4,3,2,1,0:T(8,128)(2,1)S(1)} %collective-permute-done.7.refs_6_), channel_id=1, source_target_pairs={{0,16},{1,17},{2,18},{3,19},{4,20},{5,21},{6,22},{7,23},{8,24},{9,... | collective-permute-start | bytes 3145736 | tf_op jit(solution)/shard_map/ppermute | solution.py:46
  66.4 14.2 %copy-start.7 = (bf16[4,4,2,32,512]{4,3,2,1,0:T(8,128)(2,1)}, bf16[4,4,2,32,512]{4,3,2,1,0:T(8,128)(2,1)S(1)}, u32[]{:S(2)}) copy-start(bf16[4,4,2,32,512]{4,3,2,1,0:T(8,128)(2,1)S(1)} %collective-permute-done.11.refs_8_) | copy-start | bytes 3145732
  76.7 16.5 %collective-permute-start.14 = (bf16[8,2,2,32,512]{4,3,2,1,0:T(8,128)(2,1)}, bf16[8,2,2,32,512]{4,3,2,1,0:T(8,128)(2,1)S(1)}, u32[]{:S(2)}, u32[]{:S(2)}) collective-permute-start(bf16[8,2,2,32,512]{4,3,2,1,0:T(8,128)(2,1)} %pad_maximum_fusion.4), channel_id=1, source_target_pairs={{0,12},{1,13},{2,14},{3,15},{4,8},{5,9},{6,10},{7,11},{8,4},{9,5},... | collective-permute-start | bytes 3145736 | tf_op jit(solution)/shard_map/ppermute | solution.py:46
  79.2 14.2 %collective-permute-start.15 = (bf16[8,2,2,32,512]{4,3,2,1,0:T(8,128)(2,1)}, bf16[8,2,2,32,512]{4,3,2,1,0:T(8,128)(2,1)S(1)}, u32[]{:S(2)}, u32[]{:S(2)}) collective-permute-start(bf16[8,2,2,32,512]{4,3,2,1,0:T(8,128)(2,1)} %pad_maximum_fusion.5), channel_id=1, source_target_pairs={{0,4},{1,5},{2,6},{3,7},{4,0},{5,1},{6,2},{7,3},{8,12},{9,13},{10,... | collective-permute-start | bytes 3145736 | tf_op jit(solution)/shard_map/ppermute | solution.py:46
  79.3 2.7 %collective-permute-start.17 = (bf16[8,1,2,32,512]{4,3,2,1,0:T(8,128)(2,1)S(1)}, bf16[8,1,2,32,512]{4,3,2,1,0:T(8,128)(2,1)S(1)}, u32[]{:S(2)}, u32[]{:S(2)}) collective-permute-start(bf16[8,1,2,32,512]{4,3,2,1,0:T(8,128)(2,1)S(1)} %slice.105), channel_id=1, source_target_pairs={{0,16},{1,17},{2,18},{3,19},{4,20},{5,21},{6,22},{7,23},{8,24},{9,... | collective-permute-start | bytes 1572872 | tf_op jit(solution)/shard_map/ppermute | solution.py:46
  80.5 2.4 %collective-permute-start.16 = (bf16[8,1,2,32,512]{4,3,2,1,0:T(8,128)(2,1)S(1)}, bf16[8,1,2,32,512]{4,3,2,1,0:T(8,128)(2,1)}, u32[]{:S(2)}, u32[]{:S(2)}) collective-permute-start(bf16[8,1,2,32,512]{4,3,2,1,0:T(8,128)(2,1)S(1)} %slice.104), channel_id=1, source_target_pairs={{0,16},{1,17},{2,18},{3,19},{4,20},{5,21},{6,22},{7,23},{8,24},{9,... | collective-permute-start | bytes 1572872 | tf_op jit(solution)/shard_map/ppermute | solution.py:46
  93.3 5.6 %collective-permute-start.18 = (bf16[8,2,2,32,512]{4,3,2,1,0:T(8,128)(2,1)S(1)}, bf16[8,2,2,32,512]{4,3,2,1,0:T(8,128)(2,1)S(1)}, u32[]{:S(2)}, u32[]{:S(2)}) collective-permute-start(bf16[8,2,2,32,512]{4,3,2,1,0:T(8,128)(2,1)S(1)} %collective-permute-done.14.refs_11_), channel_id=1, source_target_pairs={{0,16},{1,17},{2,18},{3,19},{4,20},{5,21},{6,22},{7,23},{8,24},{9,... | collective-permute-start | bytes 3145736 | tf_op jit(solution)/shard_map/ppermute | solution.py:46
  95.2 3.9 %collective-permute-start.19 = (bf16[8,2,2,32,512]{4,3,2,1,0:T(8,128)(2,1)S(1)}, bf16[8,2,2,32,512]{4,3,2,1,0:T(8,128)(2,1)}, u32[]{:S(2)}, u32[]{:S(2)}) collective-permute-start(bf16[8,2,2,32,512]{4,3,2,1,0:T(8,128)(2,1)S(1)} %collective-permute-done.15.refs_12_), channel_id=1, source_target_pairs={{0,16},{1,17},{2,18},{3,19},{4,20},{5,21},{6,22},{7,23},{8,24},{9,... | collective-permute-start | bytes 3145736 | tf_op jit(solution)/shard_map/ppermute | solution.py:46
  (10 other events, 57.0 us)

commit v5 on v4

--- a/solution.py
+++ b/solution.py
@@ -63,8 +63,8 @@
     return exchange(value, lambda core: 0, lambda core: masks[core])
 
 
-def pick_kernel(ids, owner, jones, mine, other, semaphore):
-    core = ids[0]
+def pick_kernel(owner, jones, mine, other, semaphore):
+    core = lax.axis_index("wa") & 1
     copies = []
     for index in range(RUN):
         slot = owner[index] & 3
@@ -78,18 +78,18 @@
         copy.wait()
 
 
-def pick(ids, owner, jones):
+def pick(owner, jones):
     shape = jax.ShapeDtypeStruct((RUN, 4, ROWS, G), jnp.bfloat16)
     scalars = pl.BlockSpec(memory_space=pltpu.SMEM)
     return pl.pallas_call(
         pick_kernel,
         out_shape=(shape, shape),
-        in_specs=[scalars, scalars, pl.BlockSpec(memory_space=pl.ANY)],
+        in_specs=[scalars, pl.BlockSpec(memory_space=pl.ANY)],
         out_specs=(pl.BlockSpec(memory_space=pltpu.VMEM), pl.BlockSpec(memory_space=pltpu.VMEM)),
         scratch_shapes=[pltpu.SemaphoreType.DMA((RUN * 2,))],
-        compiler_params=pltpu.CompilerParams(vmem_limit_bytes=60 * 1024 * 1024),
+        compiler_params=pltpu.CompilerParams(vmem_limit_bytes=61 * 1024 * 1024),
         name="pick",
-    )(ids, owner, jones)
+    )(owner, jones)
 
 
 def transform_kernel(types, *refs):
@@ -251,7 +251,7 @@
     grid = lax.axis_index("grid")
     core = wa & 1
     ids = jnp.stack([core, grid]).astype(jnp.int32)
-    mine, other = pick(ids, owner, jones)
+    mine, other = pick(owner, jones)
 
     kr, ki = w_operator[:, 0], w_operator[:, 1]
     plain = jnp.stack([kr, ki], 2).reshape(PLANES, 2 * ROWS, G)
@@ -283,12 +283,14 @@
 
     last = [swap_grid(one, half, 3) for half, one in enumerate(send(slice(0, 2)))]
     rest = send(slice(2, 4))
-    moved = together((*last, *rest, *near, *next_blocks, *far_near, *far_next))
-    lasts, rest, shared = [moved[:2]], moved[2:4], tuple(moved[4:])
+    others = [swap_grid(one, half, 3) for half, one in enumerate(rest)]
+    moved = together((*last, *near, *next_blocks, *far_near, *far_next))
+    lasts, shared = [moved[:2]], tuple(moved[2:])
     far_last = together([swap_core(last[:, :1]) for last in lasts[0]])
-    lasts.append(together([swap_grid(one, half, 3) for half, one in enumerate(rest)]))
     result = transform((0,), ids, keep, ku, shared, lasts[0], far_last, (), None)
-    far_last = [swap_core(after(last, result)) for last in lasts[1]]
+    *others, result = together((*others, result))
+    lasts.append(others)
+    far_last = [swap_core(last) for last in others]
     result = transform((1, 2), ids, keep, ku, shared, lasts[1], far_last, lasts[0], result)
     return result
 

time: 116 us -> 114 us (0.983)
  waiting for transfers between devices: 45.9 us -> 42.2 us
  local copies, waits for them, and re-layouts: 5.4 us -> 7.3 us
    ppermute x20, waiting for transfers between devices: 45.9 us -> 42.2 us  [exchange(): return lax.ppermute(value, ('wa', 'grid'), perm)]
    unnamed x28 -> x30, local copies, waits for them, and re-layouts: 0.84 us -> 2.71 us
  transfers between devices with their start and end apart: 20 -> 20, of which waited for: 15 -> 14; matrix products, arithmetic and copies ran while one was open for 8% -> 8% of each run, Pallas kernels for 9% -> 9%
where the time goes in v5:
time: 114 us; the launch traced here: 113 us
  waiting for transfers between devices  42.2 us (37%)
  Pallas kernels  28.7 us (25%)
  starting transfers between devices  28 us (25%)
  local copies, waits for them, and re-layouts  7.3 us (6%)
  other arithmetic  6.56 us (6%)
    ppermute x20, waiting for transfers between devices, exchange(): return lax.ppermute(value, ('wa', 'grid'), perm)  42.2 us
    ppermute x20, starting transfers between devices, exchange(): return lax.ppermute(value, ('wa', 'grid'), perm)  28 us
    pallas_call x2, Pallas kernels, transform(): pl.pallas_call(kernel, out_shape=jax.ShapeDtypeStruct((ROWS, PLANES, RUN,...  25.9 us
    pallas_call x1, Pallas kernels, pick(): pl.pallas_call(pick_kernel, out_shape=(shape, shape), in_specs=[scalars,...  2.79 us
    unnamed x30, local copies, waits for them, and re-layouts  2.71 us
    concatenate x4, other arithmetic, send(): jnp.concatenate([near[half][:, members], next_blocks[half][:, members]], 0)  2.45 us
  transfers between devices with their start and end apart: 20, of which 14 were waited for; matrix products, arithmetic and copies ran while one was open for 8% of the time, Pallas kernels for 9%

profile of v5, /device:TPU:1, one launch (start us, length us, event | category | flops | bytes accessed | tf_op | source)
XLA Modules:
  0.0 113.3 jit_solution(15549348399571521058)
XLA Ops:
  0.0 2.8 %pick.1 = (bf16[3,4,32,512]{3,2,1,0:T(8,128)(2,1)}, bf16[3,4,32,512]{3,2,1,0:T(8,128)(2,1)}) custom-call(s32[32]{0:T(128)} %owner.1, bf16[4,4,2,32,512]{4,3,2,1,0:T(8,128)(2,1)} %jones.1), custom_call_target="tpu_custom_call" | custom-call | tf_op jit(solution)/shard_map/pick/pallas_call | solution.py:84
  2.8 1.5 %collective-permute-start = (bf16[3,4,32,512]{3,2,1,0:T(8,128)(2,1)}, bf16[3,4,32,512]{3,2,1,0:T(8,128)(2,1)S(1)}, u32[]{:S(2)}, u32[]{:S(2)}) collective-permute-start(bf16[3,4,32,512]{3,2,1,0:T(8,128)(2,1)} %get-tuple-element.32), channel_id=1, source_target_pairs={{0,16},{1,17},{2,18},{3,19},{4,20},{5,21},{6,22},{7,23},{8,24},{9,... | collective-permute-start | bytes 1179656 | tf_op jit(solution)/shard_map/ppermute | solution.py:46
  7.0 3.9 %collective-permute-start.1 = (bf16[3,4,32,512]{3,2,1,0:T(8,128)(2,1)S(1)}, bf16[3,4,32,512]{3,2,1,0:T(8,128)(2,1)S(1)}, u32[]{:S(2)}, u32[]{:S(2)}) collective-permute-start(bf16[3,4,32,512]{3,2,1,0:T(8,128)(2,1)S(1)} %broadcast_select_fusion), channel_id=1, source_target_pairs={{0,32},{1,33},{2,34},{3,35},{4,36},{5,37},{6,38},{7,39},{8,40},{9,... | collective-permute-start | bytes 1179656 | tf_op jit(solution)/shard_map/ppermute | solution.py:46
  12.9 3.1 %collective-permute-done.1 = bf16[3,4,32,512]{3,2,1,0:T(8,128)(2,1)S(1)} collective-permute-done((bf16[3,4,32,512]{3,2,1,0:T(8,128)(2,1)S(1)}, bf16[3,4,32,512]{3,2,1,0:T(8,128)(2,1)S(1)}, u32[]{:S(2)}, u32[]{:S(2)}) %collective-permute-start.1) | collective-permute-done | bytes 393248 | tf_op jit(solution)/shard_map/ppermute | solution.py:46
  16.6 1.3 %reshape.28.refs_1_ = s32[48]{0:T(128)} reshape(s32[3,4,4]{2,1,0:T(4,128)} %param.6) | data formatting | bytes 384 | tf_op jit(solution)/shard_map/reshape | solution.py:260
  20.1 3.1 %collective-permute-done.2 = bf16[3,4,32,512]{3,2,1,0:T(8,128)(2,1)S(1)} collective-permute-done((bf16[3,4,32,512]{3,2,1,0:T(8,128)(2,1)S(1)}, bf16[3,4,32,512]{3,2,1,0:T(8,128)(2,1)S(1)}, u32[]{:S(2)}, u32[]{:S(2)}) %collective-permute-start.2) | collective-permute-done | bytes 393248 | tf_op jit(solution)/shard_map/ppermute | solution.py:46
  23.4 3.0 %collective-permute-start.5 = (bf16[2,4,2,32,512]{4,3,2,1,0:T(8,128)(2,1)S(1)}, bf16[2,4,2,32,512]{4,3,2,1,0:T(8,128)(2,1)S(1)}, u32[]{:S(2)}, u32[]{:S(2)}) collective-permute-start(bf16[2,4,2,32,512]{4,3,2,1,0:T(8,128)(2,1)S(1)} %pad_maximum_fusion.6), channel_id=1, source_target_pairs={{0,2},{1,3},{2,0},{3,1},{4,6},{5,7},{6,4},{7,5},{8,10},{9,11},{10,... | collective-permute-start | bytes 1572872 | tf_op jit(solution)/shard_map/ppermute | solution.py:46
  27.2 6.2 %collective-permute-done.5 = bf16[2,4,2,32,512]{4,3,2,1,0:T(8,128)(2,1)S(1)} collective-permute-done((bf16[2,4,2,32,512]{4,3,2,1,0:T(8,128)(2,1)S(1)}, bf16[2,4,2,32,512]{4,3,2,1,0:T(8,128)(2,1)S(1)}, u32[]{:S(2)}, u32[]{:S(2)}) %collective-permute-start.5) | collective-permute-done | bytes 524320 | tf_op jit(solution)/shard_map/ppermute | solution.py:46
  33.4 5.6 %collective-permute-done.4 = bf16[2,4,2,32,512]{4,3,2,1,0:T(8,128)(2,1)S(1)} collective-permute-done((bf16[2,4,2,32,512]{4,3,2,1,0:T(8,128)(2,1)S(1)}, bf16[2,4,2,32,512]{4,3,2,1,0:T(8,128)(2,1)S(1)}, u32[]{:S(2)}, u32[]{:S(2)}) %collective-permute-start.4) | collective-permute-done | bytes 524320 | tf_op jit(solution)/shard_map/ppermute | solution.py:46
  39.6 1.3 %collective-permute-start.6 = (bf16[4,4,2,32,512]{4,3,2,1,0:T(8,128)(2,1)S(1)}, bf16[4,4,2,32,512]{4,3,2,1,0:T(8,128)(2,1)S(1)}, u32[]{:S(2)}, u32[]{:S(2)}) collective-permute-start(bf16[4,4,2,32,512]{4,3,2,1,0:T(8,128)(2,1)S(1)} %pad_maximum_fusion.refs_3_), channel_id=1, source_target_pairs={{0,4},{1,5},{2,6},{3,7},{4,0},{5,1},{6,2},{7,3},{8,12},{9,13},{10,... | collective-permute-start | bytes 3145736 | tf_op jit(solution)/shard_map/ppermute | solution.py:46
  41.1 1.9 %collective-permute-start.7 = (bf16[4,4,2,32,512]{4,3,2,1,0:T(8,128)(2,1)S(1)}, bf16[4,4,2,32,512]{4,3,2,1,0:T(8,128)(2,1)S(1)}, u32[]{:S(2)}, u32[]{:S(2)}) collective-permute-start(bf16[4,4,2,32,512]{4,3,2,1,0:T(8,128)(2,1)S(1)} %pad_maximum_fusion.1.refs_4_), channel_id=1, source_target_pairs={{0,12},{1,13},{2,14},{3,15},{4,8},{5,9},{6,10},{7,11},{8,4},{9,5},... | collective-permute-start | bytes 3145736 | tf_op jit(solution)/shard_map/ppermute | solution.py:46
  43.0 3.7 %collective-permute-start.10 = (bf16[4,4,2,32,512]{4,3,2,1,0:T(8,128)(2,1)S(1)}, bf16[4,4,2,32,512]{4,3,2,1,0:T(8,128)(2,1)S(1)}, u32[]{:S(2)}, u32[]{:S(2)}) collective-permute-start(bf16[4,4,2,32,512]{4,3,2,1,0:T(8,128)(2,1)S(1)} %pad_maximum_fusion.refs_3_), channel_id=1, source_target_pairs={{0,16},{1,17},{2,18},{3,19},{4,20},{5,21},{6,22},{7,23},{8,24},{9,... | collective-permute-start | bytes 3145736 | tf_op jit(solution)/shard_map/ppermute | solution.py:46
  46.8 6.9 %collective-permute-done.6.refs_5_ = bf16[4,4,2,32,512]{4,3,2,1,0:T(8,128)(2,1)S(1)} collective-permute-done((bf16[4,4,2,32,512]{4,3,2,1,0:T(8,128)(2,1)S(1)}, bf16[4,4,2,32,512]{4,3,2,1,0:T(8,128)(2,1)S(1)}, u32[]{:S(2)}, u32[]{:S(2)}) %collective-permute-start.6) | collective-permute-done | bytes 1048608 | tf_op jit(solution)/shard_map/ppermute | solution.py:46
  53.7 2.6 %collective-permute-done.7.refs_6_ = bf16[4,4,2,32,512]{4,3,2,1,0:T(8,128)(2,1)S(1)} collective-permute-done((bf16[4,4,2,32,512]{4,3,2,1,0:T(8,128)(2,1)S(1)}, bf16[4,4,2,32,512]{4,3,2,1,0:T(8,128)(2,1)S(1)}, u32[]{:S(2)}, u32[]{:S(2)}) %collective-permute-start.7) | collective-permute-done | bytes 1048608 | tf_op jit(solution)/shard_map/ppermute | solution.py:46
  56.7 4.0 %collective-permute-start.12 = (bf16[4,4,2,32,512]{4,3,2,1,0:T(8,128)(2,1)S(1)}, bf16[4,4,2,32,512]{4,3,2,1,0:T(8,128)(2,1)S(1)}, u32[]{:S(2)}, u32[]{:S(2)}) collective-permute-start(bf16[4,4,2,32,512]{4,3,2,1,0:T(8,128)(2,1)S(1)} %collective-permute-done.6.refs_5_), channel_id=1, source_target_pairs={{0,16},{1,17},{2,18},{3,19},{4,20},{5,21},{6,22},{7,23},{8,24},{9,... | collective-permute-start | bytes 3145736 | tf_op jit(solution)/shard_map/ppermute | solution.py:46
  60.9 2.4 %collective-permute-start.8 = (bf16[8,2,2,32,512]{4,3,2,1,0:T(8,128)(2,1)S(1)}, bf16[8,2,2,32,512]{4,3,2,1,0:T(8,128)(2,1)S(1)}, u32[]{:S(2)}, u32[]{:S(2)}) collective-permute-start(bf16[8,2,2,32,512]{4,3,2,1,0:T(8,128)(2,1)S(1)} %pad_maximum_fusion.2), channel_id=1, source_target_pairs={{0,12},{1,13},{2,14},{3,15},{4,8},{5,9},{6,10},{7,11},{8,4},{9,5},... | collective-permute-start | bytes 3145736 | tf_op jit(solution)/shard_map/ppermute | solution.py:46
  66.8 3.8 %collective-permute-done.9.refs_12_.refs_16_ = bf16[8,2,2,32,512]{4,3,2,1,0:T(8,128)(2,1)S(1)} collective-permute-done((bf16[8,2,2,32,512]{4,3,2,1,0:T(8,128)(2,1)S(1)}, bf16[8,2,2,32,512]{4,3,2,1,0:T(8,128)(2,1)S(1)}, u32[]{:S(2)}, u32[]{:S(2)}) %collective-permute-start.9) | collective-permute-done | bytes 1048608 | tf_op jit(solution)/shard_map/ppermute | solution.py:46
  70.5 1.8 %collective-permute-start.14 = (bf16[8,2,2,32,512]{4,3,2,1,0:T(8,128)(2,1)}, bf16[8,2,2,32,512]{4,3,2,1,0:T(8,128)(2,1)}, u32[]{:S(2)}, u32[]{:S(2)}) collective-permute-start(bf16[8,2,2,32,512]{4,3,2,1,0:T(8,128)(2,1)} %pad_maximum_fusion.4), channel_id=1, source_target_pairs={{0,12},{1,13},{2,14},{3,15},{4,8},{5,9},{6,10},{7,11},{8,4},{9,5},... | collective-permute-start | bytes 3145736 | tf_op jit(solution)/shard_map/ppermute | solution.py:46
  72.4 3.8 %collective-permute-done.8.refs_11_.refs_15_ = bf16[8,2,2,32,512]{4,3,2,1,0:T(8,128)(2,1)S(1)} collective-permute-done((bf16[8,2,2,32,512]{4,3,2,1,0:T(8,128)(2,1)S(1)}, bf16[8,2,2,32,512]{4,3,2,1,0:T(8,128)(2,1)S(1)}, u32[]{:S(2)}, u32[]{:S(2)}) %collective-permute-start.8) | collective-permute-done | bytes 1048608 | tf_op jit(solution)/shard_map/ppermute | solution.py:46
  77.1 1.7 %collective-permute-start.17 = (bf16[8,1,2,32,512]{4,3,2,1,0:T(8,128)(2,1)S(1)}, bf16[8,1,2,32,512]{4,3,2,1,0:T(8,128)(2,1)S(1)}, u32[]{:S(2)}, u32[]{:S(2)}) collective-permute-start(bf16[8,1,2,32,512]{4,3,2,1,0:T(8,128)(2,1)S(1)} %slice.105), channel_id=1, source_target_pairs={{0,16},{1,17},{2,18},{3,19},{4,20},{5,21},{6,22},{7,23},{8,24},{9,... | collective-permute-start | bytes 1572872 | tf_op jit(solution)/shard_map/ppermute | solution.py:46
  78.8 1.5 %collective-permute-done.17.refs_14_ = bf16[8,1,2,32,512]{4,3,2,1,0:T(8,128)(2,1)S(1)} collective-permute-done((bf16[8,1,2,32,512]{4,3,2,1,0:T(8,128)(2,1)S(1)}, bf16[8,1,2,32,512]{4,3,2,1,0:T(8,128)(2,1)S(1)}, u32[]{:S(2)}, u32[]{:S(2)}) %collective-permute-start.17) | collective-permute-done | bytes 524320 | tf_op jit(solution)/shard_map/ppermute | solution.py:46
  81.9 10.3 %transform.2.refs_17_ = bf16[32,2,3,16,2,512]{5,4,3,2,1,0:T(2,128)(2,1)} custom-call(s32[2]{0:T(128)} %pad_add_fusion.refs_0_, s32[48]{0:T(128)} %reshape.28.refs_1_, bf16[256,512]{1,0:T(8,128)(2,1)} %bitcast.17, bf16[4,4,2,32,512]{4,3,2,1,0:T(8,128)(2,1)} %copy-done, bf16[4,4,2,32,512]{4,3,2,1,0:T(8,128)(2,1)} %copy-done.1, ...), custom_call_target="tpu_custom_call" | custom-call | flops 1000000 | bytes 1000000 | tf_op jit(solution)/shard_map/transform/pallas_call | solution.py:215
  92.9 2.5 %collective-permute-done.18.refs_13_ = bf16[8,2,2,32,512]{4,3,2,1,0:T(8,128)(2,1)S(1)} collective-permute-done((bf16[8,2,2,32,512]{4,3,2,1,0:T(8,128)(2,1)}, bf16[8,2,2,32,512]{4,3,2,1,0:T(8,128)(2,1)S(1)}, u32[]{:S(2)}, u32[]{:S(2)}) %collective-permute-start.18) | collective-permute-done | bytes 1048608 | tf_op jit(solution)/shard_map/ppermute | solution.py:46
  97.5 15.6 %transform.3 = bf16[32,2,3,16,2,512]{5,4,3,2,1,0:T(2,128)(2,1)} custom-call(s32[2]{0:T(128)} %pad_add_fusion.refs_0_, s32[48]{0:T(128)} %reshape.28.refs_1_, bf16[256,512]{1,0:T(8,128)(2,1)} %bitcast.18, bf16[4,4,2,32,512]{4,3,2,1,0:T(8,128)(2,1)} %copy-done, bf16[4,4,2,32,512]{4,3,2,1,0:T(8,128)(2,1)} %copy-done.1, ...), custom_call_target="tpu_custom_call", output_to_operand_aliasing={{}: (17, {})} | custom-call | flops 1000000 | bytes 1000000 | tf_op jit(solution)/shard_map/transform/pallas_call | solution.py:215
  (82 shorter events, 18.5 us)
Async XLA Ops:
  2.8 3.1 %collective-permute-start = (bf16[3,4,32,512]{3,2,1,0:T(8,128)(2,1)}, bf16[3,4,32,512]{3,2,1,0:T(8,128)(2,1)S(1)}, u32[]{:S(2)}, u32[]{:S(2)}) collective-permute-start(bf16[3,4,32,512]{3,2,1,0:T(8,128)(2,1)} %get-tuple-element.32), channel_id=1, source_target_pairs={{0,16},{1,17},{2,18},{3,19},{4,20},{5,21},{6,22},{7,23},{8,24},{9,... | collective-permute-start | bytes 1179656 | tf_op jit(solution)/shard_map/ppermute | solution.py:46
  7.0 9.1 %collective-permute-start.1 = (bf16[3,4,32,512]{3,2,1,0:T(8,128)(2,1)S(1)}, bf16[3,4,32,512]{3,2,1,0:T(8,128)(2,1)S(1)}, u32[]{:S(2)}, u32[]{:S(2)}) collective-permute-start(bf16[3,4,32,512]{3,2,1,0:T(8,128)(2,1)S(1)} %broadcast_select_fusion), channel_id=1, source_target_pairs={{0,32},{1,33},{2,34},{3,35},{4,36},{5,37},{6,38},{7,39},{8,40},{9,... | collective-permute-start | bytes 1179656 | tf_op jit(solution)/shard_map/ppermute | solution.py:46
  16.2 7.0 %collective-permute-start.2 = (bf16[3,4,32,512]{3,2,1,0:T(8,128)(2,1)S(1)}, bf16[3,4,32,512]{3,2,1,0:T(8,128)(2,1)S(1)}, u32[]{:S(2)}, u32[]{:S(2)}) collective-permute-start(bf16[3,4,32,512]{3,2,1,0:T(8,128)(2,1)S(1)} %broadcast_select_fusion.1), channel_id=1, source_target_pairs={{0,96},{1,97},{2,98},{3,99},{4,100},{5,101},{6,102},{7,103},{8,104... | collective-permute-start | bytes 1179656 | tf_op jit(solution)/shard_map/ppermute | solution.py:46
  23.4 10.0 %collective-permute-start.5 = (bf16[2,4,2,32,512]{4,3,2,1,0:T(8,128)(2,1)S(1)}, bf16[2,4,2,32,512]{4,3,2,1,0:T(8,128)(2,1)S(1)}, u32[]{:S(2)}, u32[]{:S(2)}) collective-permute-start(bf16[2,4,2,32,512]{4,3,2,1,0:T(8,128)(2,1)S(1)} %pad_maximum_fusion.6), channel_id=1, source_target_pairs={{0,2},{1,3},{2,0},{3,1},{4,6},{5,7},{6,4},{7,5},{8,10},{9,11},{10,... | collective-permute-start | bytes 1572872 | tf_op jit(solution)/shard_map/ppermute | solution.py:46
  26.4 12.5 %collective-permute-start.4 = (bf16[2,4,2,32,512]{4,3,2,1,0:T(8,128)(2,1)S(1)}, bf16[2,4,2,32,512]{4,3,2,1,0:T(8,128)(2,1)S(1)}, u32[]{:S(2)}, u32[]{:S(2)}) collective-permute-start(bf16[2,4,2,32,512]{4,3,2,1,0:T(8,128)(2,1)S(1)} %pad_maximum_fusion.6), channel_id=1, source_target_pairs={{0,3},{1,2},{2,1},{3,0},{4,7},{5,6},{6,5},{7,4},{8,11},{9,10},{10,... | collective-permute-start | bytes 1572872 | tf_op jit(solution)/shard_map/ppermute | solution.py:46
  27.2 12.1 %collective-permute-start.3 = (bf16[2,4,2,32,512]{4,3,2,1,0:T(8,128)(2,1)S(1)}, bf16[2,4,2,32,512]{4,3,2,1,0:T(8,128)(2,1)S(1)}, u32[]{:S(2)}, u32[]{:S(2)}) collective-permute-start(bf16[2,4,2,32,512]{4,3,2,1,0:T(8,128)(2,1)S(1)} %pad_maximum_fusion.6), channel_id=1, source_target_pairs={{0,1},{1,0},{2,3},{3,2},{4,5},{5,4},{6,7},{7,6},{8,9},{9,8},{10,11... | collective-permute-start | bytes 1572872 | tf_op jit(solution)/shard_map/ppermute | solution.py:46
  39.6 21.1 %copy-start = (bf16[4,4,2,32,512]{4,3,2,1,0:T(8,128)(2,1)}, bf16[4,4,2,32,512]{4,3,2,1,0:T(8,128)(2,1)S(1)}, u32[]{:S(2)}) copy-start(bf16[4,4,2,32,512]{4,3,2,1,0:T(8,128)(2,1)S(1)} %pad_maximum_fusion.refs_3_) | copy-start | bytes 3145732
  39.6 14.0 %collective-permute-start.6 = (bf16[4,4,2,32,512]{4,3,2,1,0:T(8,128)(2,1)S(1)}, bf16[4,4,2,32,512]{4,3,2,1,0:T(8,128)(2,1)S(1)}, u32[]{:S(2)}, u32[]{:S(2)}) collective-permute-start(bf16[4,4,2,32,512]{4,3,2,1,0:T(8,128)(2,1)S(1)} %pad_maximum_fusion.refs_3_), channel_id=1, source_target_pairs={{0,4},{1,5},{2,6},{3,7},{4,0},{5,1},{6,2},{7,3},{8,12},{9,13},{10,... | collective-permute-start | bytes 3145736 | tf_op jit(solution)/shard_map/ppermute | solution.py:46
  41.1 19.8 %copy-start.1 = (bf16[4,4,2,32,512]{4,3,2,1,0:T(8,128)(2,1)}, bf16[4,4,2,32,512]{4,3,2,1,0:T(8,128)(2,1)S(1)}, u32[]{:S(2)}) copy-start(bf16[4,4,2,32,512]{4,3,2,1,0:T(8,128)(2,1)S(1)} %pad_maximum_fusion.1.refs_4_) | copy-start | bytes 3145732
  41.1 15.2 %collective-permute-start.7 = (bf16[4,4,2,32,512]{4,3,2,1,0:T(8,128)(2,1)S(1)}, bf16[4,4,2,32,512]{4,3,2,1,0:T(8,128)(2,1)S(1)}, u32[]{:S(2)}, u32[]{:S(2)}) collective-permute-start(bf16[4,4,2,32,512]{4,3,2,1,0:T(8,128)(2,1)S(1)} %pad_maximum_fusion.1.refs_4_), channel_id=1, source_target_pairs={{0,12},{1,13},{2,14},{3,15},{4,8},{5,9},{6,10},{7,11},{8,4},{9,5},... | collective-permute-start | bytes 3145736 | tf_op jit(solution)/shard_map/ppermute | solution.py:46
  43.0 20.3 %collective-permute-start.10 = (bf16[4,4,2,32,512]{4,3,2,1,0:T(8,128)(2,1)S(1)}, bf16[4,4,2,32,512]{4,3,2,1,0:T(8,128)(2,1)S(1)}, u32[]{:S(2)}, u32[]{:S(2)}) collective-permute-start(bf16[4,4,2,32,512]{4,3,2,1,0:T(8,128)(2,1)S(1)} %pad_maximum_fusion.refs_3_), channel_id=1, source_target_pairs={{0,16},{1,17},{2,18},{3,19},{4,20},{5,21},{6,22},{7,23},{8,24},{9,... | collective-permute-start | bytes 3145736 | tf_op jit(solution)/shard_map/ppermute | solution.py:46
  46.7 19.0 %collective-permute-start.11 = (bf16[4,4,2,32,512]{4,3,2,1,0:T(8,128)(2,1)S(1)}, bf16[4,4,2,32,512]{4,3,2,1,0:T(8,128)(2,1)S(1)}, u32[]{:S(2)}, u32[]{:S(2)}) collective-permute-start(bf16[4,4,2,32,512]{4,3,2,1,0:T(8,128)(2,1)S(1)} %pad_maximum_fusion.1.refs_4_), channel_id=1, source_target_pairs={{0,16},{1,17},{2,18},{3,19},{4,20},{5,21},{6,22},{7,23},{8,24},{9,... | collective-permute-start | bytes 3145736 | tf_op jit(solution)/shard_map/ppermute | solution.py:46
  56.5 14.0 %collective-permute-start.9 = (bf16[8,2,2,32,512]{4,3,2,1,0:T(8,128)(2,1)S(1)}, bf16[8,2,2,32,512]{4,3,2,1,0:T(8,128)(2,1)S(1)}, u32[]{:S(2)}, u32[]{:S(2)}) collective-permute-start(bf16[8,2,2,32,512]{4,3,2,1,0:T(8,128)(2,1)S(1)} %pad_maximum_fusion.3), channel_id=1, source_target_pairs={{0,4},{1,5},{2,6},{3,7},{4,0},{5,1},{6,2},{7,3},{8,12},{9,13},{10,... | collective-permute-start | bytes 3145736 | tf_op jit(solution)/shard_map/ppermute | solution.py:46
  56.7 19.4 %collective-permute-start.12 = (bf16[4,4,2,32,512]{4,3,2,1,0:T(8,128)(2,1)S(1)}, bf16[4,4,2,32,512]{4,3,2,1,0:T(8,128)(2,1)S(1)}, u32[]{:S(2)}, u32[]{:S(2)}) collective-permute-start(bf16[4,4,2,32,512]{4,3,2,1,0:T(8,128)(2,1)S(1)} %collective-permute-done.6.refs_5_), channel_id=1, source_target_pairs={{0,16},{1,17},{2,18},{3,19},{4,20},{5,21},{6,22},{7,23},{8,24},{9,... | collective-permute-start | bytes 3145736 | tf_op jit(solution)/shard_map/ppermute | solution.py:46
  60.9 15.2 %collective-permute-start.8 = (bf16[8,2,2,32,512]{4,3,2,1,0:T(8,128)(2,1)S(1)}, bf16[8,2,2,32,512]{4,3,2,1,0:T(8,128)(2,1)S(1)}, u32[]{:S(2)}, u32[]{:S(2)}) collective-permute-start(bf16[8,2,2,32,512]{4,3,2,1,0:T(8,128)(2,1)S(1)} %pad_maximum_fusion.2), channel_id=1, source_target_pairs={{0,12},{1,13},{2,14},{3,15},{4,8},{5,9},{6,10},{7,11},{8,4},{9,5},... | collective-permute-start | bytes 3145736 | tf_op jit(solution)/shard_map/ppermute | solution.py:46
  63.3 15.5 %copy-start.6 = (bf16[4,4,2,32,512]{4,3,2,1,0:T(8,128)(2,1)}, bf16[4,4,2,32,512]{4,3,2,1,0:T(8,128)(2,1)S(1)}, u32[]{:S(2)}) copy-start(bf16[4,4,2,32,512]{4,3,2,1,0:T(8,128)(2,1)S(1)} %collective-permute-done.10.refs_7_) | copy-start | bytes 3145732
  63.3 12.8 %collective-permute-start.13 = (bf16[4,4,2,32,512]{4,3,2,1,0:T(8,128)(2,1)S(1)}, bf16[4,4,2,32,512]{4,3,2,1,0:T(8,128)(2,1)S(1)}, u32[]{:S(2)}, u32[]{:S(2)}) collective-permute-start(bf16[4,4,2,32,512]{4,3,2,1,0:T(8,128)(2,1)S(1)} %collective-permute-done.7.refs_6_), channel_id=1, source_target_pairs={{0,16},{1,17},{2,18},{3,19},{4,20},{5,21},{6,22},{7,23},{8,24},{9,... | collective-permute-start | bytes 3145736 | tf_op jit(solution)/shard_map/ppermute | solution.py:46
  65.8 13.0 %copy-start.7 = (bf16[4,4,2,32,512]{4,3,2,1,0:T(8,128)(2,1)}, bf16[4,4,2,32,512]{4,3,2,1,0:T(8,128)(2,1)S(1)}, u32[]{:S(2)}) copy-start(bf16[4,4,2,32,512]{4,3,2,1,0:T(8,128)(2,1)S(1)} %collective-permute-done.11.refs_8_) | copy-start | bytes 3145732
  65.8 26.5 %collective-permute-start.15 = (bf16[8,2,2,32,512]{4,3,2,1,0:T(8,128)(2,1)}, bf16[8,2,2,32,512]{4,3,2,1,0:T(8,128)(2,1)S(1)}, u32[]{:S(2)}, u32[]{:S(2)}) collective-permute-start(bf16[8,2,2,32,512]{4,3,2,1,0:T(8,128)(2,1)} %pad_maximum_fusion.5), channel_id=1, source_target_pairs={{0,4},{1,5},{2,6},{3,7},{4,0},{5,1},{6,2},{7,3},{8,12},{9,13},{10,... | collective-permute-start | bytes 3145736 | tf_op jit(solution)/shard_map/ppermute | solution.py:46
  70.5 21.7 %collective-permute-start.14 = (bf16[8,2,2,32,512]{4,3,2,1,0:T(8,128)(2,1)}, bf16[8,2,2,32,512]{4,3,2,1,0:T(8,128)(2,1)}, u32[]{:S(2)}, u32[]{:S(2)}) collective-permute-start(bf16[8,2,2,32,512]{4,3,2,1,0:T(8,128)(2,1)} %pad_maximum_fusion.4), channel_id=1, source_target_pairs={{0,12},{1,13},{2,14},{3,15},{4,8},{5,9},{6,10},{7,11},{8,4},{9,5},... | collective-permute-start | bytes 3145736 | tf_op jit(solution)/shard_map/ppermute | solution.py:46
  77.1 3.2 %collective-permute-start.17 = (bf16[8,1,2,32,512]{4,3,2,1,0:T(8,128)(2,1)S(1)}, bf16[8,1,2,32,512]{4,3,2,1,0:T(8,128)(2,1)S(1)}, u32[]{:S(2)}, u32[]{:S(2)}) collective-permute-start(bf16[8,1,2,32,512]{4,3,2,1,0:T(8,128)(2,1)S(1)} %slice.105), channel_id=1, source_target_pairs={{0,16},{1,17},{2,18},{3,19},{4,20},{5,21},{6,22},{7,23},{8,24},{9,... | collective-permute-start | bytes 1572872 | tf_op jit(solution)/shard_map/ppermute | solution.py:46
  78.8 2.3 %collective-permute-start.16 = (bf16[8,1,2,32,512]{4,3,2,1,0:T(8,128)(2,1)S(1)}, bf16[8,1,2,32,512]{4,3,2,1,0:T(8,128)(2,1)S(1)}, u32[]{:S(2)}, u32[]{:S(2)}) collective-permute-start(bf16[8,1,2,32,512]{4,3,2,1,0:T(8,128)(2,1)S(1)} %slice.104), channel_id=1, source_target_pairs={{0,16},{1,17},{2,18},{3,19},{4,20},{5,21},{6,22},{7,23},{8,24},{9,... | collective-permute-start | bytes 1572872 | tf_op jit(solution)/shard_map/ppermute | solution.py:46
  92.3 3.0 %collective-permute-start.18 = (bf16[8,2,2,32,512]{4,3,2,1,0:T(8,128)(2,1)}, bf16[8,2,2,32,512]{4,3,2,1,0:T(8,128)(2,1)S(1)}, u32[]{:S(2)}, u32[]{:S(2)}) collective-permute-start(bf16[8,2,2,32,512]{4,3,2,1,0:T(8,128)(2,1)} %collective-permute-done.14.refs_11_), channel_id=1, source_target_pairs={{0,16},{1,17},{2,18},{3,19},{4,20},{5,21},{6,22},{7,23},{8,24},{9,... | collective-permute-start | bytes 3145736 | tf_op jit(solution)/shard_map/ppermute | solution.py:46
  92.7 3.8 %collective-permute-start.19 = (bf16[8,2,2,32,512]{4,3,2,1,0:T(8,128)(2,1)S(1)}, bf16[8,2,2,32,512]{4,3,2,1,0:T(8,128)(2,1)S(1)}, u32[]{:S(2)}, u32[]{:S(2)}) collective-permute-start(bf16[8,2,2,32,512]{4,3,2,1,0:T(8,128)(2,1)S(1)} %collective-permute-done.15.refs_12_), channel_id=1, source_target_pairs={{0,16},{1,17},{2,18},{3,19},{4,20},{5,21},{6,22},{7,23},{8,24},{9,... | collective-permute-start | bytes 3145736 | tf_op jit(solution)/shard_map/ppermute | solution.py:46
  (11 other events, 43.1 us)
